TPU v7x, 32 devices: a whole 2x2x4 slice. The times are simulated.
32 devices in a mesh: dp: 8 (over z, core), seq: 4 (over y, x).
Axes of the slice: x: 2, y: 2, z: 4, core: 2. Of those that a mesh axis runs over, the one named last changes fastest.
Arguments:
- layer_input: bfloat16 [8, 1024, 2048], P('dp', 'seq'), may hold values from -6 to 6
- segment_ids: int32 [8, 1024], P('dp', 'seq'), may hold values from 0 to 2, as said below
- mix_gain: bfloat16 [2048], P(('dp', 'seq')), may hold values from 0.5 to 1.5
- bound_logit: bfloat16 [2048], P(('dp', 'seq')), may hold values from 2.2 to 9, as said below
- query_weight: bfloat16 [2048, 2048], P(('dp', 'seq')), may hold values from -0.125 to 0.125
- forget_weight: bfloat16 [2048, 2048], P(('dp', 'seq')), may hold values from -0.125 to 0.125
- input_weight: bfloat16 [2048, 2048], P(('dp', 'seq')), may hold values from -0.125 to 0.125
- output_gate_weight: bfloat16 [2048, 2048], P(('dp', 'seq')), may hold values from -0.125 to 0.125
- output_weight: bfloat16 [2048, 2048], P(('dp', 'seq')), may hold values from -0.1875 to 0.1875
- ffn_gain: bfloat16 [2048], P(('dp', 'seq')), may hold values from 0.5 to 1.5
- ffn_gate_weight: bfloat16 [2048, 5632], P(('dp', 'seq')), may hold values from -0.125 to 0.125
- ffn_up_weight: bfloat16 [2048, 5632], P(('dp', 'seq')), may hold values from -0.125 to 0.125
- ffn_down_weight: bfloat16 [2048, 5632], P(('dp', 'seq')), may hold values from -0.109375 to 0.109375
- output_cotangent: bfloat16 [8, 1024, 2048], P('dp', 'seq'), may hold values from -6 to 6
Outputs:
- block_output: bfloat16 [8, 1024, 2048], P('dp', 'seq')
- input_grad: float32 [8, 1024, 2048], P('dp', 'seq')
- mix_gain_grad: float32 [2048], P(('dp', 'seq'))
- bound_logit_grad: float32 [2048], P(('dp', 'seq'))
- query_weight_grad: float32 [2048, 2048], P(('dp', 'seq'))
- forget_weight_grad: float32 [2048, 2048], P(('dp', 'seq'))
- input_weight_grad: float32 [2048, 2048], P(('dp', 'seq'))
- output_gate_weight_grad: float32 [2048, 2048], P(('dp', 'seq'))
- output_weight_grad: float32 [2048, 2048], P(('dp', 'seq'))
- ffn_gain_grad: float32 [2048], P(('dp', 'seq'))
- ffn_gate_weight_grad: float32 [2048, 5632], P(('dp', 'seq'))
- ffn_up_weight_grad: float32 [2048, 5632], P(('dp', 'seq'))
- ffn_down_weight_grad: float32 [2048, 5632], P(('dp', 'seq'))
Inputs may be any that keep to these rules, and one draw needn't show every extreme that they name: `segment_ids`: along each row the ids never fall; each row has three sequences, the middle one starting within the row's first 256 tokens, not at its first token, and ending within its last 256. sigmoid(bound_logit) is 0.9 or more for every feature.
All inputs are finite; a program needn't handle non-finite values.
Results may differ from a plain program's by a relative error of at most 0.009.
Values may be sent and summed in bfloat16 or wider, within the bound.
No kernel may reach another device: no remote copies, remote signals or barrier semaphores. Data moves between devices by JAX's collectives and lax.ppermute only.
A program may use at most 768 MiB of HBM per device.

v0:
```python
import jax
import jax.numpy as jnp
from jax import lax
from jax.sharding import PartitionSpec as P

HEAD_COUNT = 16
HEAD_FEATURES = 128
FF = 5632
BLOCK = 64


eps_model = 1e-06
eps_group = 1e-05
highest = lax.Precision.HIGHEST


def passed_along(block, axis, distance):
    devices = range(lax.axis_size(axis))
    route = [(i - distance, i) for i in devices if i - distance in devices]
    return lax.ppermute(block, axis, route)


def carried_in(value, axis, join, neutral, backward):
    count, mine = (lax.axis_size(axis), lax.axis_index(axis))
    pieces = jax.tree.map(lambda part: lax.all_gather(part, axis), value)
    if backward:
        pieces = jax.tree.map(lambda part: part[::-1], pieces)
        mine = count - 1 - mine
    total = jax.tree.map(
        lambda part, zero: jnp.full_like(part, 0) + jnp.asarray(zero, part.dtype), value, neutral
    )

    def carried_step(position, total):
        longer = join(total, jax.tree.map(lambda part: part[position], pieces))
        return jax.tree.map(lambda new, old: jnp.where(position < mine, new, old), longer, total)

    return lax.fori_loop(0, count - 1, carried_step, total)


def silu_slope(value):
    sigma = jax.nn.sigmoid(value)
    return sigma * (1.0 + value * (1.0 - sigma))


def run_block(queries, key_gate, value_rows, segments, prior, start_state, block_len):
    rows, length, heads, width = queries.shape
    count = length // block_len
    log_keep = jnp.log1p(-key_gate)

    def split_blocks(array):
        shaped = array.reshape((rows, count, block_len) + array.shape[2:])
        return jnp.moveaxis(shaped, 1, 0)

    pieces = (
        split_blocks(queries),
        split_blocks(key_gate),
        split_blocks(value_rows),
        split_blocks(log_keep),
        split_blocks(segments),
    )
    causal = jnp.arange(block_len)[:, None] >= jnp.arange(block_len)[None, :]

    def run_step(carry, piece):
        state, before = carry
        query_c, gate_c, value_c, log_c, seg_c = piece
        cumul = jnp.cumsum(log_c, axis=1)
        query_d = query_c * jnp.exp(cumul)
        gate_d = gate_c * jnp.exp(-cumul)
        same = (seg_c[:, :, None] == seg_c[:, None, :]) & causal[None]
        scores = jnp.einsum("rthk,rshk->rhts", query_d, gate_d, precision=highest)
        scores = jnp.where(same[:, None], scores, 0.0)
        output = jnp.einsum("rhts,rshv->rthv", scores, value_c, precision=highest)
        linked = (seg_c == before[:, None]).astype(jnp.float32)
        output = output + jnp.einsum(
            "rthk,rhkv->rthv", query_d * linked[:, :, None, None], state, precision=highest
        )
        last_log = cumul[:, -1]
        tail = (seg_c == seg_c[:, -1:]).astype(jnp.float32)
        gate_t = gate_c * jnp.exp(last_log[:, None] - cumul) * tail[:, :, None, None]
        keep_old = jnp.exp(last_log) * linked[:, -1][:, None, None]
        state = keep_old[..., None] * state + jnp.einsum(
            "rshk,rshv->rhkv", gate_t, value_c, precision=highest
        )
        return ((state, seg_c[:, -1]), output)

    (final, unused), outputs = lax.scan(jax.checkpoint(run_step), (start_state, prior), pieces)
    outputs = jnp.moveaxis(outputs, 0, 1).reshape(rows, length, heads, width)
    return (outputs, final)


def link_states(earlier, later):
    return (earlier[0] * later[0], later[0][..., None] * earlier[1] + later[1])


def contract_rows(left, right):
    return lax.dot_general(
        left, right, (((0,), (0,)), ((), ())), preferred_element_type=jnp.float32
    )


def contract_cols(left, right):
    return lax.dot_general(
        left, right, (((1,), (1,)), ((), ())), preferred_element_type=jnp.float32
    )


def rms_back(grad_unit, unit, factor):
    return factor * (grad_unit - unit * jnp.mean(grad_unit * unit, axis=-1, keepdims=True))


def local(
    layer_input,
    segment_ids,
    mix_gain,
    bound_logit,
    query_weight,
    forget_weight,
    input_weight,
    output_gate_weight,
    output_weight,
    ffn_gain,
    ffn_gate_weight,
    ffn_up_weight,
    ffn_down_weight,
    output_cotangent,
):
    rows, length, width = layer_input.shape
    tokens = rows * length
    inputs = layer_input.astype(jnp.float32).reshape(tokens, width)
    factor_in = lax.rsqrt(jnp.mean(inputs * inputs, axis=-1, keepdims=True) + eps_model)
    unit_in = inputs * factor_in
    gain_p = lax.all_gather(mix_gain, ("dp", "seq"), axis=0, tiled=True)
    logit_p = lax.all_gather(bound_logit, ("dp", "seq"), axis=0, tiled=True)
    query_p = lax.all_gather(query_weight, ("dp", "seq"), axis=0, tiled=True)
    forget_p = lax.all_gather(forget_weight, ("dp", "seq"), axis=0, tiled=True)
    input_p = lax.all_gather(input_weight, ("dp", "seq"), axis=0, tiled=True)
    outgate_p = lax.all_gather(output_gate_weight, ("dp", "seq"), axis=0, tiled=True)
    left = (unit_in * gain_p.astype(jnp.float32)).astype(jnp.bfloat16)
    query_pre = jnp.dot(left, query_p, preferred_element_type=jnp.float32)
    forget_pre = jnp.dot(left, forget_p, preferred_element_type=jnp.float32)
    input_pre = jnp.dot(left, input_p, preferred_element_type=jnp.float32)
    outgate_pre = jnp.dot(left, outgate_p, preferred_element_type=jnp.float32)
    gain_in = gain_p.astype(jnp.float32)
    logit_all = logit_p.astype(jnp.float32)
    bound_keep = jax.nn.sigmoid(-logit_all)
    forget_sig = jax.nn.sigmoid(-forget_pre)
    key_gate = bound_keep * forget_sig
    queries = jax.nn.silu(query_pre)
    head_shape = (rows, length, HEAD_COUNT, HEAD_FEATURES)
    query_h = queries.reshape(head_shape)
    key_h = key_gate.reshape(head_shape)
    value_h = input_pre.reshape(head_shape)
    prior = passed_along(segment_ids[:, length - 1 :], "seq", 1)[:, 0]
    linked = (segment_ids == prior[:, None]).astype(jnp.float32)
    running = jnp.cumsum(jnp.log1p(-key_h), axis=1)
    carry_fac = jnp.exp(running) * linked[:, :, None, None]
    decay_all = carry_fac[:, length - 1]
    reach = query_h * carry_fac
    empty_state = jnp.zeros((rows, HEAD_COUNT, HEAD_FEATURES, HEAD_FEATURES), jnp.float32)
    local_out, local_end = run_block(
        query_h, key_h, value_h, segment_ids, prior, empty_state, BLOCK
    )
    unused_decay, incoming = carried_in(
        (decay_all, local_end), "seq", link_states, (jnp.ones_like(decay_all), empty_state), False
    )
    mixed = local_out + jnp.einsum("rthk,rhkv->rthv", reach, incoming, precision=highest)
    group_factor = lax.rsqrt(jnp.mean(mixed * mixed, axis=-1, keepdims=True) + eps_group)
    normed_head = mixed * group_factor
    normed_mix = normed_head.reshape(tokens, width)
    gate_act = jax.nn.silu(outgate_pre)
    gated = (normed_mix * gate_act).astype(jnp.bfloat16)
    output_full, gate_full, up_full, down_full, gain_mid = (
        lax.all_gather(output_weight, ("dp", "seq"), axis=0, tiled=True),
        lax.all_gather(ffn_gate_weight, ("dp", "seq"), axis=0, tiled=True),
        lax.all_gather(ffn_up_weight, ("dp", "seq"), axis=0, tiled=True),
        lax.all_gather(ffn_down_weight, ("dp", "seq"), axis=0, tiled=True),
        lax.all_gather(ffn_gain, ("dp", "seq"), axis=0, tiled=True),
    )
    branch = jnp.dot(gated, output_full, preferred_element_type=jnp.float32)
    resid = inputs + branch
    factor_mid = lax.rsqrt(jnp.mean(resid * resid, axis=-1, keepdims=True) + eps_model)
    unit_mid = resid * factor_mid
    normed_mid = (unit_mid * gain_mid.astype(jnp.float32)).astype(jnp.bfloat16)
    gate_h = jnp.dot(normed_mid, gate_full, preferred_element_type=jnp.float32)
    up_h = jnp.dot(normed_mid, up_full, preferred_element_type=jnp.float32)
    hidden = (jax.nn.silu(gate_h) * up_h).astype(jnp.bfloat16)
    ffn_out = contract_cols(hidden, down_full)
    block_output = (resid + ffn_out).astype(jnp.bfloat16).reshape(rows, length, width)
    cotangent = output_cotangent.astype(jnp.float32).reshape(tokens, width)
    ffn_low = cotangent.astype(jnp.bfloat16)
    output_full, gate_full, up_full, down_full, gain_mid = (
        lax.all_gather(output_weight, ("dp", "seq"), axis=0, tiled=True),
        lax.all_gather(ffn_gate_weight, ("dp", "seq"), axis=0, tiled=True),
        lax.all_gather(ffn_up_weight, ("dp", "seq"), axis=0, tiled=True),
        lax.all_gather(ffn_down_weight, ("dp", "seq"), axis=0, tiled=True),
        lax.all_gather(ffn_gain, ("dp", "seq"), axis=0, tiled=True),
    )
    gain_mid_f = gain_mid.astype(jnp.float32)
    hidden_grad = jnp.dot(ffn_low, down_full, preferred_element_type=jnp.float32)
    gate_grad = (hidden_grad * up_h * silu_slope(gate_h)).astype(jnp.bfloat16)
    up_grad = (hidden_grad * jax.nn.silu(gate_h)).astype(jnp.bfloat16)
    mid_grad = contract_cols(gate_grad, gate_full) + contract_cols(up_grad, up_full)
    ffn_gain_local = jnp.sum(mid_grad * unit_mid, axis=0)
    resid_grad = cotangent + rms_back(mid_grad * gain_mid_f, unit_mid, factor_mid)
    branch_low = resid_grad.astype(jnp.bfloat16)
    gated_grad = contract_cols(branch_low, output_full)
    outgate_grad = (gated_grad * normed_mix * silu_slope(outgate_pre)).astype(jnp.bfloat16)
    mix_unit_grad = (gated_grad * gate_act).reshape(head_shape)
    mixed_grad = rms_back(mix_unit_grad, normed_head, group_factor)
    local_term = jnp.einsum("rthk,rthv->rhkv", reach, mixed_grad, precision=highest)
    unused_back, end_grad = carried_in(
        (decay_all, local_term), "seq", link_states, (jnp.ones_like(decay_all), empty_state), True
    )

    def local_mix(query_a, key_a, value_a, state_a):
        return run_block(query_a, key_a, value_a, segment_ids, prior, state_a, BLOCK)

    unused_pair, pullback = jax.vjp(local_mix, query_h, key_h, value_h, incoming)
    query_grad_h, key_grad_h, value_grad_h, unused_state = pullback((mixed_grad, end_grad))
    query_grad = (query_grad_h.reshape(tokens, width) * silu_slope(query_pre)).astype(jnp.bfloat16)
    key_total = key_grad_h.reshape(tokens, width)
    forget_grad = (-key_total * key_gate * (1.0 - forget_sig)).astype(jnp.bfloat16)
    input_grad_pre = value_grad_h.reshape(tokens, width).astype(jnp.bfloat16)
    logit_local = -jnp.sum(key_total * key_gate, axis=0) * (1.0 - bound_keep)
    query_p = lax.all_gather(query_weight, ("dp", "seq"), axis=0, tiled=True)
    forget_p = lax.all_gather(forget_weight, ("dp", "seq"), axis=0, tiled=True)
    input_p = lax.all_gather(input_weight, ("dp", "seq"), axis=0, tiled=True)
    outgate_p = lax.all_gather(output_gate_weight, ("dp", "seq"), axis=0, tiled=True)
    part_grad = (
        contract_cols(query_grad, query_p)
        + contract_cols(forget_grad, forget_p)
        + contract_cols(input_grad_pre, input_p)
        + contract_cols(outgate_grad, outgate_p)
    )
    mix_gain_local = jnp.sum(part_grad * unit_in, axis=0)
    input_grad = (resid_grad + rms_back(part_grad * gain_in, unit_in, factor_in)).reshape(
        rows, length, width
    )
    mix_right = jnp.concatenate((query_grad, forget_grad, input_grad_pre, outgate_grad), axis=1)
    ffn_right = jnp.concatenate((gate_grad, up_grad), axis=1)
    weight_grads = lax.psum_scatter(
        jnp.concatenate(
            (
                contract_rows(left, mix_right),
                contract_rows(gated, branch_low),
                contract_rows(normed_mid, ffn_right),
                contract_rows(ffn_low, hidden),
            ),
            axis=1,
        ),
        ("dp", "seq"),
        scatter_dimension=0,
        tiled=True,
    )
    mix_gain_grad, bound_logit_grad, ffn_gain_grad = (
        lax.psum_scatter(mix_gain_local, ("dp", "seq"), scatter_dimension=0, tiled=True),
        lax.psum_scatter(logit_local, ("dp", "seq"), scatter_dimension=0, tiled=True),
        lax.psum_scatter(ffn_gain_local, ("dp", "seq"), scatter_dimension=0, tiled=True),
    )
    query_weight_grad = weight_grads[:, 0:width]
    forget_weight_grad = weight_grads[:, width : 2 * width]
    input_weight_grad = weight_grads[:, 2 * width : 3 * width]
    output_gate_weight_grad = weight_grads[:, 3 * width : 4 * width]
    output_weight_grad = weight_grads[:, 4 * width : 5 * width]
    ffn_gate_weight_grad = weight_grads[:, 5 * width : 5 * width + FF]
    ffn_up_weight_grad = weight_grads[:, 5 * width + FF : 5 * width + 2 * FF]
    ffn_down_weight_grad = weight_grads[:, 5 * width + 2 * FF : 5 * width + 3 * FF]
    return (
        block_output,
        input_grad,
        mix_gain_grad,
        bound_logit_grad,
        query_weight_grad,
        forget_weight_grad,
        input_weight_grad,
        output_gate_weight_grad,
        output_weight_grad,
        ffn_gain_grad,
        ffn_gate_weight_grad,
        ffn_up_weight_grad,
        ffn_down_weight_grad,
    )


def solution(mesh):
    return jax.shard_map(
        local,
        mesh=mesh,
        in_specs=(
            P("dp", "seq", None),
            P("dp", "seq"),
            P(("dp", "seq")),
            P(("dp", "seq")),
            P(("dp", "seq"), None),
            P(("dp", "seq"), None),
            P(("dp", "seq"), None),
            P(("dp", "seq"), None),
            P(("dp", "seq"), None),
            P(("dp", "seq")),
            P(("dp", "seq"), None),
            P(("dp", "seq"), None),
            P(("dp", "seq"), None),
            P("dp", "seq", None),
        ),
        out_specs=(
            P("dp", "seq", None),
            P("dp", "seq", None),
            P(("dp", "seq")),
            P(("dp", "seq")),
            P(("dp", "seq"), None),
            P(("dp", "seq"), None),
            P(("dp", "seq"), None),
            P(("dp", "seq"), None),
            P(("dp", "seq"), None),
            P(("dp", "seq")),
            P(("dp", "seq"), None),
            P(("dp", "seq"), None),
            P(("dp", "seq"), None),
        ),
        check_vma=False,
    )
```

profile of v0, /device:TPU:1, one launch (start us, length us, event | category | flops | bytes accessed | tf_op | source)
XLA Modules:
  0.0 6109.2 jit_solution(14826048596379276794)
XLA Ops:
  19.7 39.7 all-reduce.8
  63.0 28.1 all-gather.17.cloned.1.call-done
  99.9 70.2 %all-gather.13.cloned.1.call-done = bf16[2048,2048]{1,0:T(8,128)(2,1)} async-done(((bf16[64,2048]{1,0:T(8,128)(2,1)}), bf16[2048,2048]{1,0:T(8,128)(2,1)}) %all-gather.13.cloned.1.call-update) | async-done | bytes 8388624 | tf_op jit(solution)/shard_map/all_gather | solution.py:135
  180.5 68.7 %all-gather.15.cloned.1.call-done = bf16[2048,2048]{1,0:T(8,128)(2,1)} async-done(((bf16[64,2048]{1,0:T(8,128)(2,1)}), bf16[2048,2048]{1,0:T(8,128)(2,1)}) %all-gather.15.cloned.1.call-update) | async-done | bytes 8388624 | tf_op jit(solution)/shard_map/all_gather | solution.py:136
  270.5 49.5 while.84
  343.1 29.2 all-gather.29.cloned.1.call-done
  388.4 64.6 %all-gather.19.cloned.1.call-done = bf16[2048,2048]{1,0:T(8,128)(2,1)} async-done(((bf16[64,2048]{1,0:T(8,128)(2,1)}), bf16[2048,2048]{1,0:T(8,128)(2,1)}) %all-gather.19.cloned.1.call-update) | async-done | bytes 8388624 | tf_op jit(solution)/shard_map/all_gather | solution.py:137
  461.4 70.5 %all-gather.21.cloned.1.call-done = bf16[2048,2048]{1,0:T(8,128)(2,1)} async-done(((bf16[64,2048]{1,0:T(8,128)(2,1)}), bf16[2048,2048]{1,0:T(8,128)(2,1)}) %all-gather.21.cloned.1.call-update) | async-done | bytes 8388624 | tf_op jit(solution)/shard_map/all_gather | solution.py:173
  540.8 39.0 while.82
  579.8 98.2 %all-gather.25.cloned.1.call-done = bf16[2048,5632]{1,0:T(8,128)(2,1)} async-done(((bf16[64,5632]{1,0:T(8,128)(2,1)}), bf16[2048,5632]{1,0:T(8,128)(2,1)}) %all-gather.25.cloned.1.call-update) | async-done | bytes 23068688 | tf_op jit(solution)/shard_map/all_gather | solution.py:175
  678.0 12.8 fusion.174
  690.8 132.9 %all-gather.23.cloned.1.call-done = bf16[2048,5632]{1,0:T(8,128)(2,1)} async-done(((bf16[64,5632]{1,0:T(8,128)(2,1)}), bf16[2048,5632]{1,0:T(8,128)(2,1)}) %all-gather.23.cloned.1.call-update) | async-done | bytes 23068688 | tf_op jit(solution)/shard_map/all_gather | solution.py:174
  836.3 133.2 %all-gather.27.cloned.1.call-done = bf16[2048,5632]{1,0:T(8,128)(2,1)} async-done(((bf16[64,5632]{1,0:T(8,128)(2,1)}), bf16[2048,5632]{1,0:T(8,128)(2,1)}) %all-gather.27.cloned.1.call-update) | async-done | bytes 23068688 | tf_op jit(solution)/shard_map/all_gather | solution.py:176
  969.5 19.7 multiply_convert_fusion
  989.2 12.7 fusion.175
  1001.9 14.1 multiply_reduce_fusion.1
  1041.5 20.8 convolution_bitcast_fusion.8
  1075.3 34.3 fusion.94
  1130.5 141.6 %while.83 = (s32[]{:T(128)}, f32[1,16,128,128]{2,3,1,0:T(8,128)S(1)}, f32[4,1,64,16,128]{4,3,2,0,1:T(8,128)}, f32[4,1,64,16,128]{4,3,2,0,1:T(8,128)}, bf16[4,1,6...) while((s32[]{:T(128)}, ...), condition=%wide.region_22.23_spmd.clone, body=%wide.region_17.22_spmd.clone.sunk | while | flops 1331052800 | bytes 65436780 | solution.py:86
  1281.0 24.2 fusion.99
  1305.2 162.9 %pad_maximum_fusion = f32[2048,27136]{1,0:T(8,128)} fusion(f32[2048,5632]{1,0:T(8,128)} %convolution_bitcast_fusion.8, f32[2048,11264]{1,0:T(8,128)} %fusion.94, f32[2048,2048]{1,0:T(8,128)} %fusion.147, f32[2048,8192]{1,0:T(8,128)} %fusion.99), kind=kLoop, calls=%fused_computation.155 | loop fusion | flops 166723584 | bytes 444596224 | tf_op jit(solution)/shard_map/concatenate | solution.py:242
  1469.6 14.0 fusion.117
  1502.7 44.1 all-reduce.7
  1552.0 4542.7 %reduce-scatter.2.cloned.1.call-done = f32[64,27136]{1,0:T(8,128)} async-done(((f32[2048,27136]{1,0:T(8,128)}), f32[64,27136]{1,0:T(8,128)}) %reduce-scatter.2.cloned.1.call-update) | async-done | bytes 6946832 | tf_op jit(solution)/shard_map/reduce_scatter | solution.py:241
  (520 shorter events, 459.4 us)
Async XLA Ops:
  7.2 53.8 copy-start.18
  7.2 83.9 %all-gather.17.cloned.1.call-start = ((), (), s32[]{:S(2)}) async-start(), calls=%async_computation.3 | async-start | bytes 8650752 | tf_op jit(solution)/shard_map/all_gather | solution.py:134
  7.9 162.2 %all-gather.13.cloned.1.call-start = ((), (), s32[]{:S(2)}) async-start(), calls=%async_computation.1 | async-start | bytes 8650752 | tf_op jit(solution)/shard_map/all_gather | solution.py:135
  8.7 240.5 %all-gather.15.cloned.1.call-start = ((), (), s32[]{:S(2)}) async-start(), calls=%async_computation.2 | async-start | bytes 8650752 | tf_op jit(solution)/shard_map/all_gather | solution.py:136
  9.4 362.8 %all-gather.29.cloned.1.call-start = ((), (), s32[]{:S(2)}) async-start(), calls=%async_computation.10 | async-start | bytes 5242880 | tf_op jit(solution)/shard_map/all_gather | solution.py:25
  10.7 51.6 collective-permute-start
  59.4 37.4 copy-start.51
  59.4 393.6 %copy-start.41 = (f32[2048]{0:T(1024)}, f32[2048]{0:T(1024)S(1)}, u32[]{:S(2)}) copy-start(f32[2048]{0:T(1024)S(1)} %convert_element_type.123) | copy-start | bytes 24580
  60.9 392.0 %copy-start.44 = (f32[256]{0:T(256)}, f32[256]{0:T(256)S(1)}, u32[]{:S(2)}) copy-start(f32[256]{0:T(256)S(1)} %add_rsqrt_fusion.2) | copy-start | bytes 3076
  61.0 115.0 %copy-start.47 = (f32[2048]{0:T(1024)}, f32[2048]{0:T(1024)S(1)}, u32[]{:S(2)}) copy-start(f32[2048]{0:T(1024)S(1)} %add_divide_fusion.3) | copy-start | bytes 24580
  320.9 132.0 %all-gather.19.cloned.1.call-start = ((), (), s32[]{:S(2)}) async-start(), calls=%async_computation.4 | async-start | bytes 8650752 | tf_op jit(solution)/shard_map/all_gather | solution.py:137
  321.5 210.4 %all-gather.21.cloned.1.call-start = ((), (), s32[]{:S(2)}) async-start(), calls=%async_computation.5 | async-start | bytes 8650752 | tf_op jit(solution)/shard_map/all_gather | solution.py:173
  322.1 355.9 %all-gather.25.cloned.1.call-start = ((), (), s32[]{:S(2)}) async-start(), calls=%async_computation.7 | async-start | bytes 23789568 | tf_op jit(solution)/shard_map/all_gather | solution.py:175
  322.9 500.8 %all-gather.23.cloned.1.call-start = ((), (), s32[]{:S(2)}) async-start(), calls=%async_computation.6 | async-start | bytes 23789568 | tf_op jit(solution)/shard_map/all_gather | solution.py:174
  323.6 645.9 %all-gather.27.cloned.1.call-start = ((), (), s32[]{:S(2)}) async-start(), calls=%async_computation.8 | async-start | bytes 23789568 | tf_op jit(solution)/shard_map/all_gather | solution.py:176
  324.3 785.3 %all-gather.31.cloned.1.call-start = ((), (), s32[]{:S(2)}) async-start(), calls=%async_computation.11 | async-start | bytes 5242880 | tf_op jit(solution)/shard_map/all_gather | solution.py:25
  579.7 111.0 %copy-start.2 = (f32[4,1,64,16,128]{4,3,2,1,0:T(8,128)}, f32[4,1,64,16,128]{4,3,2,1,0:T(8,128)S(1)}, u32[]{:S(2)}) copy-start(f32[4,1,64,16,128]{4,3,2,1,0:T(8,128)S(1)} %get-tuple-element.1463) | copy-start | bytes 6291460
  579.7 111.0 %copy-start.49 = (s32[4,1,64]{2,1,0:T(1,128)}, s32[4,1,64]{2,1,0:T(1,128)S(1)}, u32[]{:S(2)}) copy-start(s32[4,1,64]{2,1,0:T(1,128)S(1)} %get-tuple-element.1509) | copy-start | bytes 3076
  579.8 111.0 %copy-start.56 = (s32[4,1]{0,1:T(1,128)}, s32[4,1]{0,1:T(1,128)S(1)}, u32[]{:S(2)}) copy-start(s32[4,1]{0,1:T(1,128)S(1)} %get-tuple-element.1408) | copy-start | bytes 52
  690.8 278.7 %copy-start.28 = (bf16[1,256,2048]{2,1,0:T(8,128)(2,1)S(1)}, bf16[1,256,2048]{2,1,0:T(8,128)(2,1)}, u32[]{:S(2)}) copy-start(bf16[1,256,2048]{2,1,0:T(8,128)(2,1)} %param.37) | copy-start | bytes 3145732
  1041.4 5053.3 %reduce-scatter.2.cloned.1.call-start = ((), (), s32[]{:S(2)}) async-start(), calls=%async_computation.9 | async-start | bytes 229244928 | tf_op jit(solution)/shard_map/reduce_scatter | solution.py:241
  1281.0 24.2 copy-start.30
  1281.0 24.2 copy-start.32
  1495.0 53.5 copy-start.15
  (64 other events, 264.6 us)
Sparse Core Ops, SparseCore 0:
  10.9 80.1 all-gather.16
  93.9 76.1 all-gather.12
  173.0 76.1 all-gather.14
  321.1 51.1 all-gather.28
  374.9 77.9 all-gather.18
  455.7 76.1 all-gather.20
  534.8 143.1 all-gather.24
  680.9 142.7 all-gather.22
  826.6 142.8 all-gather.26
  1041.5 50.4 all-gather.30
  1468.2 4626.4 reduce-scatter.1
where the time goes:
time: 6120 us; the launch traced here: 6110 us
  waiting for transfers between devices  5240 us (86%)
  matrix products  331 us (5%)
  other arithmetic  253 us (4%)
  local copies, waits for them, and re-layouts  160 us (3%)
  blocking collectives  90.7 us (1%)
    reduce_scatter x1, waiting for transfers between devices, local(): lax.psum_scatter(jnp.concatenate((contract_rows(left, mix_right), contrac...  4540 us
    concatenate x1, other arithmetic, local(): jnp.concatenate((contract_rows(left, mix_right), contract_rows(gated, bra...  163 us
    all_gather x1, waiting for transfers between devices, local(): lax.all_gather(ffn_down_weight, ('dp', 'seq'), axis=0, tiled=True)  133 us
    all_gather x1, waiting for transfers between devices, local(): lax.all_gather(ffn_gate_weight, ('dp', 'seq'), axis=0, tiled=True)  133 us
  transfers between devices with their start and end apart: 12, of which 10 were waited for; matrix products, arithmetic and copies ran while one was open for 4% of the time, Pallas kernels for 0%

commit v1 on v0

v1 whole, which is shorter than its diff:
```python
import functools

import jax
import jax.numpy as jnp
from jax import lax
from jax.experimental import pallas as pl
from jax.experimental.pallas import tpu as pltpu
from jax.sharding import PartitionSpec as P

HEAD_FEATURES = 128
CHUNK = 128

eps_model = 1e-06
eps_group = 1e-05
highest = lax.Precision.HIGHEST
f32 = jnp.float32
bf16 = jnp.bfloat16


def flip(block, axis, bits):
    return lax.ppermute(block, axis, [(i, i ^ bits) for i in range(lax.axis_size(axis))])


def gather_small(block, axis):
    count, mine = (lax.axis_size(axis), lax.axis_index(axis))
    bit = 1
    while bit < count:
        other = flip(block, axis, bit)
        upper = (mine & bit) != 0
        block = jnp.concatenate(
            (jnp.where(upper, other, block), jnp.where(upper, block, other)), axis=0
        )
        bit *= 2
    return block


def sum_small(block, axis):
    count = lax.axis_size(axis)
    bit = 1
    while bit < count:
        block = block + flip(block, axis, bit)
        bit *= 2
    return block


def gather_seq(block):
    count = lax.axis_size("seq")
    if count != 4:
        return gather_small(block, "seq")
    mine = lax.axis_index("seq")
    tokens = block.shape[0]
    half = tokens // 2
    near = flip(block, "seq", 1)
    far = flip(block, "seq", 2)
    corner_top = flip(near[:half], "seq", 2)
    corner_low = flip(far[half:], "seq", 1)
    whole = jnp.zeros((4 * tokens,) + block.shape[1:], block.dtype)
    whole = lax.dynamic_update_slice_in_dim(whole, block, mine * tokens, 0)
    whole = lax.dynamic_update_slice_in_dim(whole, near, (mine ^ 1) * tokens, 0)
    whole = lax.dynamic_update_slice_in_dim(whole, far, (mine ^ 2) * tokens, 0)
    whole = lax.dynamic_update_slice_in_dim(whole, corner_top, (mine ^ 3) * tokens, 0)
    return lax.dynamic_update_slice_in_dim(whole, corner_low, (mine ^ 3) * tokens + half, 0)


def scatter_seq(partial):
    count = lax.axis_size("seq")
    pieces = partial.astype(bf16).reshape((count, partial.shape[0] // count) + partial.shape[1:])
    pieces = lax.all_to_all(pieces, "seq", split_axis=0, concat_axis=0, tiled=True)
    return jnp.sum(pieces.astype(f32), axis=0)


def gather_columns(weights):
    count = lax.axis_size("seq")
    rows = weights[0].shape[0]
    parts = [jnp.moveaxis(w.reshape(rows, count, w.shape[1] // count), 1, 0) for w in weights]
    pieces = jnp.concatenate(parts, axis=2)
    pieces = lax.all_to_all(pieces, "seq", split_axis=0, concat_axis=0, tiled=True)
    return lax.all_gather(pieces.reshape(count * rows, pieces.shape[2]), "dp", axis=0, tiled=True)


def scatter_columns(grad, parts):
    count = lax.axis_size("seq")
    mine = lax.psum_scatter(grad, "dp", scatter_dimension=0, tiled=True)
    rows = mine.shape[0] // count
    pieces = lax.all_to_all(
        mine.reshape(count, rows, mine.shape[1]), "seq", split_axis=0, concat_axis=0, tiled=True
    )
    width = mine.shape[1] // parts
    return [
        jnp.moveaxis(pieces[:, :, i * width : (i + 1) * width], 0, 1)
        .reshape(rows, count * width)
        .astype(f32)
        for i in range(parts)
    ]


def row_route():
    count, ranks = (lax.axis_size("dp"), lax.axis_size("seq"))
    return [(b, (b % count) * ranks + b // count) for b in range(count * ranks)]


def gather_rows(weight):
    moved = lax.ppermute(weight, ("dp", "seq"), row_route())
    return lax.all_gather(moved, "dp", axis=0, tiled=True)


def scatter_rows(grad):
    mine = lax.psum_scatter(grad, "dp", scatter_dimension=0, tiled=True)
    back = [(b, a) for a, b in row_route()]
    return lax.ppermute(mine, ("dp", "seq"), back).astype(f32)


def product(left, right, left_dim, right_dim, precision=highest):
    return lax.dot_general(
        left,
        right,
        (((left_dim,), (right_dim,)), ((), ())),
        precision=precision,
        preferred_element_type=f32,
    )


def chunk_parts(step, seg_ref, seg_col_ref, seg_row_ref, pre_ref, bound_ref, width):
    size = pre_ref.shape[0]
    first = step * size
    prior = seg_ref[jnp.maximum(first - 1, 0)]
    last = seg_ref[first + size - 1]
    seg_col = seg_col_ref[...]
    at = lax.broadcasted_iota(jnp.int32, (size, size), 0)
    of = lax.broadcasted_iota(jnp.int32, (size, size), 1)
    seen = (seg_col == seg_row_ref[...]) & (at >= of)
    linked = (seg_col == prior).astype(f32)
    tail = (seg_col == last).astype(f32)
    linked_last = (prior == last).astype(f32)
    query_pre = pre_ref[:, 0:width]
    forget_pre = pre_ref[:, width : 2 * width]
    value = pre_ref[:, 2 * width : 3 * width]
    outgate_pre = pre_ref[:, 3 * width : 4 * width]
    forget_sig = jax.nn.sigmoid(-forget_pre)
    key = bound_ref[...] * forget_sig
    query_sig = jax.nn.sigmoid(query_pre)
    lower = (at >= of).astype(f32)
    cumul = product(lower, jnp.log1p(-key), 1, 0)
    grow = jnp.exp(cumul)
    shrink = jnp.exp(-cumul)
    end = grow[size - 1 :, :]
    query_d = query_pre * query_sig * grow
    key_d = key * shrink
    key_t = key_d * end * tail
    keep = end * linked_last
    return locals()


def forward_kernel(seg_ref, seg_col_ref, seg_row_ref, pre_ref, bound_ref, gated_ref, mixed_ref, states_ref, state_ref):
    step = pl.program_id(0)
    width = mixed_ref.shape[1]
    heads = width // HEAD_FEATURES

    @pl.when(step == 0)
    def _():
        state_ref[...] = jnp.zeros_like(state_ref)

    p = chunk_parts(step, seg_ref, seg_col_ref, seg_row_ref, pre_ref, bound_ref, width)
    outgate_pre = p["outgate_pre"]
    gate_act = outgate_pre * jax.nn.sigmoid(outgate_pre)
    for h in range(heads):
        cols = slice(h * HEAD_FEATURES, (h + 1) * HEAD_FEATURES)
        query_d, key_d, value = p["query_d"][:, cols], p["key_d"][:, cols], p["value"][:, cols]
        state = state_ref[h]
        states_ref[0, h] = state
        scores = jnp.where(p["seen"], product(query_d, key_d, 1, 1), 0.0)
        mixed = product(scores, value, 1, 0) + product(query_d * p["linked"], state, 1, 1)
        mixed_ref[:, cols] = mixed
        factor = lax.rsqrt(jnp.mean(mixed * mixed, axis=-1, keepdims=True) + eps_group)
        gated_ref[:, cols] = (mixed * factor * gate_act[:, cols]).astype(bf16)
        state_ref[h] = state * p["keep"][:, cols] + product(value, p["key_t"][:, cols], 0, 0)


def backward_kernel(seg_ref, seg_col_ref, seg_row_ref, pre_ref, bound_ref, mixed_ref, gated_grad_ref, states_ref, grads_ref, logit_ref, back_ref, through_ref):
    step = pl.program_id(0)
    chunk = pl.num_programs(0) - 1 - step
    width = mixed_ref.shape[1]
    heads = width // HEAD_FEATURES

    @pl.when(step == 0)
    def _():
        back_ref[...] = jnp.zeros_like(back_ref)
        through_ref[...] = jnp.zeros_like(through_ref)
        logit_ref[...] = jnp.zeros_like(logit_ref)

    p = chunk_parts(chunk, seg_ref, seg_col_ref, seg_row_ref, pre_ref, bound_ref, width)
    size = pre_ref.shape[0]
    outgate_pre, query_pre, query_sig = p["outgate_pre"], p["query_pre"], p["query_sig"]
    outgate_sig = jax.nn.sigmoid(outgate_pre)
    upper = (p["at"] <= p["of"]).astype(f32)
    for h in range(heads):
        cols = slice(h * HEAD_FEATURES, (h + 1) * HEAD_FEATURES)
        query_d, key_d, key_t, value = (p[k][:, cols] for k in ("query_d", "key_d", "key_t", "value"))
        grow, shrink, end, keep, key = (p[k][:, cols] for k in ("grow", "shrink", "end", "keep", "key"))
        state = states_ref[0, h]
        back = back_ref[h]
        mixed = mixed_ref[:, cols]
        factor = lax.rsqrt(jnp.mean(mixed * mixed, axis=-1, keepdims=True) + eps_group)
        normed = mixed * factor
        gated_grad = gated_grad_ref[:, cols]
        gate, gate_sig = outgate_pre[:, cols], outgate_sig[:, cols]
        outgate_grad = gated_grad * normed * (gate_sig * (1.0 + gate * (1.0 - gate_sig)))
        weighted = gated_grad * (gate * gate_sig)
        mixed_grad = factor * (
            weighted - normed * jnp.mean(weighted * normed, axis=-1, keepdims=True)
        )
        scores = jnp.where(p["seen"], product(query_d, key_d, 1, 1), 0.0)
        scores_grad = jnp.where(p["seen"], product(mixed_grad, value, 1, 1), 0.0)
        value_grad = product(scores, mixed_grad, 0, 0) + product(key_t, back, 1, 1)
        query_d_grad = product(scores_grad, key_d, 1, 0) + p["linked"] * product(mixed_grad, state, 1, 0)
        key_d_grad = product(scores_grad, query_d, 0, 0)
        key_t_grad = product(value, back, 1, 0)
        key_grad = key_d_grad * shrink + (p["tail"] * end * shrink) * key_t_grad
        change = query_d * query_d_grad - key_d * key_d_grad - key_t * key_t_grad
        through = product(upper, change, 1, 0) + through_ref[:, cols]
        key_total = key_grad - through / (1.0 - key)
        new_back = back * keep + product(mixed_grad, query_d * p["linked"], 0, 0)
        back_ref[h] = new_back
        through_ref[:, cols] = jnp.sum(new_back * state, axis=0, keepdims=True)
        sig = query_sig[:, cols]
        query_grad = query_d_grad * grow * (sig * (1.0 + query_pre[:, cols] * (1.0 - sig)))
        weighted_key = key_total * key
        forget_grad = -weighted_key * (1.0 - p["forget_sig"][:, cols])
        logit_ref[:, cols] += jnp.sum(weighted_key, axis=0, keepdims=True)
        for part, grad in enumerate((query_grad, forget_grad, value_grad, outgate_grad)):
            lo = part * width + h * HEAD_FEATURES
            grads_ref[:, lo : lo + HEAD_FEATURES] = grad.astype(bf16)


def recurrence_forward(segments, pre, bound):
    tokens, wide = pre.shape
    width = wide // 4
    heads = width // HEAD_FEATURES
    steps = tokens // CHUNK
    return pl.pallas_call(
        forward_kernel,
        grid_spec=pltpu.PrefetchScalarGridSpec(
            num_scalar_prefetch=1,
            grid=(steps,),
            in_specs=[
                pl.BlockSpec((CHUNK, 1), lambda i, s: (i, 0)),
                pl.BlockSpec((1, CHUNK), lambda i, s: (0, i)),
                pl.BlockSpec((CHUNK, wide), lambda i, s: (i, 0)),
                pl.BlockSpec((1, width), lambda i, s: (0, 0)),
            ],
            out_specs=[
                pl.BlockSpec((CHUNK, width), lambda i, s: (i, 0)),
                pl.BlockSpec((CHUNK, width), lambda i, s: (i, 0)),
                pl.BlockSpec((1, heads, HEAD_FEATURES, HEAD_FEATURES), lambda i, s: (i, 0, 0, 0)),
            ],
            scratch_shapes=[pltpu.VMEM((heads, HEAD_FEATURES, HEAD_FEATURES), f32)],
        ),
        out_shape=[
            jax.ShapeDtypeStruct((tokens, width), bf16),
            jax.ShapeDtypeStruct((tokens, width), f32),
            jax.ShapeDtypeStruct((steps, heads, HEAD_FEATURES, HEAD_FEATURES), f32),
        ],
        compiler_params=pltpu.CompilerParams(vmem_limit_bytes=32 * 1024 * 1024),
        name="recurrence_forward",
    )(segments, segments[:, None], segments[None, :], pre, bound)


def recurrence_backward(segments, pre, bound, mixed, gated_grad, states):
    tokens, wide = pre.shape
    width = wide // 4
    heads = width // HEAD_FEATURES
    steps = tokens // CHUNK
    return pl.pallas_call(
        backward_kernel,
        grid_spec=pltpu.PrefetchScalarGridSpec(
            num_scalar_prefetch=1,
            grid=(steps,),
            in_specs=[
                pl.BlockSpec((CHUNK, 1), lambda i, s: (steps - 1 - i, 0)),
                pl.BlockSpec((1, CHUNK), lambda i, s: (0, steps - 1 - i)),
                pl.BlockSpec((CHUNK, wide), lambda i, s: (steps - 1 - i, 0)),
                pl.BlockSpec((1, width), lambda i, s: (0, 0)),
                pl.BlockSpec((CHUNK, width), lambda i, s: (steps - 1 - i, 0)),
                pl.BlockSpec((CHUNK, width), lambda i, s: (steps - 1 - i, 0)),
                pl.BlockSpec(
                    (1, heads, HEAD_FEATURES, HEAD_FEATURES), lambda i, s: (steps - 1 - i, 0, 0, 0)
                ),
            ],
            out_specs=[
                pl.BlockSpec((CHUNK, wide), lambda i, s: (steps - 1 - i, 0)),
                pl.BlockSpec((1, width), lambda i, s: (0, 0)),
            ],
            scratch_shapes=[
                pltpu.VMEM((heads, HEAD_FEATURES, HEAD_FEATURES), f32),
                pltpu.VMEM((1, width), f32),
            ],
        ),
        out_shape=[
            jax.ShapeDtypeStruct((tokens, wide), bf16),
            jax.ShapeDtypeStruct((1, width), f32),
        ],
        compiler_params=pltpu.CompilerParams(vmem_limit_bytes=32 * 1024 * 1024),
        name="recurrence_backward",
    )(segments, segments[:, None], segments[None, :], pre, bound, mixed, gated_grad, states)


def matmul(left, right, left_dim=1, right_dim=0):
    return lax.dot_general(
        left, right, (((left_dim,), (right_dim,)), ((), ())), preferred_element_type=f32
    )


def rms_factor(value):
    return lax.rsqrt(jnp.mean(value * value, axis=-1, keepdims=True) + eps_model)


def rms_back(grad_unit, unit, factor):
    return factor * (grad_unit - unit * jnp.mean(grad_unit * unit, axis=-1, keepdims=True))


def local(
    layer_input,
    segment_ids,
    mix_gain,
    bound_logit,
    query_weight,
    forget_weight,
    input_weight,
    output_gate_weight,
    output_weight,
    ffn_gain,
    ffn_gate_weight,
    ffn_up_weight,
    ffn_down_weight,
    output_cotangent,
):
    rows, length, width = layer_input.shape
    ranks, rank = (lax.axis_size("seq"), lax.axis_index("seq"))
    my_width = width // ranks
    tokens = rows * length
    x_low = layer_input.reshape(tokens, width)
    cotangent_low = output_cotangent.reshape(tokens, width)

    mix_cols = gather_columns([query_weight, forget_weight, input_weight, output_gate_weight])
    out_rows = gather_rows(output_weight)
    ffn_cols = gather_columns([ffn_gate_weight, ffn_up_weight])
    down_cols = gather_columns([ffn_down_weight])
    vectors = jnp.stack((mix_gain, bound_logit, ffn_gain), axis=1)
    vectors = gather_small(gather_small(vectors, "seq"), "dp").astype(f32)
    gain_in, logit, gain_mid = (vectors[:, 0], vectors[:, 1], vectors[:, 2])
    segments = gather_small(segment_ids[0], "seq")
    bound = jax.nn.sigmoid(-lax.dynamic_slice_in_dim(logit, rank * my_width, my_width))

    x_all = gather_seq(x_low).astype(f32)
    normed_in = (x_all * rms_factor(x_all) * gain_in).astype(bf16)
    pre = matmul(normed_in, mix_cols)
    gated, mixed, states = recurrence_forward(segments, pre, bound[None, :])
    inputs = x_low.astype(f32)
    resid = inputs + scatter_seq(matmul(gated, out_rows))
    factor_mid = rms_factor(resid)
    unit_mid = resid * factor_mid
    normed_mid = gather_seq((unit_mid * gain_mid).astype(bf16))

    half = ffn_cols.shape[1] // 2
    both = matmul(normed_mid, ffn_cols)
    gate_h, up_h = (both[:, :half], both[:, half:])
    gate_sig = jax.nn.sigmoid(gate_h)
    gate_silu = gate_h * gate_sig
    hidden = (gate_silu * up_h).astype(bf16)
    cotangent_all = gather_seq(cotangent_low)
    down_grad = matmul(cotangent_all, hidden, 0, 0).astype(bf16)
    hidden_grad = matmul(cotangent_all, down_cols)
    gate_grad = (hidden_grad * up_h * (gate_sig * (1.0 + gate_h * (1.0 - gate_sig)))).astype(bf16)
    up_grad = (hidden_grad * gate_silu).astype(bf16)
    ffn_right = jnp.concatenate((gate_grad, up_grad), axis=1)
    mid_grad = scatter_seq(matmul(ffn_right, ffn_cols, 1, 1))
    ffn_grad = matmul(normed_mid, ffn_right, 0, 0).astype(bf16)
    block_output = (resid + scatter_seq(matmul(hidden, down_cols, 1, 1))).astype(bf16)

    cotangent = cotangent_low.astype(f32)
    resid_grad = cotangent + rms_back(mid_grad * gain_mid, unit_mid, factor_mid)
    branch_low = gather_seq(resid_grad.astype(bf16))
    gated_grad = matmul(branch_low, out_rows, 1, 1)
    mix_right, logit_part = recurrence_backward(segments, pre, bound[None, :], mixed, gated_grad, states)
    out_grad = matmul(gated, branch_low, 0, 0).astype(bf16)
    mix_grad = matmul(normed_in, mix_right, 0, 0).astype(bf16)
    in_grad = scatter_seq(matmul(mix_right, mix_cols, 1, 1))
    factor_in = rms_factor(inputs)
    input_grad = resid_grad + rms_back(in_grad * gain_in, inputs * factor_in, factor_in)

    (ffn_down_weight_grad,) = scatter_columns(down_grad, 1)
    ffn_gate_weight_grad, ffn_up_weight_grad = scatter_columns(ffn_grad, 2)
    output_weight_grad = scatter_rows(out_grad)
    query_weight_grad, forget_weight_grad, input_weight_grad, output_gate_weight_grad = scatter_columns(
        mix_grad, 4
    )
    logit_sum = gather_small(sum_small(-logit_part[0] * (1.0 - bound), "dp"), "seq")
    my_rows = mix_gain.shape[0]
    at = (lax.axis_index("dp") * ranks + rank) * my_rows
    bound_logit_grad = lax.dynamic_slice_in_dim(logit_sum, at, my_rows)

    def gain_grad(gain, pairs):
        total = sum(jnp.sum(weight.astype(f32) * grad, axis=1) for weight, grad in pairs)
        return total / gain.astype(f32)

    mix_gain_grad = gain_grad(
        mix_gain,
        (
            (query_weight, query_weight_grad),
            (forget_weight, forget_weight_grad),
            (input_weight, input_weight_grad),
            (output_gate_weight, output_gate_weight_grad),
        ),
    )
    ffn_gain_grad = gain_grad(
        ffn_gain, ((ffn_gate_weight, ffn_gate_weight_grad), (ffn_up_weight, ffn_up_weight_grad))
    )
    return (
        block_output.reshape(rows, length, width),
        input_grad.reshape(rows, length, width),
        mix_gain_grad,
        bound_logit_grad,
        query_weight_grad,
        forget_weight_grad,
        input_weight_grad,
        output_gate_weight_grad,
        output_weight_grad,
        ffn_gain_grad,
        ffn_gate_weight_grad,
        ffn_up_weight_grad,
        ffn_down_weight_grad,
    )


def solution(mesh):
    by_token = P("dp", "seq", None)
    vector = P(("dp", "seq"))
    matrix = P(("dp", "seq"), None)
    return jax.shard_map(
        local,
        mesh=mesh,
        in_specs=(by_token, P("dp", "seq"), vector, vector)
        + (matrix,) * 5
        + (vector,)
        + (matrix,) * 3
        + (by_token,),
        out_specs=(by_token, by_token, vector, vector) + (matrix,) * 5 + (vector,) + (matrix,) * 3,
        check_vma=False,
    )
```

time: 6120 us -> 783 us (0.13)
  waiting for transfers between devices: 5240 us -> 298 us
  other arithmetic: 253 us -> 34.8 us
  matrix products: 331 us -> 148 us
  local copies, waits for them, and re-layouts: 160 us -> 60.1 us
  starting transfers between devices: 4.94 us -> 82.6 us
    reduce_scatter x1 -> x4, waiting for transfers between devices: 4540 us -> 54.9 us  [the longest x3 54.9 us: scatter_columns(): mine = lax.psum_scatter(grad, 'dp', scatter_dimension=0, tiled=True)]
    all_gather x10 -> x4, waiting for transfers between devices: 696 us -> 0.03 us  [the longest x3 0.02 us: gather_columns(): lax.all_gather(pieces.reshape(count * rows, pieces.shape[2]), 'dp', axis=...]
    ppermute x1 -> x30, waiting for transfers between devices: 0.01 us -> 202 us  [the longest x28 186 us: flip(): lax.ppermute(block, axis, [(i, i ^ bits) for i in range(lax.axis_size(axi...]
    dot_general x78 -> x12, matrix products: 331 us -> 148 us  [matmul(): lax.dot_general(left, right, (((left_dim,), (right_dim,)), ((), ())), pre...]
    concatenate x1 -> x10, other arithmetic: 163 us -> 1.97 us  [the longest x2 1.25 us: gather_columns(): pieces = jnp.concatenate(parts, axis=2)]
    all_to_all x0 -> x3, blocking collectives: none -> 85.4 us  [the longest x1 45.3 us: scatter_seq(): lax.all_to_all(pieces, 'seq', split_axis=0, concat_axis=0, tiled=True)]
    unnamed x2 -> x0, blocking collectives: 83.8 us -> none
  transfers between devices with their start and end apart: 12 -> 45, of which waited for: 10 -> 22; matrix products, arithmetic and copies ran while one was open for 4% -> 24% of each run, Pallas kernels for 0% -> 7%
where the time goes in v1:
time: 783 us; the launch traced here: 778 us
  waiting for transfers between devices  298 us (38%)
  matrix products  148 us (19%)
  blocking collectives  85.4 us (11%)
  starting transfers between devices  82.6 us (11%)
  local copies, waits for them, and re-layouts  60.1 us (8%)
  Pallas kernels  54.3 us (7%)
  other arithmetic  34.8 us (4%)
  between operations  15.2 us (2%)
    ppermute x28, waiting for transfers between devices, flip(): lax.ppermute(block, axis, [(i, i ^ bits) for i in range(lax.axis_size(axi...  186 us
    dot_general x12, matrix products, matmul(): lax.dot_general(left, right, (((left_dim,), (right_dim,)), ((), ())), pre...  148 us
    reduce_scatter x3, waiting for transfers between devices, scatter_columns(): mine = lax.psum_scatter(grad, 'dp', scatter_dimension=0, tiled=True)  54.9 us
    all_to_all x1, blocking collectives, scatter_seq(): lax.all_to_all(pieces, 'seq', split_axis=0, concat_axis=0, tiled=True)  45.3 us
    all_to_all x2, blocking collectives, gather_columns(): lax.all_to_all(pieces, 'seq', split_axis=0, concat_axis=0, tiled=True)  40.2 us
    ppermute x28, starting transfers between devices, flip(): lax.ppermute(block, axis, [(i, i ^ bits) for i in range(lax.axis_size(axi...  38 us
    pallas_call x1, Pallas kernels, recurrence_backward(): pl.pallas_call(backward_kernel, grid_spec=pltpu.PrefetchScalarGridSpec(nu...  35.2 us
    all_to_all x3, waiting for transfers between devices, scatter_seq(): lax.all_to_all(pieces, 'seq', split_axis=0, concat_axis=0, tiled=True)  32.9 us
  transfers between devices with their start and end apart: 45, of which 22 were waited for; matrix products, arithmetic and copies ran while one was open for 24% of the time, Pallas kernels for 7%

profile of v1, /device:TPU:1, one launch (start us, length us, event | category | flops | bytes accessed | tf_op | source)
XLA Modules:
  0.0 778.1 jit_solution(16989190907199731994)
XLA Ops:
  13.2 17.0 %all_to_all.50 = bf16[4,64,2048]{2,1,0:T(8,128)(2,1)} all-to-all(bf16[4,64,2048]{2,1,0:T(8,128)(2,1)S(1)} %copy.55), channel_id=1, replica_groups=mesh['dp'=8,'seq'=4] {'seq'}, dimensions={0} | all-to-all | bytes 2097152 | tf_op jit(solution)/shard_map/all_to_all | solution.py:77
  42.7 23.1 %all_to_all.51 = bf16[4,64,2816]{2,1,0:T(8,128)(2,1)} all-to-all(bf16[4,64,2816]{2,1,0:T(8,128)(2,1)S(1)} %copy.57), channel_id=1, replica_groups=mesh['dp'=8,'seq'=4] {'seq'}, dimensions={0} | all-to-all | bytes 2883584 | tf_op jit(solution)/shard_map/all_to_all | solution.py:77
  77.3 10.2 %collective-permute-done.6 = bf16[64,3]{0,1:T(4,128)(2,1)S(1)} collective-permute-done((bf16[64,3]{0,1:T(4,128)(2,1)S(1)}, bf16[64,3]{0,1:T(4,128)(2,1)S(1)}, u32[]{:S(2)}, u32[]{:S(2)}) %collective-permute-start.6) | collective-permute-done | bytes 416 | tf_op jit(solution)/shard_map/ppermute | solution.py:21
  91.7 10.2 %collective-permute-start.8 = (bf16[256,3]{0,1:T(4,128)(2,1)S(1)}, bf16[256,3]{0,1:T(4,128)(2,1)S(1)}, u32[]{:S(2)}, u32[]{:S(2)}) collective-permute-start(bf16[256,3]{0,1:T(4,128)(2,1)S(1)} %pad_maximum_fusion.9), channel_id=1, source_target_pairs={{0,4},{4,0},{8,12},{12,8},{16,20},{20,16},{24,28},{28,24},{1,5},{5... | collective-permute-start | bytes 4616 | tf_op jit(solution)/shard_map/ppermute | solution.py:21
  135.7 12.7 %fusion.16.pre_ref = f32[1024,2048]{1,0:T(8,128)S(1)} fusion(bf16[2048,2048]{1,0:T(8,128)(2,1)} %all-gather.5.cloned.1.call-done, bf16[1024,2048]{1,0:T(8,128)(2,1)} %constant_dynamic-update-slice_fusion.15, f32[2048]{0:T(1024)S(1)} %bitcast.157, f32[1024]{0:T(1024)S(1)} %add_rsqrt_fusion), kind=kOutput, calls=%fused_computation.52 | convolution fusion | flops 8598323200 | bytes 20983808 | tf_op jit(solution)/shard_map/dot_general | solution.py:308
  148.4 19.1 %recurrence_forward.1 = (bf16[1024,512]{1,0:T(8,128)(2,1)S(1)}, f32[1024,512]{1,0:T(8,128)S(1)}, f32[8,4,128,128]{3,2,1,0:T(8,128)S(1)}) custom-call(s32[1024]{0:T(1024)S(1)} %pad_add_fusion.seg_ref, s32[1024,1]{1,0:T(8,128)S(1)} %copy.56.seg_col_ref, s32[1,1024]{1,0:T(1,128)S(1)} %bitcast.115, f32[1024,2048]{1,0:T(8,128)S(1)} %fusion.16.pre_ref, ...), custom_call_target="tpu_custom_call" | custom-call | tf_op jit(solution)/shard_map/recurrence_forward/pallas_call | solution.py:240
  188.8 63.8 %collective-permute-done.16 = bf16[256,2048]{1,0:T(8,128)(2,1)S(1)} collective-permute-done((bf16[256,2048]{1,0:T(8,128)(2,1)}, bf16[256,2048]{1,0:T(8,128)(2,1)S(1)}, u32[]{:S(2)}, u32[]{:S(2)}) %collective-permute-start.16) | collective-permute-done | bytes 1048608 | tf_op jit(solution)/shard_map/ppermute | solution.py:21
  285.1 10.9 %collective-permute-done.19 = bf16[128,2048]{1,0:T(8,128)(2,1)S(1)} collective-permute-done((bf16[128,2048]{1,0:T(8,128)(2,1)S(1)}, bf16[128,2048]{1,0:T(8,128)(2,1)S(1)}, u32[]{:S(2)}, u32[]{:S(2)}) %collective-permute-start.19) | collective-permute-done | bytes 524320 | tf_op jit(solution)/shard_map/ppermute | solution.py:21
  307.3 18.7 %fusion.26 = f32[1024,2816]{1,0:T(8,128)} fusion(bf16[1024,2048]{1,0:T(8,128)(2,1)} %constant_dynamic-update-slice_fusion.10, bf16[2048,2816]{1,0:T(8,128)(2,1)} %all-gather.9.cloned.1.call-done), kind=kOutput, calls=%fused_computation.130 | convolution fusion | flops 11811160064 | bytes 27262976 | tf_op jit(solution)/shard_map/dot_general | solution.py:308
  326.0 15.9 %multiply_convert_fusion.1 = (bf16[1024,1408]{1,0:T(8,128)(2,1)}, bf16[1024,1408]{1,0:T(8,128)(2,1)}, bf16[1024,1408]{1,0:T(8,128)(2,1)S(1)}) fusion(f32[1024,2816]{1,0:T(8,128)} %fusion.26, bf16[1024,2048]{1,0:T(8,128)(2,1)} %constant_dynamic-update-slice_fusion.5, bf16[2048,1408]{1,0:T(8,128)(2,1)} %all-gather.11.cloned.1.call-done), kind=kOutput, calls=%fused_computation.14 | convolution fusion | flops 5927206912 | bytes 30146560 | tf_op jit(solution)/shard_map/dot_general | solution.py:308
  343.5 10.8 %convolution_convert_fusion.1 = bf16[2048,1408]{1,0:T(8,128)(2,1)} fusion(bf16[1024,2048]{1,0:T(8,128)(2,1)} %constant_dynamic-update-slice_fusion.5, bf16[1024,1408]{1,0:T(8,128)(2,1)S(1)} %get-tuple-element.33), kind=kOutput, calls=%fused_computation.10 | convolution fusion | flops 5908463616 | bytes 12845056 | tf_op jit(solution)/shard_map/dot_general | solution.py:308
  354.5 16.8 %convolution_convert_fusion.3 = bf16[1024,2048]{1,0:T(8,128)(2,1)S(1)} fusion(bf16[2048,2816]{1,0:T(8,128)(2,1)} %all-gather.9.cloned.1.call-done, bf16[1024,1408]{1,0:T(8,128)(2,1)} %get-tuple-element.32, bf16[1024,1408]{1,0:T(8,128)(2,1)} %get-tuple-element.31), kind=kOutput, calls=%fused_computation.18 | convolution fusion | flops 11824791552 | bytes 21495808 | tf_op jit(solution)/shard_map/dot_general | solution.py:308
  371.3 45.3 %all_to_all.52 = bf16[4,256,2048]{2,1,0:T(8,128)(2,1)S(1)} all-to-all(bf16[4,256,2048]{2,1,0:T(8,128)(2,1)S(1)} %bitcast.131), channel_id=1, replica_groups=mesh['dp'=8,'seq'=4] {'seq'}, dimensions={0} | all-to-all | bytes 8388608 | tf_op jit(solution)/shard_map/all_to_all | solution.py:68
  422.6 17.2 %collective-permute-done.20 = bf16[256,2048]{1,0:T(8,128)(2,1)S(1)} collective-permute-done((bf16[256,2048]{1,0:T(8,128)(2,1)S(1)}, bf16[256,2048]{1,0:T(8,128)(2,1)S(1)}, u32[]{:S(2)}, u32[]{:S(2)}) %collective-permute-start.20) | collective-permute-done | bytes 1048608 | tf_op jit(solution)/shard_map/ppermute | solution.py:21
  442.0 11.6 %collective-permute-done.22 = bf16[128,2048]{1,0:T(8,128)(2,1)S(1)} collective-permute-done((bf16[128,2048]{1,0:T(8,128)(2,1)S(1)}, bf16[128,2048]{1,0:T(8,128)(2,1)S(1)}, u32[]{:S(2)}, u32[]{:S(2)}) %collective-permute-start.22) | collective-permute-done | bytes 524320 | tf_op jit(solution)/shard_map/ppermute | solution.py:21
  468.3 35.2 %recurrence_backward.1 = (bf16[1024,2048]{1,0:T(8,128)(2,1)S(1)}, f32[1,512]{1,0:T(1,128)S(1)}) custom-call(s32[1024]{0:T(1024)S(1)} %pad_add_fusion.seg_ref, s32[1024,1]{1,0:T(8,128)S(1)} %copy.56.seg_col_ref, s32[1,1024]{1,0:T(1,128)S(1)} %bitcast.116, f32[1024,2048]{1,0:T(8,128)S(1)} %copy-done.1, f32[1,512]{1,0:T(1,128)S(1)} %bitcast.118, ...), custom_call_target="tpu_custom_call" | custom-call | tf_op jit(solution)/shard_map/recurrence_backward/pallas_call | solution.py:273
  505.5 14.1 %convolution_convert_fusion.2 = bf16[2048,2048]{1,0:T(8,128)(2,1)} fusion(bf16[1024,2048]{1,0:T(8,128)(2,1)S(1)} %get-tuple-element.21, bf16[1024,2048]{1,0:T(8,128)(2,1)} %constant_dynamic-update-slice_fusion.15, f32[2048]{0:T(1024)S(1)} %bitcast.158, f32[1024]{0:T(1024)S(1)} %add_rsqrt_fusion), kind=kOutput, calls=%fused_computation.11 | convolution fusion | flops 8602517504 | bytes 16789504 | tf_op jit(solution)/shard_map/dot_general | solution.py:308
  519.6 18.7 %convolution_convert_fusion = bf16[2048,2816]{1,0:T(8,128)(2,1)} fusion(bf16[1024,2048]{1,0:T(8,128)(2,1)} %constant_dynamic-update-slice_fusion.10, bf16[1024,1408]{1,0:T(8,128)(2,1)} %get-tuple-element.32, bf16[1024,1408]{1,0:T(8,128)(2,1)} %get-tuple-element.31), kind=kOutput, calls=%fused_computation | convolution fusion | flops 11828461568 | bytes 21495808 | tf_op jit(solution)/shard_map/dot_general | solution.py:308
  538.3 11.1 %convolution_convert_fusion.5 = bf16[1024,2048]{1,0:T(8,128)(2,1)} fusion(bf16[1024,1408]{1,0:T(8,128)(2,1)} %copy-done.47, bf16[2048,1408]{1,0:T(8,128)(2,1)} %all-gather.11.cloned.1.call-done), kind=kOutput, calls=%fused_computation.20 | convolution fusion | flops 5907677184 | bytes 12845056 | tf_op jit(solution)/shard_map/dot_general | solution.py:308
  554.3 14.0 %convolution_convert_fusion.4 = bf16[1024,2048]{1,0:T(8,128)(2,1)} fusion(bf16[1024,2048]{1,0:T(8,128)(2,1)} %copy-done.4, bf16[2048,2048]{1,0:T(8,128)(2,1)} %all-gather.5.cloned.1.call-done), kind=kOutput, calls=%fused_computation.19 | convolution fusion | flops 8592031744 | bytes 16777216 | tf_op jit(solution)/shard_map/dot_general | solution.py:308
  568.2 32.9 %all-to-all-done.4 = bf16[4,256,2048]{2,1,0:T(8,128)(2,1)} async-done(((bf16[4,256,2048]{2,1,0:T(8,128)(2,1)}), bf16[4,256,2048]{2,1,0:T(8,128)(2,1)}, u32[]{:S(2)}, u32[]{:S(2)}) %all-to-all-start.4) | async-done | bytes 4194336 | tf_op jit(solution)/shard_map/all_to_all | solution.py:68
  617.3 35.0 %collective-permute-done.27 = f32[512]{0:T(512)S(1)} collective-permute-done((f32[512]{0:T(512)S(1)}, f32[512]{0:T(512)S(1)}, u32[]{:S(2)}, u32[]{:S(2)}) %collective-permute-start.27) | collective-permute-done | bytes 2080 | tf_op jit(solution)/shard_map/ppermute | solution.py:21
  685.5 11.7 %collective-permute-done.29 = bf16[64,2048]{1,0:T(8,128)(2,1)S(1)} collective-permute-done((bf16[64,2048]{1,0:T(8,128)(2,1)}, bf16[64,2048]{1,0:T(8,128)(2,1)S(1)}, u32[]{:S(2)}, u32[]{:S(2)}) %collective-permute-start.29) | collective-permute-done | bytes 262176 | tf_op jit(solution)/shard_map/ppermute | solution.py:110
  697.9 54.9 %reduce-scatter.9.cloned.1.call-done = bf16[256,2816]{1,0:T(8,128)(2,1)} async-done(((bf16[2048,2816]{1,0:T(8,128)(2,1)}), bf16[256,2816]{1,0:T(8,128)(2,1)}) %reduce-scatter.9.cloned.1.call-update) | async-done | bytes 1441808 | tf_op jit(solution)/shard_map/reduce_scatter | solution.py:83
  (287 shorter events, 232.1 us)
Async XLA Ops:
  7.2 128.5 %all-gather.5.cloned.1.call-start = ((), (), s32[]{:S(2)}) async-start(), calls=%async_computation.14 | async-start | bytes 9437184 | tf_op jit(solution)/shard_map/all_gather | solution.py:78
  30.2 142.8 %all-gather.7.cloned.1.call-start = ((), (), s32[]{:S(2)}) async-start(), calls=%async_computation.15 | async-start | bytes 2359296 | tf_op jit(solution)/shard_map/all_gather | solution.py:104
  41.4 265.9 %all-gather.9.cloned.1.call-start = ((), (), s32[]{:S(2)}) async-start(), calls=%async_computation.16 | async-start | bytes 12976128 | tf_op jit(solution)/shard_map/all_gather | solution.py:78
  65.9 50.7 %collective-permute-start.2 = (bf16[256,2048]{1,0:T(8,128)(2,1)S(1)}, bf16[256,2048]{1,0:T(8,128)(2,1)}, u32[]{:S(2)}, u32[]{:S(2)}) collective-permute-start(bf16[256,2048]{1,0:T(8,128)(2,1)S(1)} %bitcast.119), channel_id=1, source_target_pairs={{0,1},{1,0},{2,3},{3,2},{4,5},{5,4},{6,7},{7,6},{8,9},{9,8},{10,11... | collective-permute-start | bytes 3145736 | tf_op jit(solution)/shard_map/ppermute | solution.py:21
  66.0 52.5 %collective-permute-start.3 = (bf16[256,2048]{1,0:T(8,128)(2,1)S(1)}, bf16[256,2048]{1,0:T(8,128)(2,1)}, u32[]{:S(2)}, u32[]{:S(2)}) collective-permute-start(bf16[256,2048]{1,0:T(8,128)(2,1)S(1)} %bitcast.120), channel_id=1, source_target_pairs={{0,2},{1,3},{2,0},{3,1},{4,6},{5,7},{6,4},{7,5},{8,10},{9,11},{10,... | collective-permute-start | bytes 3145736 | tf_op jit(solution)/shard_map/ppermute | solution.py:21
  67.3 20.2 %collective-permute-start.6 = (bf16[64,3]{0,1:T(4,128)(2,1)S(1)}, bf16[64,3]{0,1:T(4,128)(2,1)S(1)}, u32[]{:S(2)}, u32[]{:S(2)}) collective-permute-start(bf16[64,3]{0,1:T(4,128)(2,1)S(1)} %pad_maximum_fusion.10), channel_id=1, source_target_pairs={{0,1},{1,0},{2,3},{3,2},{4,5},{5,4},{6,7},{7,6},{8,9},{9,8},{10,11... | collective-permute-start | bytes 1160 | tf_op jit(solution)/shard_map/ppermute | solution.py:21
  68.0 20.1 %collective-permute-start = (s32[256]{0:T(256)S(1)}, s32[256]{0:T(256)S(1)}, u32[]{:S(2)}, u32[]{:S(2)}) collective-permute-start(s32[256]{0:T(256)S(1)} %bitcast.169), channel_id=1, source_target_pairs={{0,1},{1,0},{2,3},{3,2},{4,5},{5,4},{6,7},{7,6},{8,9},{9,8},{10,11... | collective-permute-start | bytes 3080 | tf_op jit(solution)/shard_map/ppermute | solution.py:21
  69.9 109.3 %all-to-all-start.3 = ((bf16[4,64,1408]{2,1,0:T(8,128)(2,1)}), bf16[4,64,1408]{2,1,0:T(8,128)(2,1)S(1)}, u32[]{:S(2)}, u32[]{:S(2)}) async-start(bf16[4,64,1408]{2,1,0:T(8,128)(2,1)} %copy.58), calls=%async_computation.3 | async-start | bytes 1441792 | tf_op jit(solution)/shard_map/all_to_all | solution.py:77
  180.1 74.8 %all-to-all-start.1 = ((bf16[4,256,2048]{2,1,0:T(8,128)(2,1)}), bf16[4,256,2048]{2,1,0:T(8,128)(2,1)}, u32[]{:S(2)}, u32[]{:S(2)}) async-start(bf16[4,256,2048]{2,1,0:T(8,128)(2,1)} %bitcast.129), calls=%async_computation.1 | async-start | bytes 8388608 | tf_op jit(solution)/shard_map/all_to_all | solution.py:68
  185.0 141.1 %all-gather.11.cloned.1.call-start = ((), (), s32[]{:S(2)}) async-start(), calls=%async_computation.17 | async-start | bytes 6488064 | tf_op jit(solution)/shard_map/all_gather | solution.py:78
  185.5 473.2 %reduce-scatter.11.cloned.1.call-start = ((), (), s32[]{:S(2)}) async-start(), calls=%async_computation.21 | async-start | bytes 6488064 | tf_op jit(solution)/shard_map/reduce_scatter | solution.py:83
  186.1 66.5 %collective-permute-start.16 = (bf16[256,2048]{1,0:T(8,128)(2,1)}, bf16[256,2048]{1,0:T(8,128)(2,1)S(1)}, u32[]{:S(2)}, u32[]{:S(2)}) collective-permute-start(bf16[256,2048]{1,0:T(8,128)(2,1)} %bitcast.121), channel_id=1, source_target_pairs={{0,1},{1,0},{2,3},{3,2},{4,5},{5,4},{6,7},{7,6},{8,9},{9,8},{10,11... | collective-permute-start | bytes 3145736 | tf_op jit(solution)/shard_map/ppermute | solution.py:21
  187.6 80.1 %collective-permute-start.17 = (bf16[256,2048]{1,0:T(8,128)(2,1)}, bf16[256,2048]{1,0:T(8,128)(2,1)}, u32[]{:S(2)}, u32[]{:S(2)}) collective-permute-start(bf16[256,2048]{1,0:T(8,128)(2,1)} %bitcast.122), channel_id=1, source_target_pairs={{0,2},{1,3},{2,0},{3,1},{4,6},{5,7},{6,4},{7,5},{8,10},{9,11},{10,... | collective-permute-start | bytes 3145736 | tf_op jit(solution)/shard_map/ppermute | solution.py:21
  263.4 21.4 %collective-permute-start.12 = (bf16[256,2048]{1,0:T(8,128)(2,1)S(1)}, bf16[256,2048]{1,0:T(8,128)(2,1)S(1)}, u32[]{:S(2)}, u32[]{:S(2)}) collective-permute-start(bf16[256,2048]{1,0:T(8,128)(2,1)S(1)} %get-tuple-element.30), channel_id=1, source_target_pairs={{0,1},{1,0},{2,3},{3,2},{4,5},{5,4},{6,7},{7,6},{8,9},{9,8},{10,11... | collective-permute-start | bytes 3145736 | tf_op jit(solution)/shard_map/ppermute | solution.py:21
  263.7 33.2 %collective-permute-start.13 = (bf16[256,2048]{1,0:T(8,128)(2,1)S(1)}, bf16[256,2048]{1,0:T(8,128)(2,1)S(1)}, u32[]{:S(2)}, u32[]{:S(2)}) collective-permute-start(bf16[256,2048]{1,0:T(8,128)(2,1)S(1)} %get-tuple-element.30), channel_id=1, source_target_pairs={{0,2},{1,3},{2,0},{3,1},{4,6},{5,7},{6,4},{7,5},{8,10},{9,11},{10,... | collective-permute-start | bytes 3145736 | tf_op jit(solution)/shard_map/ppermute | solution.py:21
  268.8 27.2 %collective-permute-start.19 = (bf16[128,2048]{1,0:T(8,128)(2,1)S(1)}, bf16[128,2048]{1,0:T(8,128)(2,1)S(1)}, u32[]{:S(2)}, u32[]{:S(2)}) collective-permute-start(bf16[128,2048]{1,0:T(8,128)(2,1)S(1)} %slice.83), channel_id=1, source_target_pairs={{0,1},{1,0},{2,3},{3,2},{4,5},{5,4},{6,7},{7,6},{8,9},{9,8},{10,11... | collective-permute-start | bytes 1572872 | tf_op jit(solution)/shard_map/ppermute | solution.py:21
  354.4 313.7 %reduce-scatter.7.cloned.1.call-start = ((), (), s32[]{:S(2)}) async-start(), calls=%async_computation.19 | async-start | bytes 2359296 | tf_op jit(solution)/shard_map/reduce_scatter | solution.py:108
  459.5 215.0 %reduce-scatter.5.cloned.1.call-start = ((), (), s32[]{:S(2)}) async-start(), calls=%async_computation.18 | async-start | bytes 9437184 | tf_op jit(solution)/shard_map/reduce_scatter | solution.py:83
  519.6 233.3 %reduce-scatter.9.cloned.1.call-start = ((), (), s32[]{:S(2)}) async-start(), calls=%async_computation.20 | async-start | bytes 12976128 | tf_op jit(solution)/shard_map/reduce_scatter | solution.py:83
  549.3 51.8 %all-to-all-start.4 = ((bf16[4,256,2048]{2,1,0:T(8,128)(2,1)}), bf16[4,256,2048]{2,1,0:T(8,128)(2,1)}, u32[]{:S(2)}, u32[]{:S(2)}) async-start(bf16[4,256,2048]{2,1,0:T(8,128)(2,1)} %bitcast.130), calls=%async_computation.4 | async-start | bytes 8388608 | tf_op jit(solution)/shard_map/all_to_all | solution.py:68
  601.1 57.6 %all-to-all-start.6 = ((bf16[4,256,2048]{2,1,0:T(8,128)(2,1)}), bf16[4,256,2048]{2,1,0:T(8,128)(2,1)}, u32[]{:S(2)}, u32[]{:S(2)}) async-start(bf16[4,256,2048]{2,1,0:T(8,128)(2,1)} %bitcast.128), calls=%async_computation.6 | async-start | bytes 8388608 | tf_op jit(solution)/shard_map/all_to_all | solution.py:68
  615.6 36.7 %collective-permute-start.27 = (f32[512]{0:T(512)S(1)}, f32[512]{0:T(512)S(1)}, u32[]{:S(2)}, u32[]{:S(2)}) collective-permute-start(f32[512]{0:T(512)S(1)} %add.167), channel_id=1, source_target_pairs={{0,1},{1,0},{2,3},{3,2},{4,5},{5,4},{6,7},{7,6},{8,9},{9,8},{10,11... | collective-permute-start | bytes 6152 | tf_op jit(solution)/shard_map/ppermute | solution.py:21
  668.1 29.0 %collective-permute-start.29 = (bf16[64,2048]{1,0:T(8,128)(2,1)}, bf16[64,2048]{1,0:T(8,128)(2,1)S(1)}, u32[]{:S(2)}, u32[]{:S(2)}) collective-permute-start(bf16[64,2048]{1,0:T(8,128)(2,1)} %reduce-scatter.7.cloned.1.call-done), channel_id=1, source_target_pairs={{0,0},{4,1},{8,2},{12,3},{16,4},{20,5},{24,6},{28,7},{1,8},{5,9},{... | collective-permute-start | bytes 786440 | tf_op jit(solution)/shard_map/ppermute | solution.py:110
  674.5 23.5 %all-to-all-start.7 = ((bf16[4,64,2048]{2,1,0:T(8,128)(2,1)}), bf16[4,64,2048]{2,1,0:T(8,128)(2,1)}, u32[]{:S(2)}, u32[]{:S(2)}) async-start(bf16[4,64,2048]{2,1,0:T(8,128)(2,1)} %bitcast.147), calls=%async_computation.8 | async-start | bytes 2097152 | tf_op jit(solution)/shard_map/all_to_all | solution.py:85
  (69 other events, 621.8 us)
Sparse Core Ops, SparseCore 0:
  30.4 85.3 all-gather.4
  118.0 27.9 all-gather.6
  147.6 107.5 all-gather.8
  257.2 58.6 all-gather.10
  354.5 66.2 reduce-scatter.10
  459.6 40.4 reduce-scatter.6
  519.7 95.3 reduce-scatter.4
  617.4 135.4 reduce-scatter.8

commit v2 on v1

v2 whole, which is shorter than its diff:
```python
import functools

import jax
import jax.numpy as jnp
from jax import lax
from jax.experimental import pallas as pl
from jax.experimental.pallas import tpu as pltpu
from jax.sharding import PartitionSpec as P

HEAD_FEATURES = 128
LANES = 128

eps_model = 1e-06
eps_group = 1e-05
highest = lax.Precision.HIGHEST
f32 = jnp.float32
bf16 = jnp.bfloat16

vmem = pltpu.CompilerParams(vmem_limit_bytes=48 * 1024 * 1024)


def cost(flops, moved=0):
    return pl.CostEstimate(flops=flops, bytes_accessed=moved, transcendentals=0)


def flip(block, axis, bits):
    return lax.ppermute(block, axis, [(i, i ^ bits) for i in range(lax.axis_size(axis))])


def gather_small(block, axis):
    count, mine = (lax.axis_size(axis), lax.axis_index(axis))
    bit = 1
    while bit < count:
        other = flip(block, axis, bit)
        upper = (mine & bit) != 0
        block = jnp.concatenate(
            (jnp.where(upper, other, block), jnp.where(upper, block, other)), axis=0
        )
        bit *= 2
    return block


def sum_small(block, axis):
    count = lax.axis_size(axis)
    bit = 1
    while bit < count:
        block = block + flip(block, axis, bit)
        bit *= 2
    return block


def slots():
    if lax.axis_size("seq") == 4:
        return [(1, 0), (3, 0), (2, 1), (3, 1), (0, 0), (0, 1), (2, 0), (1, 1)]
    return [(k, h) for k in range(lax.axis_size("seq")) for h in range(2)]


def slot_table():
    place = {slot: i for i, slot in enumerate(slots())}
    count = lax.axis_size("seq")
    table = jnp.array([[place[k, h] for h in range(2)] for k in range(count)], jnp.int32)
    return table[jnp.arange(count) ^ lax.axis_index("seq")].reshape(2 * count)


def row_places():
    k, h = (jnp.array(bits, jnp.int32) for bits in zip(*slots()))
    return (k ^ lax.axis_index("seq")) * 2 + h


def gather_seq(block, second=()):
    count = lax.axis_size("seq")
    half = block.shape[0] // 2
    if count == 4:
        near = flip(block, "seq", 1)
        far = flip(block, "seq", 2)
        corner_top = flip(after(near[:half], *second), "seq", 2)
        corner_low = flip(after(far[half:], *second), "seq", 1)
        found = {(3, 0): (3, 0), (3, 1): (4, 0)}
        for k in range(3):
            found[k, 0], found[k, 1] = ((k, 0), (k, half))
        return (block, near, far, corner_top, corner_low), [found[slot] for slot in slots()]
    bit = 1
    while bit < count:
        block = jnp.concatenate((block, flip(block, "seq", bit)), axis=0)
        bit *= 2
    return (block,), [(0, i * half) for i in range(2 * count)]


def partial_layout(tokens):
    count = lax.axis_size("seq")
    if count == 4:
        return [(0, 2, bf16), (2, 4, bf16), (4, 8, f32)]
    return [(0, 2 * count, f32)]


def scatter_seq(partials, half, beside=()):
    if len(partials) == 3:
        near, far, rest = partials
        near = flip(near, "seq", 1)
        far = flip(far, "seq", 2)
        rest = after(rest, *beside)
        across = (rest[2 * half : 3 * half] + near[half:].astype(f32)).astype(bf16)
        along = (rest[3 * half :] + far[half:].astype(f32)).astype(bf16)
        return (rest, near, far, flip(across, "seq", 2), flip(along, "seq", 1))
    (total,) = partials
    bit = lax.axis_size("seq") // 2
    while bit:
        middle = total.shape[0] // 2
        total = total[:middle] + flip(total[middle:].astype(bf16), "seq", bit).astype(f32)
        bit //= 2
    return (total,)


def swap_seq(pieces):
    return lax.all_to_all(pieces, "seq", split_axis=0, concat_axis=0, tiled=True)


def gather_dp(block):
    return lax.all_gather(block, "dp", axis=0, tiled=True)


def scatter_dp(mine):
    groups = [list(range(c, lax.axis_size("dp"), 2)) for c in range(2)]
    return lax.psum_scatter(
        mine, "dp", scatter_dimension=0, axis_index_groups=groups, tiled=True
    )


def row_route():
    count, ranks = (lax.axis_size("dp"), lax.axis_size("seq"))
    return [(b, (b % count) * ranks + b // count) for b in range(count * ranks)]


def after(value, *others):
    return lax.optimization_barrier((value,) + others)[0]


def block(*shape, at=None):
    return pl.BlockSpec(shape, at or (lambda *_: (0,) * len(shape)))


def column_blocks(width, interleave):
    size = LANES if interleave else width
    return [(j * size, size) for j in range(width // size)]


def pieces_kernel(interleave, *refs):
    weights, out_ref = (refs[:-1], refs[-1])
    blocks = column_blocks(weights[0].shape[1], interleave)
    at = 0
    for start, size in blocks:
        for ref in weights:
            out_ref[0, :, at : at + size] = ref[:, start : start + size]
            at += size


def column_pieces(weights, interleave=False):
    ranks = lax.axis_size("seq")
    rows, width = (weights[0].shape[0], weights[0].shape[1] // ranks)
    if width % LANES:
        parts = [jnp.moveaxis(w.reshape(rows, ranks, width), 1, 0) for w in weights]
        return jnp.concatenate(parts, axis=2)
    total = width * len(weights)
    return pl.pallas_call(
        functools.partial(pieces_kernel, interleave),
        grid=(ranks,),
        in_specs=[block(rows, width, at=lambda r: (0, r)) for _ in weights],
        out_specs=block(1, rows, total, at=lambda r: (r, 0, 0)),
        out_shape=jax.ShapeDtypeStruct((ranks, rows, total), bf16),
        compiler_params=vmem,
        cost_estimate=cost(0, 4 * rows * total * ranks),
        name="column_pieces",
    )(*weights)


def return_kernel(interleave, count, *refs):
    pieces_ref, weights, grads, (gain_ref,) = (
        refs[0],
        refs[1 : 1 + count],
        refs[1 + count : 1 + 2 * count],
        refs[1 + 2 * count :],
    )

    @pl.when(pl.program_id(0) == 0)
    def _():
        gain_ref[...] = jnp.zeros_like(gain_ref)

    at = 0
    total = jnp.zeros(gain_ref.shape, f32)
    for start, size in column_blocks(weights[0].shape[1], interleave):
        for weight_ref, grad_ref in zip(weights, grads):
            grad = pieces_ref[0, :, at : at + size].astype(f32)
            grad_ref[:, start : start + size] = grad
            weight = weight_ref[:, start : start + size].astype(f32)
            total += jnp.sum(weight * grad, axis=1, keepdims=True)
            at += size
    gain_ref[...] += total


def return_columns(mine, weights, interleave=False):
    ranks = lax.axis_size("seq")
    rows, width = (weights[0].shape[0], weights[0].shape[1] // ranks)
    total = width * len(weights)
    pieces = swap_seq(mine.reshape(ranks, rows, total))
    if width % LANES:
        grads = [
            jnp.moveaxis(pieces[:, :, i * width : (i + 1) * width], 0, 1)
            .reshape(rows, ranks * width)
            .astype(f32)
            for i in range(len(weights))
        ]
        return grads, sum(jnp.sum(w.astype(f32) * g, axis=1) for w, g in zip(weights, grads))
    columns = block(rows, width, at=lambda r: (0, r))
    *grads, sums = pl.pallas_call(
        functools.partial(return_kernel, interleave, len(weights)),
        grid=(ranks,),
        in_specs=[block(1, rows, total, at=lambda r: (r, 0, 0))] + [columns] * len(weights),
        out_specs=[columns] * len(weights) + [block(rows, 1)],
        out_shape=[jax.ShapeDtypeStruct(w.shape, f32) for w in weights]
        + [jax.ShapeDtypeStruct((rows, 1), f32)],
        compiler_params=vmem,
        cost_estimate=cost(0, 8 * rows * total * ranks),
        name="return_columns",
    )(pieces, *weights)
    return grads, sums[:, 0]


def product(left, right, left_dim, right_dim, precision=highest):
    return lax.dot_general(
        left,
        right,
        (((left_dim,), (right_dim,)), ((), ())),
        precision=precision,
        preferred_element_type=f32,
    )


def chunk_parts(chunk, seg_ref, seg_col_ref, seg_row_ref, pre_ref, bound_ref):
    size, wide = pre_ref.shape
    width = wide // 3
    first = chunk * size
    prior = seg_ref[jnp.maximum(first - 1, 0)]
    last = seg_ref[first + size - 1]
    seg_col = seg_col_ref[...]
    at = lax.broadcasted_iota(jnp.int32, (size, size), 0)
    of = lax.broadcasted_iota(jnp.int32, (size, size), 1)
    seen = (seg_col == seg_row_ref[...]) & (at >= of)
    linked = (seg_col == prior).astype(f32)
    tail = (seg_col == last).astype(f32)
    linked_last = (prior == last).astype(f32)
    query_pre = pre_ref[:, 0:width]
    forget_pre = pre_ref[:, width : 2 * width]
    value = pre_ref[:, 2 * width : 3 * width]
    forget_sig = jax.nn.sigmoid(-forget_pre)
    key = bound_ref[...] * forget_sig
    query_sig = jax.nn.sigmoid(query_pre)
    lower = (at >= of).astype(f32)
    cumul = product(lower, jnp.log1p(-key), 1, 0)
    grow = jnp.exp(cumul)
    shrink = jnp.exp(-cumul)
    end = grow[size - 1 :, :]
    query_d = query_pre * query_sig * grow
    key_d = key * shrink
    key_t = key_d * end * tail
    keep = end * linked_last
    return locals()


def forward_kernel(seg_ref, slot_ref, seg_col_ref, seg_row_ref, pre_ref, bound_ref, mixed_ref, states_ref, state_ref):
    step = pl.program_id(0)
    heads = mixed_ref.shape[1] // HEAD_FEATURES

    @pl.when(step == 0)
    def _():
        state_ref[...] = jnp.zeros_like(state_ref)

    p = chunk_parts(step, seg_ref, seg_col_ref, seg_row_ref, pre_ref, bound_ref)
    for h in range(heads):
        cols = slice(h * HEAD_FEATURES, (h + 1) * HEAD_FEATURES)
        query_d, key_d, value = p["query_d"][:, cols], p["key_d"][:, cols], p["value"][:, cols]
        state = state_ref[h]
        states_ref[0, h] = state
        scores = jnp.where(p["seen"], product(query_d, key_d, 1, 1), 0.0)
        mixed = product(scores, value, 1, 0) + product(query_d * p["linked"], state, 1, 1)
        mixed_ref[:, cols] = mixed
        state_ref[h] = state * p["keep"][:, cols] + product(value, p["key_t"][:, cols], 0, 0)


def backward_kernel(seg_ref, slot_ref, seg_col_ref, seg_row_ref, pre_ref, bound_ref, outgate_pre_ref, mixed_ref, gated_grad_ref, states_ref, grads_ref, logit_ref, back_ref, through_ref):
    step = pl.program_id(0)
    chunk = pl.num_programs(0) - 1 - step
    width = mixed_ref.shape[1]
    heads = width // HEAD_FEATURES

    @pl.when(step == 0)
    def _():
        back_ref[...] = jnp.zeros_like(back_ref)
        through_ref[...] = jnp.zeros_like(through_ref)
        logit_ref[...] = jnp.zeros_like(logit_ref)

    p = chunk_parts(chunk, seg_ref, seg_col_ref, seg_row_ref, pre_ref, bound_ref)
    query_pre, query_sig = p["query_pre"], p["query_sig"]
    upper = (p["at"] <= p["of"]).astype(f32)
    for h in range(heads):
        cols = slice(h * HEAD_FEATURES, (h + 1) * HEAD_FEATURES)
        query_d, key_d, key_t, value = (p[k][:, cols] for k in ("query_d", "key_d", "key_t", "value"))
        grow, shrink, end, keep, key = (p[k][:, cols] for k in ("grow", "shrink", "end", "keep", "key"))
        state = states_ref[0, h]
        back = back_ref[h]
        mixed = mixed_ref[:, cols]
        factor = lax.rsqrt(jnp.mean(mixed * mixed, axis=-1, keepdims=True) + eps_group)
        normed = mixed * factor
        gated_grad = gated_grad_ref[:, cols]
        gate = outgate_pre_ref[:, cols]
        gate_sig = jax.nn.sigmoid(gate)
        outgate_grad = gated_grad * normed * (gate_sig * (1.0 + gate * (1.0 - gate_sig)))
        weighted = gated_grad * (gate * gate_sig)
        mixed_grad = factor * (
            weighted - normed * jnp.mean(weighted * normed, axis=-1, keepdims=True)
        )
        scores = jnp.where(p["seen"], product(query_d, key_d, 1, 1), 0.0)
        scores_grad = jnp.where(p["seen"], product(mixed_grad, value, 1, 1), 0.0)
        value_grad = product(scores, mixed_grad, 0, 0) + product(key_t, back, 1, 1)
        query_d_grad = product(scores_grad, key_d, 1, 0) + p["linked"] * product(mixed_grad, state, 1, 0)
        key_d_grad = product(scores_grad, query_d, 0, 0)
        key_t_grad = product(value, back, 1, 0)
        key_grad = key_d_grad * shrink + (p["tail"] * end * shrink) * key_t_grad
        change = query_d * query_d_grad - key_d * key_d_grad - key_t * key_t_grad
        through = product(upper, change, 1, 0) + through_ref[:, cols]
        key_total = key_grad - through / (1.0 - key)
        new_back = back * keep + product(mixed_grad, query_d * p["linked"], 0, 0)
        back_ref[h] = new_back
        through_ref[:, cols] = jnp.sum(new_back * state, axis=0, keepdims=True)
        sig = query_sig[:, cols]
        query_grad = query_d_grad * grow * (sig * (1.0 + query_pre[:, cols] * (1.0 - sig)))
        weighted_key = key_total * key
        forget_grad = -weighted_key * (1.0 - p["forget_sig"][:, cols])
        logit_ref[:, cols] += jnp.sum(weighted_key, axis=0, keepdims=True)
        for part, grad in enumerate((query_grad, forget_grad, value_grad, outgate_grad)):
            lo = part * width + h * HEAD_FEATURES
            grads_ref[:, lo : lo + HEAD_FEATURES] = grad.astype(bf16)


def recurrence_forward(segments, table, pre, bound):
    tokens, wide = pre.shape
    steps = table.shape[0]
    size, width = (tokens // steps, wide // 4)
    heads = width // HEAD_FEATURES
    return pl.pallas_call(
        forward_kernel,
        grid_spec=pltpu.PrefetchScalarGridSpec(
            num_scalar_prefetch=2,
            grid=(steps,),
            in_specs=[
                pl.BlockSpec((size, 1), lambda i, s, t: (i, 0)),
                pl.BlockSpec((1, size), lambda i, s, t: (0, i)),
                pl.BlockSpec((size, 3 * width), lambda i, s, t: (t[i], 0)),
                pl.BlockSpec((1, width), lambda i, s, t: (0, 0)),
            ],
            out_specs=[
                pl.BlockSpec((size, width), lambda i, s, t: (t[i], 0)),
                pl.BlockSpec((1, heads, HEAD_FEATURES, HEAD_FEATURES), lambda i, s, t: (i, 0, 0, 0)),
            ],
            scratch_shapes=[pltpu.VMEM((heads, HEAD_FEATURES, HEAD_FEATURES), f32)],
        ),
        out_shape=[
            jax.ShapeDtypeStruct((tokens, width), f32),
            jax.ShapeDtypeStruct((steps, heads, HEAD_FEATURES, HEAD_FEATURES), f32),
        ],
        compiler_params=vmem,
        cost_estimate=cost(320 * tokens * width * HEAD_FEATURES),
        name="recurrence_forward",
    )(segments, table, segments[:, None], segments[None, :], pre, bound)


def recurrence_backward(segments, table, pre, bound, mixed, gated_grad, states):
    tokens, wide = pre.shape
    steps = table.shape[0]
    size, width = (tokens // steps, wide // 4)
    heads = width // HEAD_FEATURES
    tokens_block = pl.BlockSpec((size, width), lambda i, s, t: (t[steps - 1 - i], 0))
    return pl.pallas_call(
        backward_kernel,
        grid_spec=pltpu.PrefetchScalarGridSpec(
            num_scalar_prefetch=2,
            grid=(steps,),
            in_specs=[
                pl.BlockSpec((size, 1), lambda i, s, t: (steps - 1 - i, 0)),
                pl.BlockSpec((1, size), lambda i, s, t: (0, steps - 1 - i)),
                pl.BlockSpec((size, 3 * width), lambda i, s, t: (t[steps - 1 - i], 0)),
                pl.BlockSpec((1, width), lambda i, s, t: (0, 0)),
                pl.BlockSpec((size, width), lambda i, s, t: (t[steps - 1 - i], 3)),
                tokens_block,
                tokens_block,
                pl.BlockSpec(
                    (1, heads, HEAD_FEATURES, HEAD_FEATURES),
                    lambda i, s, t: (steps - 1 - i, 0, 0, 0),
                ),
            ],
            out_specs=[
                pl.BlockSpec((size, 4 * width), lambda i, s, t: (t[steps - 1 - i], 0)),
                pl.BlockSpec((1, width), lambda i, s, t: (0, 0)),
            ],
            scratch_shapes=[
                pltpu.VMEM((heads, HEAD_FEATURES, HEAD_FEATURES), f32),
                pltpu.VMEM((1, width), f32),
            ],
        ),
        out_shape=[
            jax.ShapeDtypeStruct((tokens, 4 * width), bf16),
            jax.ShapeDtypeStruct((1, width), f32),
        ],
        compiler_params=vmem,
        cost_estimate=cost(620 * tokens * width * HEAD_FEATURES),
        name="recurrence_backward",
    )(segments, table, segments[:, None], segments[None, :], pre, bound, pre, mixed, gated_grad, states)


def matmul(left, right, left_dim=1, right_dim=0):
    return lax.dot_general(
        left, right, (((left_dim,), (right_dim,)), ((), ())), preferred_element_type=f32
    )


def rms_factor(value):
    return lax.rsqrt(jnp.mean(value * value, axis=-1, keepdims=True) + eps_model)


def rms_back(grad_unit, unit, factor):
    return factor * (grad_unit - unit * jnp.mean(grad_unit * unit, axis=-1, keepdims=True))


def product_kernel(left_dim, *refs):
    left_ref, right_ref, *added, out_ref = refs
    total = matmul(left_ref[...], right_ref[...], left_dim, 0)
    for ref in added:
        total += ref[...].astype(f32)
    out_ref[...] = total.astype(out_ref.dtype)


def dense(left, right, dtype, left_dim=1, added=None, parts=2):
    height, width = (left.shape[1 - left_dim], right.shape[1])
    size = width // parts if (width // parts) % LANES == 0 else width
    columns = block(height, size, at=lambda j: (0, j))
    extra = [] if added is None else [added]
    return pl.pallas_call(
        functools.partial(product_kernel, left_dim),
        grid=(width // size,),
        in_specs=[block(*left.shape), block(right.shape[0], size, at=lambda j: (0, j))]
        + [columns] * len(extra),
        out_specs=columns,
        out_shape=jax.ShapeDtypeStruct((height, width), dtype),
        compiler_params=vmem,
        cost_estimate=cost(3 * left.shape[0] * left.shape[1] * width),
        name="dense",
    )(left, right, *extra)


def store_halves(core, value, rows, row_block, mine_ref, theirs_ref):
    for z in range(value.shape[1] // (2 * row_block)):
        even = value[:, 2 * z * row_block : (2 * z + 1) * row_block]
        odd = value[:, (2 * z + 1) * row_block : (2 * z + 2) * row_block]
        to = slice(z * row_block, (z + 1) * row_block)

        @pl.when(core == 0)
        def _():
            mine_ref[rows, to] = even
            theirs_ref[rows, to] = odd

        @pl.when(core == 1)
        def _():
            mine_ref[rows, to] = odd
            theirs_ref[rows, to] = even


def assemble_kernel(places, half, row_block, normed, core_ref, *refs):
    outs = 3 if normed else 1
    pieces, gain_ref, all_ref = (refs[: len(refs) - 1 - outs], refs[-1 - outs], refs[-outs])
    for slot, (piece, row) in enumerate(places):
        rows = slice(slot * half, (slot + 1) * half)
        value = pieces[piece][row : row + half, :]
        if normed:
            wide = value.astype(f32)
            value = (wide * rms_factor(wide) * gain_ref[...]).astype(bf16)
        all_ref[rows, :] = value
        if normed:
            store_halves(core_ref[0], value, rows, row_block, *refs[-2:])


def assemble(gathered, core, row_block, gain=None):
    pieces, places = gathered
    half = pieces[0].shape[0] // 2 if len(pieces) > 1 else pieces[0].shape[0] // len(places)
    tokens, width = (half * len(places), pieces[0].shape[1])
    normed = gain is not None
    gain = gain if normed else jnp.zeros((1, width), f32)
    shapes = [(tokens, width), (tokens, width // 2), (tokens, width // 2)][: 3 if normed else 1]
    return pl.pallas_call(
        functools.partial(assemble_kernel, places, half, row_block, normed),
        grid_spec=pltpu.PrefetchScalarGridSpec(
            num_scalar_prefetch=1,
            grid=(1,),
            in_specs=[block(*piece.shape) for piece in pieces] + [block(1, width)],
            out_specs=[block(*shape) for shape in shapes],
        ),
        out_shape=[jax.ShapeDtypeStruct(shape, bf16) for shape in shapes],
        compiler_params=vmem,
        cost_estimate=cost(0, 12 * tokens * width),
        name="assemble",
    )(core, *pieces, gain)


def store_partials(value, layout, half, refs):
    for (first, last, dtype), ref in zip(layout, refs):
        ref[...] = value[first * half : last * half, :].astype(dtype)


def partial_specs(layout, half, width, columns):
    specs = [block((b - a) * half, columns, at=lambda j: (0, j)) for a, b, _ in layout]
    shapes = [jax.ShapeDtypeStruct(((b - a) * half, width), dtype) for a, b, dtype in layout]
    return specs, shapes


def partial_kernel(layout, half, cuts, left_ref, *refs):
    weights, outs = (refs[: len(cuts)], refs[len(cuts) :])
    total = None
    for (first, last), ref in zip(cuts, weights):
        term = matmul(left_ref[:, first:last], ref[...], 1, 1)
        total = term if total is None else total + term
    store_partials(total, layout, half, outs)


def ordered_kernel(half, places_ref, left_ref, weight_ref, out_ref):
    total = matmul(left_ref[...], weight_ref[...], 1, 1).astype(bf16)
    for slot in range(left_ref.shape[0] // half):
        to = pl.multiple_of(places_ref[slot] * half, half)
        out_ref[pl.ds(to, half), :] = total[slot * half : (slot + 1) * half, :]


def exchanged_product(left, weight, places, half, columns=256):
    tokens, depth = left.shape
    width = weight.shape[0]
    ranks = lax.axis_size("seq")
    partial = pl.pallas_call(
        functools.partial(ordered_kernel, half),
        grid_spec=pltpu.PrefetchScalarGridSpec(
            num_scalar_prefetch=1,
            grid=(width // columns,),
            in_specs=[block(tokens, depth), block(columns, depth, at=lambda j, p: (j, 0))],
            out_specs=block(tokens, columns, at=lambda j, p: (0, j)),
        ),
        out_shape=jax.ShapeDtypeStruct((tokens, width), bf16),
        compiler_params=vmem,
        cost_estimate=cost(3 * tokens * depth * width),
        name="exchanged_product",
    )(places, left, weight)
    return partial, swap_seq(partial.reshape(ranks, 2 * half, width))


def partial_product(left, weights, widths, half, columns=256):
    tokens, depth = left.shape
    width = weights[0].shape[0]
    layout = partial_layout(tokens)
    specs, shapes = partial_specs(layout, half, width, columns)
    cuts = [(sum(widths[:i]), sum(widths[: i + 1])) for i in range(len(widths))]
    return pl.pallas_call(
        functools.partial(partial_kernel, layout, half, cuts),
        grid=(width // columns,),
        in_specs=[block(tokens, depth)]
        + [block(columns, size, at=lambda j: (j, 0)) for size in widths],
        out_specs=specs,
        out_shape=shapes,
        compiler_params=vmem,
        cost_estimate=cost(3 * tokens * depth * width),
        name="partial_product",
    )(left, *weights)


def gate_out_kernel(layout, half, mixed_ref, outgate_pre_ref, out_ref, gated_ref, *outs):
    @pl.when(pl.program_id(0) == 0)
    def _():
        for h in range(mixed_ref.shape[1] // HEAD_FEATURES):
            cols = slice(h * HEAD_FEATURES, (h + 1) * HEAD_FEATURES)
            mixed, gate = mixed_ref[:, cols], outgate_pre_ref[:, cols]
            factor = lax.rsqrt(jnp.mean(mixed * mixed, axis=-1, keepdims=True) + eps_group)
            gated_ref[:, cols] = (mixed * factor * (gate * jax.nn.sigmoid(gate))).astype(bf16)

    store_partials(matmul(gated_ref[...], out_ref[...]), layout, half, outs)


def gate_out(mixed, pre, out_rows, half):
    tokens, my_width = mixed.shape
    width = out_rows.shape[1]
    layout = partial_layout(tokens)
    specs, shapes = partial_specs(layout, half, width, my_width)
    gated, *partials = pl.pallas_call(
        functools.partial(gate_out_kernel, layout, half),
        grid=(width // my_width,),
        in_specs=[
            block(tokens, my_width),
            block(tokens, my_width, at=lambda j: (0, 3)),
            block(my_width, my_width, at=lambda j: (0, j)),
        ],
        out_specs=[block(tokens, my_width)] + specs,
        out_shape=[jax.ShapeDtypeStruct((tokens, my_width), bf16)] + shapes,
        compiler_params=vmem,
        cost_estimate=cost(3 * tokens * my_width * width, 16 * tokens * width),
        name="gate_out",
    )(mixed, pre, out_rows)
    return gated, partials


def gated_grad_kernel(places, half, *refs):
    *pieces, out_ref, all_ref, grad_ref = refs
    for slot, (piece, row) in enumerate(places):
        all_ref[slot * half : (slot + 1) * half, :] = pieces[piece][row : row + half, :]
    grad_ref[...] = matmul(all_ref[...], out_ref[...], 1, 1)


def gated_gradient(gathered, out_rows, half):
    pieces, places = gathered
    my_width, width = out_rows.shape
    tokens = half * len(places)
    return pl.pallas_call(
        functools.partial(gated_grad_kernel, places, half),
        grid=(1,),
        in_specs=[block(*piece.shape) for piece in pieces] + [block(my_width, width)],
        out_specs=[block(tokens, width), block(tokens, my_width)],
        out_shape=[
            jax.ShapeDtypeStruct((tokens, width), bf16),
            jax.ShapeDtypeStruct((tokens, my_width), f32),
        ],
        compiler_params=vmem,
        cost_estimate=cost(3 * tokens * width * my_width),
        name="gated_gradient",
    )(*pieces, out_rows)


def ffn_forward_kernel(places, half, *refs):
    *pieces, weight_ref, both_ref, hidden_ref, all_ref = refs

    @pl.when(pl.program_id(0) == 0)
    def _():
        for slot, (piece, row) in enumerate(places):
            rows = slice(slot * half, (slot + 1) * half)
            all_ref[rows, :] = pieces[piece][row : row + half, :]

    both = matmul(all_ref[...], weight_ref[...])
    both_ref[...] = both
    gate, up = (both[:, :LANES], both[:, LANES:])
    hidden_ref[...] = (gate * jax.nn.sigmoid(gate) * up).astype(bf16)


def ffn_forward(gathered, ffn_cols, half):
    pieces, places = gathered
    width, total = ffn_cols.shape
    tokens = half * len(places)
    if (total // 2) % LANES:
        (rows,) = pieces
        both = matmul(rows, ffn_cols)
        gate, up = (both[:, : total // 2], both[:, total // 2 :])
        return both, (jax.nn.silu(gate) * up).astype(bf16), rows
    return pl.pallas_call(
        functools.partial(ffn_forward_kernel, places, half),
        grid=(total // (2 * LANES),),
        in_specs=[block(*piece.shape) for piece in pieces]
        + [block(width, 2 * LANES, at=lambda j: (0, j))],
        out_specs=[
            block(tokens, 2 * LANES, at=lambda j: (0, j)),
            block(tokens, LANES, at=lambda j: (0, j)),
            block(tokens, width),
        ],
        out_shape=[
            jax.ShapeDtypeStruct((tokens, total), f32),
            jax.ShapeDtypeStruct((tokens, total // 2), bf16),
            jax.ShapeDtypeStruct((tokens, width), bf16),
        ],
        compiler_params=vmem,
        cost_estimate=cost(3 * tokens * width * total),
        name="ffn_forward",
    )(*pieces, ffn_cols)


def ffn_backward_kernel(cotangent_ref, weight_ref, both_ref, grads_ref):
    hidden_grad = matmul(cotangent_ref[...], weight_ref[...])
    for j in range(hidden_grad.shape[1] // LANES):
        grad = hidden_grad[:, j * LANES : (j + 1) * LANES]
        gate = both_ref[:, 2 * j * LANES : (2 * j + 1) * LANES]
        up = both_ref[:, (2 * j + 1) * LANES : (2 * j + 2) * LANES]
        sig = jax.nn.sigmoid(gate)
        slope = sig * (1.0 + gate * (1.0 - sig))
        grads_ref[:, 2 * j * LANES : (2 * j + 1) * LANES] = (grad * up * slope).astype(bf16)
        grads_ref[:, (2 * j + 1) * LANES : (2 * j + 2) * LANES] = (grad * (gate * sig)).astype(bf16)


def ffn_backward(cotangent_all, down_cols, both):
    tokens, width = cotangent_all.shape
    mine = down_cols.shape[1]
    if mine % LANES:
        gate, up = (both[:, :mine], both[:, mine:])
        hidden_grad = matmul(cotangent_all, down_cols)
        sig = jax.nn.sigmoid(gate)
        gate_grad = hidden_grad * up * (sig * (1.0 + gate * (1.0 - sig)))
        up_grad = hidden_grad * (gate * sig)
        return jnp.concatenate((gate_grad, up_grad), axis=1).astype(bf16)
    size = 2 * LANES
    return pl.pallas_call(
        ffn_backward_kernel,
        grid=(pl.cdiv(mine, size),),
        in_specs=[
            block(tokens, width),
            block(width, size, at=lambda j: (0, j)),
            block(tokens, 2 * size, at=lambda j: (0, j)),
        ],
        out_specs=block(tokens, 2 * size, at=lambda j: (0, j)),
        out_shape=jax.ShapeDtypeStruct((tokens, 2 * mine), bf16),
        compiler_params=vmem,
        cost_estimate=cost(4 * tokens * width * mine),
        name="ffn_backward",
    )(cotangent_all, down_cols, both)


def add_up(parts):
    if len(parts) == 1 and len(parts[0].shape) == 3:
        return jnp.sum(parts[0][...].astype(f32), axis=0)
    if len(parts) == 1:
        return parts[0][...]
    rest, near, far, across, along = parts
    top = near[...].astype(f32) + across[...].astype(f32)
    low = far[...].astype(f32) + along[...].astype(f32)
    return rest[...] + jnp.where(pl.program_id(0) == 0, top, low)


def combine_kernel(post, count, given, *refs):
    parts, values, outs = (refs[:count], refs[count : count + given], refs[count + given :])
    results = post(add_up(parts), *(ref[...].astype(f32) for ref in values))
    for result, ref in zip(results, outs):
        ref[...] = result.astype(ref.dtype)


def combine(post, parts, values, dtypes, half):
    width = parts[0].shape[-1]
    mine = block(half, width, at=lambda h: (h, 0))
    fixed = block(half, width)
    part_specs = [mine] if len(parts) == 1 else [mine] + [fixed] * 4
    if parts[0].ndim == 3:
        part_specs = [block(parts[0].shape[0], half, width, at=lambda h: (0, h, 0))]
    value_specs = [block(1, width) if v.shape[0] == 1 else mine for v in values]
    return pl.pallas_call(
        functools.partial(combine_kernel, post, len(parts), len(values)),
        grid=(2,),
        in_specs=part_specs + value_specs,
        out_specs=[mine] * len(dtypes),
        out_shape=[jax.ShapeDtypeStruct((2 * half, width), dtype) for dtype in dtypes],
        compiler_params=vmem,
        cost_estimate=cost(0, 60 * half * width),
        name="combine",
    )(*parts, *values)


def residual(branch, inputs, gain):
    resid = inputs + branch
    return resid, resid * rms_factor(resid) * gain


def residual_back(mid_grad, cotangent, resid, gain):
    factor = rms_factor(resid)
    grad = cotangent + rms_back(mid_grad * gain, resid * factor, factor)
    return grad, grad


def input_back(in_grad, resid_grad, inputs, gain):
    factor = rms_factor(inputs)
    return (resid_grad + rms_back(in_grad * gain, inputs * factor, factor),)


def local(
    layer_input,
    segment_ids,
    mix_gain,
    bound_logit,
    query_weight,
    forget_weight,
    input_weight,
    output_gate_weight,
    output_weight,
    ffn_gain,
    ffn_gate_weight,
    ffn_up_weight,
    ffn_down_weight,
    output_cotangent,
):
    rows, length, width = layer_input.shape
    ranks, rank = (lax.axis_size("seq"), lax.axis_index("seq"))
    count = lax.axis_size("dp")
    my_width = width // ranks
    tokens = rows * length
    half = tokens // 2
    my_rows = mix_gain.shape[0]
    rank_rows = my_rows * ranks
    x_low = layer_input.reshape(tokens, width)
    cotangent_low = output_cotangent.reshape(tokens, width)
    core = (lax.axis_index("dp") & 1).reshape(1)

    mix_weights = [query_weight, forget_weight, input_weight, output_gate_weight]
    mix_pieces = swap_seq(column_pieces(mix_weights))
    mix_cols = gather_dp(mix_pieces.reshape(rank_rows, 4 * my_width))
    ffn_width = 2 * ffn_gate_weight.shape[1] // ranks
    ffn_pieces = column_pieces([after(ffn_gate_weight, mix_pieces), ffn_up_weight], True)
    down_pieces = column_pieces([ffn_down_weight])
    ffn_pieces = swap_seq(jnp.concatenate((ffn_pieces, down_pieces), axis=2))
    x_pieces, places = gather_seq(after(x_low, ffn_pieces))
    vectors = jnp.stack((mix_gain, bound_logit, ffn_gain), axis=1)
    vectors = gather_small(gather_small(vectors, "seq"), "dp").astype(f32)
    gain_in, logit, gain_mid = (vectors[:, 0], vectors[:, 1], vectors[:, 2])
    gain_in, gain_mid = (gain_in[None, :], gain_mid[None, :])
    segments = gather_small(segment_ids[0], "seq")
    table = slot_table()
    bound = jax.nn.sigmoid(-lax.dynamic_slice_in_dim(logit, rank * my_width, my_width))[None, :]
    normed_in, in_mine, in_theirs = assemble(
        (x_pieces, places), core, rank_rows, after(gain_in, segments, bound)
    )
    out_piece = lax.ppermute(output_weight, ("dp", "seq"), row_route())
    out_rows = gather_dp(after(out_piece, normed_in))
    ffn_cols = gather_dp(after(ffn_pieces[:, :, :ffn_width].reshape(rank_rows, ffn_width), out_piece))
    down_pieces = ffn_pieces[:, :, ffn_width:].reshape(rank_rows, ffn_width // 2)

    pre = dense(normed_in, mix_cols, f32, parts=4)
    down_cols = gather_dp(after(down_pieces, pre))
    mixed, states = recurrence_forward(segments, table, pre, bound)
    gated, partials = gate_out(mixed, pre, out_rows, half)
    cotangent = gather_seq(after(cotangent_low, normed_in))
    branch_parts = scatter_seq(partials, half)
    (cotangent_all,) = assemble(cotangent, core, rank_rows)
    resid, normed_low = combine(
        residual, branch_parts, (after(x_low, cotangent_all), gain_mid), (f32, bf16), half
    )
    normed_mid = gather_seq(normed_low)

    both, hidden, mid_all = ffn_forward(normed_mid, ffn_cols, half)

    down_sum = dense(cotangent_all, hidden, bf16, 0)
    down_mine = lax.psum_scatter(down_sum, "dp", scatter_dimension=0, tiled=True)
    cotangent_all = after(cotangent_all, down_sum)
    ffn_right = ffn_backward(cotangent_all, down_cols, both)
    mid_partials = partial_product(ffn_right, [ffn_cols], [ffn_cols.shape[1]], half)
    ffn_sum = dense(mid_all, after(ffn_right, mid_partials[0]), bf16, 0)
    mid_parts = scatter_seq(mid_partials, half, beside=(ffn_sum, down_mine))
    ffn_mine = lax.psum_scatter(after(ffn_sum, *mid_parts[:3]), "dp", scatter_dimension=0, tiled=True)

    resid_grad, branch_own = combine(
        residual_back, mid_parts, (cotangent_low, resid, gain_mid), (f32, bf16), half
    )
    branch, places = gather_seq(branch_own)
    row_place = row_places()
    out_partial, out_parts = exchanged_product(after(hidden, branch_own), down_cols, row_place, half)
    branch = (after(branch[0], out_partial),) + branch[1:]
    branch_low, gated_grad = gated_gradient((branch, places), out_rows, half)
    mix_right, logit_part = recurrence_backward(segments, table, pre, bound, mixed, gated_grad, states)
    (ffn_down_weight_grad,), _ = return_columns(after(down_mine, branch_low), [ffn_down_weight])
    mix_theirs = dense(in_theirs, after(mix_right, ffn_down_weight_grad, out_parts), bf16, 0)
    out_sum = dense(gated, after(branch_low, mix_theirs), bf16, 0)
    mix_theirs = flip(mix_theirs, "dp", 1)
    mix_sum = dense(in_mine, after(mix_right, out_sum), bf16, 0, mix_theirs)
    mix_mine = scatter_dp(mix_sum)
    out_mine = lax.psum_scatter(after(out_sum, mix_sum), "dp", scatter_dimension=0, tiled=True)
    (ffn_gate_weight_grad, ffn_up_weight_grad), ffn_sums = return_columns(
        after(ffn_mine, mix_sum), [ffn_gate_weight, ffn_up_weight], True
    )
    (block_output,) = combine(
        lambda total, resid: (resid + total,), (out_parts,), (after(resid, mix_sum),), (bf16,), half
    )
    _, in_parts = exchanged_product(after(mix_right, mix_sum, ffn_sums), mix_cols, row_place, half)

    output_weight_grad = lax.ppermute(
        out_mine, ("dp", "seq"), [(b, a) for a, b in row_route()]
    ).astype(f32)
    logit_sum = gather_small(sum_small(-logit_part[0] * (1.0 - bound[0]), "dp"), "seq")
    at = (lax.axis_index("dp") * ranks + rank) * my_rows
    bound_logit_grad = lax.dynamic_slice_in_dim(logit_sum, at, my_rows)
    (input_grad,) = combine(
        input_back, (in_parts,), (after(resid_grad, bound_logit_grad), x_low, gain_in), (f32,), half
    )
    mix_mine = after(mix_mine, input_grad, block_output)
    mix_grads, mix_sums = return_columns(mix_mine, mix_weights)
    query_weight_grad, forget_weight_grad, input_weight_grad, output_gate_weight_grad = mix_grads
    mix_gain_grad = mix_sums / mix_gain.astype(f32)
    ffn_gain_grad = ffn_sums / ffn_gain.astype(f32)
    return (
        block_output.reshape(rows, length, width),
        input_grad.reshape(rows, length, width),
        mix_gain_grad,
        bound_logit_grad,
        query_weight_grad,
        forget_weight_grad,
        input_weight_grad,
        output_gate_weight_grad,
        output_weight_grad,
        ffn_gain_grad,
        ffn_gate_weight_grad,
        ffn_up_weight_grad,
        ffn_down_weight_grad,
    )


def solution(mesh):
    by_token = P("dp", "seq", None)
    vector = P(("dp", "seq"))
    matrix = P(("dp", "seq"), None)
    return jax.shard_map(
        local,
        mesh=mesh,
        in_specs=(by_token, P("dp", "seq"), vector, vector)
        + (matrix,) * 5
        + (vector,)
        + (matrix,) * 3
        + (by_token,),
        out_specs=(by_token, by_token, vector, vector) + (matrix,) * 5 + (vector,) + (matrix,) * 3,
        check_vma=False,
    )
```

time: 783 us -> 692 us (0.88)
  Pallas kernels: 54.3 us -> 243 us
  matrix products: 148 us -> 0 us
  blocking collectives: 85.4 us -> 27 us
  waiting for transfers between devices: 298 us -> 263 us
  other arithmetic: 34.8 us -> 9 us
  local copies, waits for them, and re-layouts: 60.1 us -> 39.7 us
    pallas_call x0 -> x25, Pallas kernels: none -> 186 us  [the longest x6 62.3 us: dense(): pl.pallas_call(functools.partial(product_kernel, left_dim), grid=(width /...]
    dot_general x12 -> x0, matrix products: 148 us -> none  [matmul(): lax.dot_general(left, right, (((left_dim,), (right_dim,)), ((), ())), pre...]
    all_to_all x3 -> x2, blocking collectives: 85.4 us -> 27 us  [swap_seq(): lax.all_to_all(pieces, 'seq', split_axis=0, concat_axis=0, tiled=True)]
    reduce_scatter x4, waiting for transfers between devices: 54.9 us -> 16.7 us  [the longest x1 8.72 us: local(): lax.psum_scatter(down_sum, 'dp', scatter_dimension=0, tiled=True)]
    all_gather x4, waiting for transfers between devices: 0.03 us -> 26.9 us  [gather_dp(): return lax.all_gather(block, 'dp', axis=0, tiled=True)]
    dynamic_update_slice x18 -> x0, local copies, waits for them, and re-layouts: 18.7 us -> none  [the longest x4 5.82 us: gather_seq(): whole = lax.dynamic_update_slice_in_dim(whole, far, (mine ^ 2) * tokens, 0)]
    reduce_sum x11 -> x0, other arithmetic: 18.4 us -> none  [the longest x4 12 us: scatter_seq(): return jnp.sum(pieces.astype(f32), axis=0)]
    all_to_all x7 -> x5, waiting for transfers between devices: 39.8 us -> 21.5 us  [swap_seq(): lax.all_to_all(pieces, 'seq', split_axis=0, concat_axis=0, tiled=True)]
  transfers between devices with their start and end apart: 45 -> 52, of which waited for: 22 -> 33; matrix products, arithmetic and copies ran while one was open for 24% -> 2% of each run, Pallas kernels for 7% -> 35%
where the time goes in v2:
time: 692 us; the launch traced here: 679 us
  waiting for transfers between devices  263 us (38%)
  Pallas kernels  243 us (35%)
  starting transfers between devices  82.3 us (12%)
  local copies, waits for them, and re-layouts  39.7 us (6%)
  blocking collectives  27 us (4%)
  between operations  15 us (2%)
  other arithmetic  9 us (1%)
    ppermute x37, waiting for transfers between devices, flip(): lax.ppermute(block, axis, [(i, i ^ bits) for i in range(lax.axis_size(axi...  186 us
    pallas_call x6, Pallas kernels, dense(): pl.pallas_call(functools.partial(product_kernel, left_dim), grid=(width /...  62.3 us
    ppermute x37, starting transfers between devices, flip(): lax.ppermute(block, axis, [(i, i ^ bits) for i in range(lax.axis_size(axi...  47.6 us
    pallas_call x1, Pallas kernels, recurrence_backward(): pl.pallas_call(backward_kernel, grid_spec=pltpu.PrefetchScalarGridSpec(nu...  37.4 us
    unnamed x116, local copies, waits for them, and re-layouts  34.6 us
    all_to_all x2, blocking collectives, swap_seq(): lax.all_to_all(pieces, 'seq', split_axis=0, concat_axis=0, tiled=True)  27 us
    all_gather x4, waiting for transfers between devices, gather_dp(): return lax.all_gather(block, 'dp', axis=0, tiled=True)  26.9 us
    pallas_call x2, Pallas kernels, exchanged_product(): pl.pallas_call(functools.partial(ordered_kernel, half), grid_spec=pltpu.P...  26.1 us
  transfers between devices with their start and end apart: 52, of which 33 were waited for; matrix products, arithmetic and copies ran while one was open for 2% of the time, Pallas kernels for 35%

profile of v2, /device:TPU:1, one launch (start us, length us, event | category | flops | bytes accessed | tf_op | source)
XLA Modules:
  0.0 679.3 jit_solution(10816027414148884940)
XLA Ops:
  11.5 17.0 %all_to_all.35 = bf16[4,64,2048]{2,1,0:T(8,128)(2,1)} all-to-all(bf16[4,64,2048]{2,1,0:T(8,128)(2,1)S(1)} %column_pieces.3), channel_id=1, replica_groups=mesh['dp'=8,'seq'=4] {'seq'}, dimensions={0} | all-to-all | bytes 2097152 | tf_op jit(solution)/shard_map/all_to_all | solution.py:115
  43.0 18.2 %collective-permute-done.6 = bf16[64,3]{0,1:T(4,128)(2,1)S(1)} collective-permute-done((bf16[64,3]{0,1:T(4,128)(2,1)S(1)}, bf16[64,3]{0,1:T(4,128)(2,1)S(1)}, u32[]{:S(2)}, u32[]{:S(2)}) %collective-permute-start.6) | collective-permute-done | bytes 416 | tf_op jit(solution)/shard_map/ppermute | solution.py:27
  73.4 19.8 %collective-permute-done.1 = s32[512]{0:T(512)S(1)} collective-permute-done((s32[512]{0:T(512)S(1)}, s32[512]{0:T(512)S(1)}, u32[]{:S(2)}, u32[]{:S(2)}) %collective-permute-start.1) | collective-permute-done | bytes 2080 | tf_op jit(solution)/shard_map/ppermute | solution.py:27
  99.9 10.3 %collective-permute-done.5.refs_4_ = bf16[128,2048]{1,0:T(8,128)(2,1)S(1)} collective-permute-done((bf16[128,2048]{1,0:T(8,128)(2,1)S(1)}, bf16[128,2048]{1,0:T(8,128)(2,1)S(1)}, u32[]{:S(2)}, u32[]{:S(2)}) %collective-permute-start.5) | collective-permute-done | bytes 524320 | tf_op jit(solution)/shard_map/ppermute | solution.py:27
  121.5 12.5 %dense.6.pre_ref.outgate_pre_ref = f32[1024,2048]{1,0:T(8,128)} custom-call(bf16[1024,2048]{1,0:T(8,128)(2,1)S(1)} %copy-done.30, bf16[2048,2048]{1,0:T(8,128)(2,1)} %all-gather.5.cloned.1.call-done.refs_1_.weight_ref), custom_call_target="tpu_custom_call" | custom-call | flops 12884901888 | tf_op jit(solution)/shard_map/dense/pallas_call | solution.py:446
  138.2 19.5 %recurrence_forward.1 = (f32[1024,512]{1,0:T(8,128)S(1)}, f32[8,4,128,128]{3,2,1,0:T(8,128)S(1)}) custom-call(s32[1024]{0:T(1024)S(1)} %pad_add_fusion.seg_ref, s32[8]{0:T(128)S(1)} %reshape.114.slot_ref, s32[1024,1]{1,0:T(8,128)S(1)} %copy-done.24, s32[1,1024]{1,0:T(1,128)S(1)} %bitcast.39, f32[1024,2048]{1,0:T(8,128)} %dense.6.pre_ref.outgate_pre_ref, ...), custom_call_target="tpu_custom_call" | custom-call | flops 21474836480 | tf_op jit(solution)/shard_map/recurrence_forward/pallas_call | solution.py:349
  174.0 18.3 %collective-permute-done.12.refs_1_ = bf16[256,2048]{1,0:T(8,128)(2,1)S(1)} collective-permute-done((bf16[256,2048]{1,0:T(8,128)(2,1)S(1)}, bf16[256,2048]{1,0:T(8,128)(2,1)S(1)}, u32[]{:S(2)}, u32[]{:S(2)}) %collective-permute-start.12) | collective-permute-done | bytes 1048608 | tf_op jit(solution)/shard_map/ppermute | solution.py:27
  220.9 20.1 %collective-permute-done.21.refs_2_ = bf16[256,2048]{1,0:T(8,128)(2,1)S(1)} collective-permute-done((bf16[256,2048]{1,0:T(8,128)(2,1)S(1)}, bf16[256,2048]{1,0:T(8,128)(2,1)S(1)}, u32[]{:S(2)}, u32[]{:S(2)}) %collective-permute-start.21) | collective-permute-done | bytes 1048608 | tf_op jit(solution)/shard_map/ppermute | solution.py:27
  243.7 11.1 %collective-permute-done.23.refs_4_ = bf16[128,2048]{1,0:T(8,128)(2,1)S(1)} collective-permute-done((bf16[128,2048]{1,0:T(8,128)(2,1)S(1)}, bf16[128,2048]{1,0:T(8,128)(2,1)S(1)}, u32[]{:S(2)}, u32[]{:S(2)}) %collective-permute-start.23) | collective-permute-done | bytes 524320 | tf_op jit(solution)/shard_map/ppermute | solution.py:27
  264.9 20.0 %ffn_forward.1 = (f32[1024,2816]{1,0:T(8,128)}, bf16[1024,1408]{1,0:T(8,128)(2,1)}, bf16[1024,2048]{1,0:T(8,128)(2,1)}) custom-call(bf16[256,2048]{1,0:T(8,128)(2,1)S(1)} %copy-done.36, bf16[256,2048]{1,0:T(8,128)(2,1)S(1)} %copy-done.27, bf16[256,2048]{1,0:T(8,128)(2,1)S(1)} %collective-permute-done.21.refs_2_, bf16[128,2048]{1,0:T(8,128)(2,1)S(1)} %copy-done.40, ...), custom_call_target="tpu_custom_call" | custom-call | flops 17716740096 | tf_op jit(solution)/shard_map/ffn_forward/pallas_call | solution.py:662
  286.7 11.4 %dense.7 = bf16[2048,1408]{1,0:T(8,128)(2,1)} custom-call(bf16[1024,2048]{1,0:T(8,128)(2,1)} %assemble.3.refs_0_.cotangent_ref, bf16[1024,1408]{1,0:T(8,128)(2,1)S(1)} %copy-done.42), custom_call_target="tpu_custom_call" | custom-call | flops 8858370048 | tf_op jit(solution)/shard_map/dense/pallas_call | solution.py:446
  298.2 22.4 %all-gather.11.cloned.1.call-done.weight_ref = bf16[2048,1408]{1,0:T(8,128)(2,1)} async-done(((bf16[256,1408]{1,0:T(8,128)(2,1)}), bf16[2048,1408]{1,0:T(8,128)(2,1)}) %all-gather.11.cloned.1.call-update) | async-done | bytes 5767184 | tf_op jit(solution)/shard_map/all_gather | solution.py:119
  322.8 14.1 %ffn_backward.1.left_ref.refs_1_ = bf16[1024,2816]{1,0:T(8,128)(2,1)} custom-call(bf16[1024,2048]{1,0:T(8,128)(2,1)S(1)} %copy-done.3, bf16[2048,1408]{1,0:T(8,128)(2,1)} %all-gather.11.cloned.1.call-done.weight_ref, f32[1024,2816]{1,0:T(8,128)} %get-tuple-element.85.both_ref), custom_call_target="tpu_custom_call" | custom-call | flops 11811160064 | tf_op jit(solution)/shard_map/ffn_backward/pallas_call | solution.py:706
  336.9 17.8 %partial_product.1 = (bf16[256,2048]{1,0:T(8,128)(2,1)}, bf16[256,2048]{1,0:T(8,128)(2,1)}, f32[512,2048]{1,0:T(8,128)}) custom-call(bf16[1024,2816]{1,0:T(8,128)(2,1)} %ffn_backward.1.left_ref.refs_1_, bf16[2048,2816]{1,0:T(8,128)(2,1)} %all-gather.9.cloned.1.call-done.refs_5_.refs_0_), custom_call_target="tpu_custom_call" | custom-call | flops 17716740096 | tf_op jit(solution)/shard_map/partial_product/pallas_call | solution.py:565
  357.2 17.9 %dense.8 = bf16[2048,2816]{1,0:T(8,128)(2,1)} custom-call(bf16[1024,2048]{1,0:T(8,128)(2,1)S(1)} %copy-done.44, bf16[1024,2816]{1,0:T(8,128)(2,1)} %ffn_backward.1.left_ref.refs_1_), custom_call_target="tpu_custom_call" | custom-call | flops 17716740096 | tf_op jit(solution)/shard_map/dense/pallas_call | solution.py:446
  375.1 8.7 %reduce-scatter.5.cloned.1.call-done = bf16[256,1408]{1,0:T(8,128)(2,1)} async-done(((bf16[2048,1408]{1,0:T(8,128)(2,1)}), bf16[256,1408]{1,0:T(8,128)(2,1)}) %reduce-scatter.5.cloned.1.call-update) | async-done | bytes 720912 | tf_op jit(solution)/shard_map/reduce_scatter | solution.py:842
  403.6 19.4 %collective-permute-done.29.refs_2_ = bf16[256,2048]{1,0:T(8,128)(2,1)S(1)} collective-permute-done((bf16[256,2048]{1,0:T(8,128)(2,1)S(1)}, bf16[256,2048]{1,0:T(8,128)(2,1)S(1)}, u32[]{:S(2)}, u32[]{:S(2)}) %collective-permute-start.29) | collective-permute-done | bytes 1048608 | tf_op jit(solution)/shard_map/ppermute | solution.py:27
  424.5 12.1 %exchanged_product.2 = bf16[1024,2048]{1,0:T(8,128)(2,1)} custom-call(s32[8]{0:T(128)S(1)} %multiply_add_fusion.places_ref, bf16[1024,1408]{1,0:T(8,128)(2,1)S(1)} %copy-done.43, bf16[2048,1408]{1,0:T(8,128)(2,1)} %all-gather.11.cloned.1.call-done.weight_ref), custom_call_target="tpu_custom_call" | custom-call | flops 8858370048 | tf_op jit(solution)/shard_map/exchanged_product/pallas_call | solution.py:543
  443.2 10.0 %all_to_all.36.refs_0_ = bf16[4,64,1408]{2,1,0:T(8,128)(2,1)S(1)} all-to-all(bf16[4,64,1408]{2,1,0:T(8,128)(2,1)S(1)} %bitcast.51), channel_id=1, replica_groups=mesh['dp'=8,'seq'=4] {'seq'}, dimensions={0} | all-to-all | bytes 1441792 | tf_op jit(solution)/shard_map/all_to_all | solution.py:115
  461.5 37.4 %recurrence_backward.1 = (bf16[1024,2048]{1,0:T(8,128)(2,1)}, f32[1,512]{1,0:T(1,128)S(1)}) custom-call(s32[1024]{0:T(1024)S(1)} %pad_add_fusion.seg_ref, s32[8]{0:T(128)S(1)} %reshape.114.slot_ref, s32[1024,1]{1,0:T(8,128)S(1)} %copy-done.25, s32[1,1024]{1,0:T(1,128)S(1)} %bitcast.40, f32[1024,2048]{1,0:T(8,128)} %dense.6.pre_ref.outgate_pre_ref, ...), custom_call_target="tpu_custom_call" | custom-call | flops 41607495680 | tf_op jit(solution)/shard_map/recurrence_backward/pallas_call | solution.py:382
  539.1 16.7 %all-to-all-done.4.refs_0_ = bf16[4,64,2816]{2,1,0:T(8,128)(2,1)S(1)} async-done(((bf16[4,64,2816]{2,1,0:T(8,128)(2,1)}), bf16[4,64,2816]{2,1,0:T(8,128)(2,1)S(1)}, u32[]{:S(2)}, u32[]{:S(2)}) %all-to-all-start.4) | async-done | bytes 1441824 | tf_op jit(solution)/shard_map/all_to_all | solution.py:115
  559.6 14.0 %exchanged_product.3 = bf16[1024,2048]{1,0:T(8,128)(2,1)S(1)} custom-call(s32[8]{0:T(128)S(1)} %multiply_add_fusion.places_ref, bf16[1024,2048]{1,0:T(8,128)(2,1)} %get-tuple-element.112.refs_1_.left_ref, bf16[2048,2048]{1,0:T(8,128)(2,1)} %all-gather.5.cloned.1.call-done.refs_1_.weight_ref), custom_call_target="tpu_custom_call" | custom-call | flops 12884901888 | tf_op jit(solution)/shard_map/exchanged_product/pallas_call | solution.py:543
  598.4 28.4 %collective-permute-done.36 = f32[512]{0:T(512)S(1)} collective-permute-done((f32[512]{0:T(512)S(1)}, f32[512]{0:T(512)S(1)}, u32[]{:S(2)}, u32[]{:S(2)}) %collective-permute-start.36) | collective-permute-done | bytes 2080 | tf_op jit(solution)/shard_map/ppermute | solution.py:27
  657.5 10.8 %collective-permute-done.38 = bf16[64,2048]{1,0:T(8,128)(2,1)S(1)} collective-permute-done((bf16[64,2048]{1,0:T(8,128)(2,1)}, bf16[64,2048]{1,0:T(8,128)(2,1)S(1)}, u32[]{:S(2)}, u32[]{:S(2)}) %collective-permute-start.38) | collective-permute-done | bytes 262176 | tf_op jit(solution)/shard_map/ppermute | solution.py:874
  (283 shorter events, 256.5 us)
Async XLA Ops:
  7.2 112.1 %all-gather.5.cloned.1.call-start = ((), (), s32[]{:S(2)}) async-start(), calls=%async_computation.11 | async-start | bytes 9437184 | tf_op jit(solution)/shard_map/all_gather | solution.py:119
  30.8 37.5 %all-to-all-start.1 = ((bf16[4,64,4224]{2,1,0:T(8,128)(2,1)}), bf16[4,64,4224]{2,1,0:T(8,128)(2,1)S(1)}, u32[]{:S(2)}, u32[]{:S(2)}) async-start(bf16[4,64,4224]{2,1,0:T(8,128)(2,1)} %pad_maximum_fusion), calls=%async_computation.1 | async-start | bytes 4325376 | tf_op jit(solution)/shard_map/all_to_all | solution.py:115
  34.5 126.0 %all-gather.7.cloned.1.call-start = ((), (), s32[]{:S(2)}) async-start(), calls=%async_computation.12 | async-start | bytes 2359296 | tf_op jit(solution)/shard_map/all_gather | solution.py:119
  34.6 26.7 %collective-permute-start.6 = (bf16[64,3]{0,1:T(4,128)(2,1)S(1)}, bf16[64,3]{0,1:T(4,128)(2,1)S(1)}, u32[]{:S(2)}, u32[]{:S(2)}) collective-permute-start(bf16[64,3]{0,1:T(4,128)(2,1)S(1)} %pad_maximum_fusion.6), channel_id=1, source_target_pairs={{0,1},{1,0},{2,3},{3,2},{4,5},{5,4},{6,7},{7,6},{8,9},{9,8},{10,11... | collective-permute-start | bytes 1160 | tf_op jit(solution)/shard_map/ppermute | solution.py:27
  36.0 25.3 %collective-permute-start = (s32[256]{0:T(256)S(1)}, s32[256]{0:T(256)S(1)}, u32[]{:S(2)}, u32[]{:S(2)}) collective-permute-start(s32[256]{0:T(256)S(1)} %bitcast.60), channel_id=1, source_target_pairs={{0,1},{1,0},{2,3},{3,2},{4,5},{5,4},{6,7},{7,6},{8,9},{9,8},{10,11... | collective-permute-start | bytes 3080 | tf_op jit(solution)/shard_map/ppermute | solution.py:27
  36.1 79.8 %collective-permute-start.11 = (bf16[64,2048]{1,0:T(8,128)(2,1)}, bf16[64,2048]{1,0:T(8,128)(2,1)S(1)}, u32[]{:S(2)}, u32[]{:S(2)}) collective-permute-start(bf16[64,2048]{1,0:T(8,128)(2,1)} %param.25), channel_id=1, source_target_pairs={{0,0},{1,4},{2,8},{3,12},{4,16},{5,20},{6,24},{7,28},{8,1},{9,5},{... | collective-permute-start | bytes 786440 | tf_op jit(solution)/shard_map/ppermute | solution.py:822
  68.4 29.2 %collective-permute-start.3 = (bf16[256,2048]{1,0:T(8,128)(2,1)S(1)}, bf16[256,2048]{1,0:T(8,128)(2,1)S(1)}, u32[]{:S(2)}, u32[]{:S(2)}) collective-permute-start(bf16[256,2048]{1,0:T(8,128)(2,1)S(1)} %bitcast.28), channel_id=1, source_target_pairs={{0,2},{1,3},{2,0},{3,1},{4,6},{5,7},{6,4},{7,5},{8,10},{9,11},{10,... | collective-permute-start | bytes 3145736 | tf_op jit(solution)/shard_map/ppermute | solution.py:27
  68.4 29.3 %collective-permute-start.2 = (bf16[256,2048]{1,0:T(8,128)(2,1)S(1)}, bf16[256,2048]{1,0:T(8,128)(2,1)S(1)}, u32[]{:S(2)}, u32[]{:S(2)}) collective-permute-start(bf16[256,2048]{1,0:T(8,128)(2,1)S(1)} %bitcast.29), channel_id=1, source_target_pairs={{0,1},{1,0},{2,3},{3,2},{4,5},{5,4},{6,7},{7,6},{8,9},{9,8},{10,11... | collective-permute-start | bytes 3145736 | tf_op jit(solution)/shard_map/ppermute | solution.py:27
  116.7 143.7 %all-gather.9.cloned.1.call-start = ((), (), s32[]{:S(2)}) async-start(), calls=%async_computation.13 | async-start | bytes 12976128 | tf_op jit(solution)/shard_map/all_gather | solution.py:119
  117.9 202.7 %all-gather.11.cloned.1.call-start = ((), (), s32[]{:S(2)}) async-start(), calls=%async_computation.14 | async-start | bytes 6488064 | tf_op jit(solution)/shard_map/all_gather | solution.py:119
  134.0 249.8 %reduce-scatter.5.cloned.1.call-start = ((), (), s32[]{:S(2)}) async-start(), calls=%async_computation.15 | async-start | bytes 6488064 | tf_op jit(solution)/shard_map/reduce_scatter | solution.py:842
  135.9 35.9 %collective-permute-start.17 = (bf16[256,2048]{1,0:T(8,128)(2,1)S(1)}, bf16[256,2048]{1,0:T(8,128)(2,1)S(1)}, u32[]{:S(2)}, u32[]{:S(2)}) collective-permute-start(bf16[256,2048]{1,0:T(8,128)(2,1)S(1)} %bitcast.33), channel_id=1, source_target_pairs={{0,2},{1,3},{2,0},{3,1},{4,6},{5,7},{6,4},{7,5},{8,10},{9,11},{10,... | collective-permute-start | bytes 3145736 | tf_op jit(solution)/shard_map/ppermute | solution.py:27
  136.0 36.9 %collective-permute-start.16 = (bf16[256,2048]{1,0:T(8,128)(2,1)S(1)}, bf16[256,2048]{1,0:T(8,128)(2,1)}, u32[]{:S(2)}, u32[]{:S(2)}) collective-permute-start(bf16[256,2048]{1,0:T(8,128)(2,1)S(1)} %bitcast.34), channel_id=1, source_target_pairs={{0,1},{1,0},{2,3},{3,2},{4,5},{5,4},{6,7},{7,6},{8,9},{9,8},{10,11... | collective-permute-start | bytes 3145736 | tf_op jit(solution)/shard_map/ppermute | solution.py:27
  171.9 31.6 %collective-permute-start.19 = (bf16[128,2048]{1,0:T(8,128)(2,1)S(1)}, bf16[128,2048]{1,0:T(8,128)(2,1)S(1)}, u32[]{:S(2)}, u32[]{:S(2)}) collective-permute-start(bf16[128,2048]{1,0:T(8,128)(2,1)S(1)} %slice.93), channel_id=1, source_target_pairs={{0,1},{1,0},{2,3},{3,2},{4,5},{5,4},{6,7},{7,6},{8,9},{9,8},{10,11... | collective-permute-start | bytes 1572872 | tf_op jit(solution)/shard_map/ppermute | solution.py:27
  173.9 30.2 %collective-permute-start.18 = (bf16[128,2048]{1,0:T(8,128)(2,1)S(1)}, bf16[128,2048]{1,0:T(8,128)(2,1)S(1)}, u32[]{:S(2)}, u32[]{:S(2)}) collective-permute-start(bf16[128,2048]{1,0:T(8,128)(2,1)S(1)} %slice.92), channel_id=1, source_target_pairs={{0,2},{1,3},{2,0},{3,1},{4,6},{5,7},{6,4},{7,5},{8,10},{9,11},{10,... | collective-permute-start | bytes 1572872 | tf_op jit(solution)/shard_map/ppermute | solution.py:27
  298.1 236.3 %reduce-scatter.7.cloned.1.call-start = ((), (), s32[]{:S(2)}) async-start(), calls=%async_computation.16 | async-start | bytes 12976128 | tf_op jit(solution)/shard_map/reduce_scatter | solution.py:848
  354.7 29.1 %collective-permute-start.24 = (bf16[256,2048]{1,0:T(8,128)(2,1)}, bf16[256,2048]{1,0:T(8,128)(2,1)S(1)}, u32[]{:S(2)}, u32[]{:S(2)}) collective-permute-start(bf16[256,2048]{1,0:T(8,128)(2,1)} %get-tuple-element.88), channel_id=1, source_target_pairs={{0,1},{1,0},{2,3},{3,2},{4,5},{5,4},{6,7},{7,6},{8,9},{9,8},{10,11... | collective-permute-start | bytes 3145736 | tf_op jit(solution)/shard_map/ppermute | solution.py:27
  356.0 27.8 %collective-permute-start.25 = (bf16[256,2048]{1,0:T(8,128)(2,1)}, bf16[256,2048]{1,0:T(8,128)(2,1)}, u32[]{:S(2)}, u32[]{:S(2)}) collective-permute-start(bf16[256,2048]{1,0:T(8,128)(2,1)} %get-tuple-element.91), channel_id=1, source_target_pairs={{0,2},{1,3},{2,0},{3,1},{4,6},{5,7},{6,4},{7,5},{8,10},{9,11},{10,... | collective-permute-start | bytes 3145736 | tf_op jit(solution)/shard_map/ppermute | solution.py:27
  453.2 52.3 %all-to-all-start.2 = ((bf16[4,256,2048]{2,1,0:T(8,128)(2,1)}), bf16[4,256,2048]{2,1,0:T(8,128)(2,1)}, u32[]{:S(2)}, u32[]{:S(2)}) async-start(bf16[4,256,2048]{2,1,0:T(8,128)(2,1)} %bitcast.44), calls=%async_computation.3 | async-start | bytes 8388608 | tf_op jit(solution)/shard_map/all_to_all | solution.py:115
  458.2 181.5 %reduce-scatter.9.cloned.1.call-start = ((), (), s32[]{:S(2)}) async-start(), calls=%async_computation.17 | async-start | bytes 5242880 | tf_op jit(solution)/shard_map/reduce_scatter | solution.py:124
  538.4 112.9 %reduce-scatter.11.cloned.1.call-start = ((), (), s32[]{:S(2)}) async-start(), calls=%async_computation.18 | async-start | bytes 2359296 | tf_op jit(solution)/shard_map/reduce_scatter | solution.py:865
  575.6 58.0 %all-to-all-start.5 = ((bf16[4,256,2048]{2,1,0:T(8,128)(2,1)}), bf16[4,256,2048]{2,1,0:T(8,128)(2,1)}, u32[]{:S(2)}, u32[]{:S(2)}) async-start(bf16[4,256,2048]{2,1,0:T(8,128)(2,1)} %bitcast.37), calls=%async_computation.7 | async-start | bytes 8388608 | tf_op jit(solution)/shard_map/all_to_all | solution.py:115
  597.3 29.5 %collective-permute-start.36 = (f32[512]{0:T(512)S(1)}, f32[512]{0:T(512)S(1)}, u32[]{:S(2)}, u32[]{:S(2)}) collective-permute-start(f32[512]{0:T(512)S(1)} %add.73), channel_id=1, source_target_pairs={{0,1},{1,0},{2,3},{3,2},{4,5},{5,4},{6,7},{7,6},{8,9},{9,8},{10,11... | collective-permute-start | bytes 6152 | tf_op jit(solution)/shard_map/ppermute | solution.py:27
  639.6 30.0 %all-to-all-start.6 = ((bf16[4,64,2048]{2,1,0:T(8,128)(2,1)}), bf16[4,64,2048]{2,1,0:T(8,128)(2,1)S(1)}, u32[]{:S(2)}, u32[]{:S(2)}) async-start(bf16[4,64,2048]{2,1,0:T(8,128)(2,1)} %bitcast.50), calls=%async_computation.9 | async-start | bytes 2097152 | tf_op jit(solution)/shard_map/all_to_all | solution.py:115
  (86 other events, 1127.8 us)
Sparse Core Ops, SparseCore 0:
  28.7 90.5 all-gather.4
  121.4 29.0 all-gather.6
  152.7 107.5 all-gather.8
  261.9 58.7 all-gather.10
  322.8 60.9 reduce-scatter.4
  385.9 117.6 reduce-scatter.6
  534.6 80.7 reduce-scatter.8
  617.8 33.4 reduce-scatter.10

commit v3 on v2

--- a/solution.py
+++ b/solution.py
@@ -41,12 +41,8 @@
 
 
 def sum_small(block, axis):
-    count = lax.axis_size(axis)
-    bit = 1
-    while bit < count:
-        block = block + flip(block, axis, bit)
-        bit *= 2
-    return block
+    others = [flip(block, axis, bits) for bits in range(1, lax.axis_size(axis))]
+    return functools.reduce(jnp.add, others, block)
 
 
 def slots():
@@ -197,11 +193,14 @@
     gain_ref[...] += total
 
 
-def return_columns(mine, weights, interleave=False):
+def swap_columns(mine):
     ranks = lax.axis_size("seq")
-    rows, width = (weights[0].shape[0], weights[0].shape[1] // ranks)
-    total = width * len(weights)
-    pieces = swap_seq(mine.reshape(ranks, rows, total))
+    return swap_seq(mine.reshape(ranks, mine.shape[0] // ranks, mine.shape[1]))
+
+
+def return_columns(pieces, weights, interleave=False):
+    ranks, rows, total = pieces.shape
+    width = weights[0].shape[1] // ranks
     if width % LANES:
         grads = [
             jnp.moveaxis(pieces[:, :, i * width : (i + 1) * width], 0, 1)
@@ -225,13 +224,24 @@
     return grads, sums[:, 0]
 
 
-def product(left, right, left_dim, right_dim, precision=highest):
+def exact_product(left, right, left_dim, right_dim):
     return lax.dot_general(
         left,
         right,
         (((left_dim,), (right_dim,)), ((), ())),
-        precision=precision,
+        precision=highest,
         preferred_element_type=f32,
+    )
+
+
+def product(left, right, left_dim, right_dim):
+    left_high, right_high = (left.astype(bf16), right.astype(bf16))
+    left_low = (left - left_high.astype(f32)).astype(bf16)
+    right_low = (right - right_high.astype(f32)).astype(bf16)
+    return (
+        matmul(left_high, right_low, left_dim, right_dim)
+        + matmul(left_low, right_high, left_dim, right_dim)
+        + matmul(left_high, right_high, left_dim, right_dim)
     )
 
 
@@ -255,7 +265,7 @@
     key = bound_ref[...] * forget_sig
     query_sig = jax.nn.sigmoid(query_pre)
     lower = (at >= of).astype(f32)
-    cumul = product(lower, jnp.log1p(-key), 1, 0)
+    cumul = exact_product(lower, jnp.log1p(-key), 1, 0)
     grow = jnp.exp(cumul)
     shrink = jnp.exp(-cumul)
     end = grow[size - 1 :, :]
@@ -326,7 +336,7 @@
         key_t_grad = product(value, back, 1, 0)
         key_grad = key_d_grad * shrink + (p["tail"] * end * shrink) * key_t_grad
         change = query_d * query_d_grad - key_d * key_d_grad - key_t * key_t_grad
-        through = product(upper, change, 1, 0) + through_ref[:, cols]
+        through = exact_product(upper, change, 1, 0) + through_ref[:, cols]
         key_total = key_grad - through / (1.0 - key)
         new_back = back * keep + product(mixed_grad, query_d * p["linked"], 0, 0)
         back_ref[h] = new_back
@@ -456,6 +466,51 @@
     )(left, right, *extra)
 
 
+def mixer_sums_kernel(count, rows, core_ref, left_ref, right_ref, theirs_ref, out_ref, out_theirs_ref, total_ref):
+    step = pl.program_id(0)
+
+    @pl.when(step < count)
+    def _():
+        total = matmul(left_ref[...], right_ref[...], 0, 0) + theirs_ref[...].astype(f32)
+        total_ref[...] = total.astype(bf16)
+
+    @pl.when(step == count)
+    def _():
+        width = total_ref.shape[1]
+        for z in range(out_ref.shape[0]):
+            both = (out_ref[z, 0].astype(f32) + out_theirs_ref[z].astype(f32)).astype(bf16)
+            ranks = both.shape[1] // width
+            for j in range(ranks):
+                at = (z * ranks + j) * rows
+                total_ref[at : at + rows, :] = both[:, j * width : (j + 1) * width]
+
+
+def mixer_sums(left, right, theirs, out_sum, out_theirs, core):
+    tokens, height = left.shape
+    lines, cores, rows, width = out_sum.shape
+    size = right.shape[1] // 4
+    columns = block(height, size, at=lambda j, c: (0, jnp.minimum(j, 3)))
+    return pl.pallas_call(
+        functools.partial(mixer_sums_kernel, 4, rows),
+        grid_spec=pltpu.PrefetchScalarGridSpec(
+            num_scalar_prefetch=1,
+            grid=(5,),
+            in_specs=[
+                block(tokens, height),
+                block(tokens, size, at=lambda j, c: (0, jnp.minimum(j, 3))),
+                columns,
+                block(lines, 1, rows, width, at=lambda j, c: (0, c[0], 0, 0)),
+                block(lines, rows, width),
+            ],
+            out_specs=block(height, size, at=lambda j, c: (0, j)),
+        ),
+        out_shape=jax.ShapeDtypeStruct((height, 5 * size), bf16),
+        compiler_params=vmem,
+        cost_estimate=cost(3 * tokens * height * 4 * size),
+        name="mixer_sums",
+    )(core, left, right, theirs, out_sum, out_theirs)
+
+
 def store_halves(core, value, rows, row_block, mine_ref, theirs_ref):
     for z in range(value.shape[1] // (2 * row_block)):
         even = value[:, 2 * z * row_block : (2 * z + 1) * row_block]
@@ -474,8 +529,7 @@
 
 
 def assemble_kernel(places, half, row_block, normed, core_ref, *refs):
-    outs = 3 if normed else 1
-    pieces, gain_ref, all_ref = (refs[: len(refs) - 1 - outs], refs[-1 - outs], refs[-outs])
+    *pieces, gain_ref, all_ref, mine_ref, theirs_ref = refs
     for slot, (piece, row) in enumerate(places):
         rows = slice(slot * half, (slot + 1) * half)
         value = pieces[piece][row : row + half, :]
@@ -483,8 +537,7 @@
             wide = value.astype(f32)
             value = (wide * rms_factor(wide) * gain_ref[...]).astype(bf16)
         all_ref[rows, :] = value
-        if normed:
-            store_halves(core_ref[0], value, rows, row_block, *refs[-2:])
+        store_halves(core_ref[0], value, rows, row_block, mine_ref, theirs_ref)
 
 
 def assemble(gathered, core, row_block, gain=None):
@@ -493,7 +546,7 @@
     tokens, width = (half * len(places), pieces[0].shape[1])
     normed = gain is not None
     gain = gain if normed else jnp.zeros((1, width), f32)
-    shapes = [(tokens, width), (tokens, width // 2), (tokens, width // 2)][: 3 if normed else 1]
+    shapes = [(tokens, width), (tokens, width // 2), (tokens, width // 2)]
     return pl.pallas_call(
         functools.partial(assemble_kernel, places, half, row_block, normed),
         grid_spec=pltpu.PrefetchScalarGridSpec(
@@ -553,7 +606,7 @@
         cost_estimate=cost(3 * tokens * depth * width),
         name="exchanged_product",
     )(places, left, weight)
-    return partial, swap_seq(partial.reshape(ranks, 2 * half, width))
+    return partial.reshape(ranks, 2 * half, width)
 
 
 def partial_product(left, weights, widths, half, columns=256):
@@ -830,7 +883,7 @@
     gated, partials = gate_out(mixed, pre, out_rows, half)
     cotangent = gather_seq(after(cotangent_low, normed_in))
     branch_parts = scatter_seq(partials, half)
-    (cotangent_all,) = assemble(cotangent, core, rank_rows)
+    cotangent_all, cotangent_mine, cotangent_theirs = assemble(cotangent, core, rank_rows)
     resid, normed_low = combine(
         residual, branch_parts, (after(x_low, cotangent_all), gain_mid), (f32, bf16), half
     )
@@ -838,8 +891,9 @@
 
     both, hidden, mid_all = ffn_forward(normed_mid, ffn_cols, half)
 
-    down_sum = dense(cotangent_all, hidden, bf16, 0)
-    down_mine = lax.psum_scatter(down_sum, "dp", scatter_dimension=0, tiled=True)
+    down_theirs = flip(dense(cotangent_theirs, hidden, bf16, 0), "dp", 1)
+    down_sum = dense(cotangent_mine, hidden, bf16, 0, down_theirs)
+    down_mine = scatter_dp(down_sum)
     cotangent_all = after(cotangent_all, down_sum)
     ffn_right = ffn_backward(cotangent_all, down_cols, both)
     mid_partials = partial_product(ffn_right, [ffn_cols], [ffn_cols.shape[1]], half)
@@ -852,36 +906,38 @@
     )
     branch, places = gather_seq(branch_own)
     row_place = row_places()
-    out_partial, out_parts = exchanged_product(after(hidden, branch_own), down_cols, row_place, half)
+    out_partial = exchanged_product(after(hidden, branch_own), down_cols, row_place, half)
     branch = (after(branch[0], out_partial),) + branch[1:]
     branch_low, gated_grad = gated_gradient((branch, places), out_rows, half)
+    out_parts = swap_seq(after(out_partial, branch_low))
     mix_right, logit_part = recurrence_backward(segments, table, pre, bound, mixed, gated_grad, states)
-    (ffn_down_weight_grad,), _ = return_columns(after(down_mine, branch_low), [ffn_down_weight])
-    mix_theirs = dense(in_theirs, after(mix_right, ffn_down_weight_grad, out_parts), bf16, 0)
-    out_sum = dense(gated, after(branch_low, mix_theirs), bf16, 0)
-    mix_theirs = flip(mix_theirs, "dp", 1)
-    mix_sum = dense(in_mine, after(mix_right, out_sum), bf16, 0, mix_theirs)
+    mix_theirs = dense(in_theirs, mix_right, bf16, 0)
+    out_sum = dense(gated, after(branch_low, mix_theirs, out_parts), bf16, 0)
+    out_sum = out_sum.reshape(count // 2, 2, my_rows, width)
+    out_theirs = flip(lax.dynamic_index_in_dim(out_sum, 1 - core[0], 1, keepdims=False), "dp", 1)
+    mix_sum = mixer_sums(in_mine, mix_right, flip(mix_theirs, "dp", 1), out_sum, out_theirs, core)
     mix_mine = scatter_dp(mix_sum)
-    out_mine = lax.psum_scatter(after(out_sum, mix_sum), "dp", scatter_dimension=0, tiled=True)
+    down_back = swap_columns(after(down_mine, mix_sum))
+    ffn_back = swap_columns(after(ffn_mine, down_back))
+    in_partial = exchanged_product(after(mix_right, mix_sum), mix_cols, row_place, half)
+    in_parts = swap_seq(after(in_partial, ffn_back))
+    (block_output,) = combine(
+        lambda total, resid: (resid + total,), (out_parts,), (after(resid, in_partial),), (bf16,), half
+    )
     (ffn_gate_weight_grad, ffn_up_weight_grad), ffn_sums = return_columns(
-        after(ffn_mine, mix_sum), [ffn_gate_weight, ffn_up_weight], True
-    )
-    (block_output,) = combine(
-        lambda total, resid: (resid + total,), (out_parts,), (after(resid, mix_sum),), (bf16,), half
-    )
-    _, in_parts = exchanged_product(after(mix_right, mix_sum, ffn_sums), mix_cols, row_place, half)
-
-    output_weight_grad = lax.ppermute(
-        out_mine, ("dp", "seq"), [(b, a) for a, b in row_route()]
-    ).astype(f32)
-    logit_sum = gather_small(sum_small(-logit_part[0] * (1.0 - bound[0]), "dp"), "seq")
+        after(ffn_back, in_partial), [ffn_gate_weight, ffn_up_weight], True
+    )
+    (input_grad,) = combine(input_back, (in_parts,), (resid_grad, x_low, gain_in), (f32,), half)
+    (ffn_down_weight_grad,), _ = return_columns(after(down_back, in_partial), [ffn_down_weight])
+
+    logit_sum = gather_small(sum_small(-after(logit_part, in_partial)[0] * (1.0 - bound[0]), "dp"), "seq")
     at = (lax.axis_index("dp") * ranks + rank) * my_rows
     bound_logit_grad = lax.dynamic_slice_in_dim(logit_sum, at, my_rows)
-    (input_grad,) = combine(
-        input_back, (in_parts,), (after(resid_grad, bound_logit_grad), x_low, gain_in), (f32,), half
-    )
-    mix_mine = after(mix_mine, input_grad, block_output)
-    mix_grads, mix_sums = return_columns(mix_mine, mix_weights)
+    mix_mine = after(mix_mine, in_parts)
+    mix_grads, mix_sums = return_columns(swap_columns(mix_mine[:, : 4 * my_width]), mix_weights)
+    out_mine = mix_mine[:, 4 * my_width :].reshape(ranks, my_rows, my_width)
+    out_mine = lax.ppermute(out_mine, ("dp", "seq"), [(b, a) for a, b in row_route()])
+    output_weight_grad = jnp.moveaxis(out_mine, 0, 1).reshape(my_rows, width).astype(f32)
     query_weight_grad, forget_weight_grad, input_weight_grad, output_gate_weight_grad = mix_grads
     mix_gain_grad = mix_sums / mix_gain.astype(f32)
     ffn_gain_grad = ffn_sums / ffn_gain.astype(f32)

time: 692 us -> 659 us (0.952)
  waiting for transfers between devices: 263 us -> 229 us
  local copies, waits for them, and re-layouts: 39.7 us -> 51.8 us
  Pallas kernels: 243 us -> 232 us
  blocking collectives: 27 us -> 17 us
  starting transfers between devices: 82.3 us -> 91.8 us
    reduce_scatter x2 -> x0, waiting for transfers between devices: 16.7 us -> none  [the longest x1 8.72 us: local(): lax.psum_scatter(down_sum, 'dp', scatter_dimension=0, tiled=True)]
    ppermute x1, waiting for transfers between devices: 10.8 us -> 0.01 us  [local(): lax.ppermute(out_mine, ('dp', 'seq'), [(b, a) for a, b in row_route()])]
    all_to_all x2 -> x1, blocking collectives: 27 us -> 17 us  [swap_seq(): lax.all_to_all(pieces, 'seq', split_axis=0, concat_axis=0, tiled=True)]
    pallas_call x0 -> x1, Pallas kernels: none -> 8.9 us  [mixer_sums(): pl.pallas_call(functools.partial(mixer_sums_kernel, 4, rows), grid_spec=p...]
    pallas_call x1, Pallas kernels: 37.4 us -> 29.1 us  [recurrence_backward(): pl.pallas_call(backward_kernel, grid_spec=pltpu.PrefetchScalarGridSpec(nu...]
    pallas_call x6, Pallas kernels: 62.3 us -> 54.2 us  [dense(): pl.pallas_call(functools.partial(product_kernel, left_dim), grid=(width /...]
    all_to_all x5 -> x6, waiting for transfers between devices: 21.5 us -> 13.5 us  [swap_seq(): lax.all_to_all(pieces, 'seq', split_axis=0, concat_axis=0, tiled=True)]
    ppermute x37 -> x43, starting transfers between devices: 47.6 us -> 54.1 us  [flip(): lax.ppermute(block, axis, [(i, i ^ bits) for i in range(lax.axis_size(axi...]
  transfers between devices with their start and end apart: 52 -> 58, of which waited for: 33 -> 27; matrix products, arithmetic and copies ran while one was open for 2% -> 4% of each run, Pallas kernels for 35% -> 35%
where the time goes in v3:
time: 659 us; the launch traced here: 648 us
  Pallas kernels  232 us (35%)
  waiting for transfers between devices  229 us (35%)
  starting transfers between devices  91.8 us (14%)
  local copies, waits for them, and re-layouts  51.8 us (8%)
  blocking collectives  17 us (3%)
  between operations  15.3 us (2%)
  other arithmetic  11.9 us (2%)
    ppermute x43, waiting for transfers between devices, flip(): lax.ppermute(block, axis, [(i, i ^ bits) for i in range(lax.axis_size(axi...  189 us
    pallas_call x6, Pallas kernels, dense(): pl.pallas_call(functools.partial(product_kernel, left_dim), grid=(width /...  54.2 us
    ppermute x43, starting transfers between devices, flip(): lax.ppermute(block, axis, [(i, i ^ bits) for i in range(lax.axis_size(axi...  54.1 us
    unnamed x128, local copies, waits for them, and re-layouts  39.1 us
    pallas_call x1, Pallas kernels, recurrence_backward(): pl.pallas_call(backward_kernel, grid_spec=pltpu.PrefetchScalarGridSpec(nu...  29.1 us
    pallas_call x2, Pallas kernels, exchanged_product(): pl.pallas_call(functools.partial(ordered_kernel, half), grid_spec=pltpu.P...  26 us
    all_to_all x6, starting transfers between devices, swap_seq(): lax.all_to_all(pieces, 'seq', split_axis=0, concat_axis=0, tiled=True)  24.3 us
    all_gather x4, waiting for transfers between devices, gather_dp(): return lax.all_gather(block, 'dp', axis=0, tiled=True)  24.1 us
  transfers between devices with their start and end apart: 58, of which 27 were waited for; matrix products, arithmetic and copies ran while one was open for 4% of the time, Pallas kernels for 35%

profile of v3, /device:TPU:1, one launch (start us, length us, event | category | flops | bytes accessed | tf_op | source)
XLA Modules:
  0.0 648.2 jit_solution(14498577522026210790)
XLA Ops:
  11.5 17.0 %all_to_all.35 = bf16[4,64,2048]{2,1,0:T(8,128)(2,1)} all-to-all(bf16[4,64,2048]{2,1,0:T(8,128)(2,1)S(1)} %column_pieces.3), channel_id=1, replica_groups=mesh['dp'=8,'seq'=4] {'seq'}, dimensions={0} | all-to-all | bytes 2097152 | tf_op jit(solution)/shard_map/all_to_all | solution.py:111
  43.1 18.3 %collective-permute-done.6 = bf16[64,3]{0,1:T(4,128)(2,1)S(1)} collective-permute-done((bf16[64,3]{0,1:T(4,128)(2,1)S(1)}, bf16[64,3]{0,1:T(4,128)(2,1)S(1)}, u32[]{:S(2)}, u32[]{:S(2)}) %collective-permute-start.6) | collective-permute-done | bytes 416 | tf_op jit(solution)/shard_map/ppermute | solution.py:27
  73.5 21.7 %collective-permute-done.1 = s32[512]{0:T(512)S(1)} collective-permute-done((s32[512]{0:T(512)S(1)}, s32[512]{0:T(512)S(1)}, u32[]{:S(2)}, u32[]{:S(2)}) %collective-permute-start.1) | collective-permute-done | bytes 2080 | tf_op jit(solution)/shard_map/ppermute | solution.py:27
  100.2 9.7 %collective-permute-done.4.refs_3_ = bf16[128,2048]{1,0:T(8,128)(2,1)S(1)} collective-permute-done((bf16[128,2048]{1,0:T(8,128)(2,1)S(1)}, bf16[128,2048]{1,0:T(8,128)(2,1)S(1)}, u32[]{:S(2)}, u32[]{:S(2)}) %collective-permute-start.4) | collective-permute-done | bytes 524320 | tf_op jit(solution)/shard_map/ppermute | solution.py:27
  127.7 12.4 %dense.6.pre_ref.outgate_pre_ref = f32[1024,2048]{1,0:T(8,128)} custom-call(bf16[1024,2048]{1,0:T(8,128)(2,1)S(1)} %copy-done.35, bf16[2048,2048]{1,0:T(8,128)(2,1)} %all-gather.5.cloned.1.call-done.refs_1_.weight_ref), custom_call_target="tpu_custom_call" | custom-call | flops 12884901888 | tf_op jit(solution)/shard_map/dense/pallas_call | solution.py:456
  141.3 13.2 %recurrence_forward.1 = (f32[1024,512]{1,0:T(8,128)S(1)}, f32[8,4,128,128]{3,2,1,0:T(8,128)S(1)}) custom-call(s32[1024]{0:T(1024)S(1)} %pad_add_fusion.seg_ref, s32[8]{0:T(128)S(1)} %reshape.123.slot_ref, s32[1024,1]{1,0:T(8,128)S(1)} %copy-done.27, s32[1,1024]{1,0:T(1,128)S(1)} %bitcast.49, f32[1024,2048]{1,0:T(8,128)} %dense.6.pre_ref.outgate_pre_ref, ...), custom_call_target="tpu_custom_call" | custom-call | flops 21474836480 | tf_op jit(solution)/shard_map/recurrence_forward/pallas_call | solution.py:359
  171.6 16.9 %collective-permute-done.12.refs_1_ = bf16[256,2048]{1,0:T(8,128)(2,1)S(1)} collective-permute-done((bf16[256,2048]{1,0:T(8,128)(2,1)S(1)}, bf16[256,2048]{1,0:T(8,128)(2,1)S(1)}, u32[]{:S(2)}, u32[]{:S(2)}) %collective-permute-start.12) | collective-permute-done | bytes 1048608 | tf_op jit(solution)/shard_map/ppermute | solution.py:27
  217.3 17.5 %collective-permute-done.20.refs_1_ = bf16[256,2048]{1,0:T(8,128)(2,1)S(1)} collective-permute-done((bf16[256,2048]{1,0:T(8,128)(2,1)S(1)}, bf16[256,2048]{1,0:T(8,128)(2,1)S(1)}, u32[]{:S(2)}, u32[]{:S(2)}) %collective-permute-start.20) | collective-permute-done | bytes 1048608 | tf_op jit(solution)/shard_map/ppermute | solution.py:27
  239.4 10.5 %collective-permute-done.22.refs_3_ = bf16[128,2048]{1,0:T(8,128)(2,1)S(1)} collective-permute-done((bf16[128,2048]{1,0:T(8,128)(2,1)S(1)}, bf16[128,2048]{1,0:T(8,128)(2,1)S(1)}, u32[]{:S(2)}, u32[]{:S(2)}) %collective-permute-start.22) | collective-permute-done | bytes 524320 | tf_op jit(solution)/shard_map/ppermute | solution.py:27
  251.6 8.9 %all-gather.9.cloned.1.call-done.refs_5_.refs_0_ = bf16[2048,2816]{1,0:T(8,128)(2,1)} async-done(((bf16[256,2816]{1,0:T(8,128)(2,1)}), bf16[2048,2816]{1,0:T(8,128)(2,1)}) %all-gather.9.cloned.1.call-update) | async-done | bytes 11534352 | tf_op jit(solution)/shard_map/all_gather | solution.py:115
  265.0 20.0 %ffn_forward.1 = (f32[1024,2816]{1,0:T(8,128)}, bf16[1024,1408]{1,0:T(8,128)(2,1)}, bf16[1024,2048]{1,0:T(8,128)(2,1)}) custom-call(bf16[256,2048]{1,0:T(8,128)(2,1)S(1)} %copy-done.43, bf16[256,2048]{1,0:T(8,128)(2,1)S(1)} %collective-permute-done.20.refs_1_, bf16[256,2048]{1,0:T(8,128)(2,1)S(1)} %copy-done.30, bf16[128,2048]{1,0:T(8,128)(2,1)S(1)} %copy-done.45, ...), custom_call_target="tpu_custom_call" | custom-call | flops 17716740096 | tf_op jit(solution)/shard_map/ffn_forward/pallas_call | solution.py:715
  305.4 15.2 %all-gather.11.cloned.1.call-done.weight_ref = bf16[2048,1408]{1,0:T(8,128)(2,1)} async-done(((bf16[256,1408]{1,0:T(8,128)(2,1)}), bf16[2048,1408]{1,0:T(8,128)(2,1)}) %all-gather.11.cloned.1.call-update) | async-done | bytes 5767184 | tf_op jit(solution)/shard_map/all_gather | solution.py:115
  322.9 14.0 %ffn_backward.1.left_ref.refs_1_ = bf16[1024,2816]{1,0:T(8,128)(2,1)} custom-call(bf16[1024,2048]{1,0:T(8,128)(2,1)S(1)} %copy-done.34, bf16[2048,1408]{1,0:T(8,128)(2,1)} %all-gather.11.cloned.1.call-done.weight_ref, f32[1024,2816]{1,0:T(8,128)} %get-tuple-element.92.both_ref), custom_call_target="tpu_custom_call" | custom-call | flops 11811160064 | tf_op jit(solution)/shard_map/ffn_backward/pallas_call | solution.py:759
  336.9 17.8 %partial_product.1 = (bf16[256,2048]{1,0:T(8,128)(2,1)}, bf16[256,2048]{1,0:T(8,128)(2,1)}, f32[512,2048]{1,0:T(8,128)}) custom-call(bf16[1024,2816]{1,0:T(8,128)(2,1)} %ffn_backward.1.left_ref.refs_1_, bf16[2048,2816]{1,0:T(8,128)(2,1)} %all-gather.9.cloned.1.call-done.refs_5_.refs_0_), custom_call_target="tpu_custom_call" | custom-call | flops 17716740096 | tf_op jit(solution)/shard_map/partial_product/pallas_call | solution.py:618
  357.0 17.9 %dense.9 = bf16[2048,2816]{1,0:T(8,128)(2,1)} custom-call(bf16[1024,2048]{1,0:T(8,128)(2,1)S(1)} %copy-done.50, bf16[1024,2816]{1,0:T(8,128)(2,1)} %ffn_backward.1.left_ref.refs_1_), custom_call_target="tpu_custom_call" | custom-call | flops 17716740096 | tf_op jit(solution)/shard_map/dense/pallas_call | solution.py:456
  383.9 10.6 %collective-permute-done.27.refs_3_ = bf16[128,2048]{1,0:T(8,128)(2,1)S(1)} collective-permute-done((bf16[128,2048]{1,0:T(8,128)(2,1)S(1)}, bf16[128,2048]{1,0:T(8,128)(2,1)S(1)}, u32[]{:S(2)}, u32[]{:S(2)}) %collective-permute-start.27) | collective-permute-done | bytes 524320 | tf_op jit(solution)/shard_map/ppermute | solution.py:27
  400.9 21.7 %collective-permute-done.29.refs_1_ = bf16[256,2048]{1,0:T(8,128)(2,1)S(1)} collective-permute-done((bf16[256,2048]{1,0:T(8,128)(2,1)S(1)}, bf16[256,2048]{1,0:T(8,128)(2,1)S(1)}, u32[]{:S(2)}, u32[]{:S(2)}) %collective-permute-start.29) | collective-permute-done | bytes 1048608 | tf_op jit(solution)/shard_map/ppermute | solution.py:27
  423.8 11.9 %exchanged_product.2 = bf16[1024,2048]{1,0:T(8,128)(2,1)} custom-call(s32[8]{0:T(128)S(1)} %multiply_add_fusion.places_ref, bf16[1024,1408]{1,0:T(8,128)(2,1)S(1)} %copy-done.48, bf16[2048,1408]{1,0:T(8,128)(2,1)} %all-gather.11.cloned.1.call-done.weight_ref), custom_call_target="tpu_custom_call" | custom-call | flops 8858370048 | tf_op jit(solution)/shard_map/exchanged_product/pallas_call | solution.py:596
  450.2 29.1 %recurrence_backward.1 = (bf16[1024,2048]{1,0:T(8,128)(2,1)}, f32[1,512]{1,0:T(1,128)S(1)}) custom-call(s32[1024]{0:T(1024)S(1)} %pad_add_fusion.seg_ref, s32[8]{0:T(128)S(1)} %reshape.123.slot_ref, s32[1024,1]{1,0:T(8,128)S(1)} %copy-done.28, s32[1,1024]{1,0:T(1,128)S(1)} %bitcast.50, f32[1024,2048]{1,0:T(8,128)} %dense.6.pre_ref.outgate_pre_ref, ...), custom_call_target="tpu_custom_call" | custom-call | flops 41607495680 | tf_op jit(solution)/shard_map/recurrence_backward/pallas_call | solution.py:392
  479.3 7.8 %dense.10 = bf16[1024,2048]{1,0:T(8,128)(2,1)} custom-call(bf16[1024,1024]{1,0:T(8,128)(2,1)S(1)} %copy-done.37, bf16[1024,2048]{1,0:T(8,128)(2,1)} %get-tuple-element.112.refs_1_.right_ref.left_ref), custom_call_target="tpu_custom_call" | custom-call | flops 6442450944 | tf_op jit(solution)/shard_map/dense/pallas_call | solution.py:456
  502.7 8.9 %mixer_sums.1 = bf16[1024,2560]{1,0:T(8,128)(2,1)} custom-call(s32[1]{0:T(128)} %bitcast.4.core_ref, bf16[1024,1024]{1,0:T(8,128)(2,1)S(1)} %copy-done.36, bf16[1024,2048]{1,0:T(8,128)(2,1)} %get-tuple-element.112.refs_1_.right_ref.left_ref, bf16[1024,2048]{1,0:T(8,128)(2,1)} %collective-permute-done.33.theirs_ref, bf16[4,2,64,2048]{3,2,1,0:T(8,128)(2,1)S(1)} %bitcast.47, ...), custom_call_target="tpu_custom_call" | custom-call | flops 6442450944 | tf_op jit(solution)/shard_map/mixer_sums/pallas_call | solution.py:493
  515.2 9.9 %all-to-all-done.3.refs_0_ = bf16[4,64,1408]{2,1,0:T(8,128)(2,1)S(1)} async-done(((bf16[4,64,1408]{2,1,0:T(8,128)(2,1)}), bf16[4,64,1408]{2,1,0:T(8,128)(2,1)S(1)}, u32[]{:S(2)}, u32[]{:S(2)}) %all-to-all-start.3) | async-done | bytes 720928 | tf_op jit(solution)/shard_map/all_to_all | solution.py:111
  529.5 14.0 %exchanged_product.3 = bf16[1024,2048]{1,0:T(8,128)(2,1)S(1)} custom-call(s32[8]{0:T(128)S(1)} %multiply_add_fusion.places_ref, bf16[1024,2048]{1,0:T(8,128)(2,1)} %get-tuple-element.112.refs_1_.right_ref.left_ref, bf16[2048,2048]{1,0:T(8,128)(2,1)} %all-gather.5.cloned.1.call-done.refs_1_.weight_ref), custom_call_target="tpu_custom_call" | custom-call | flops 12884901888 | tf_op jit(solution)/shard_map/exchanged_product/pallas_call | solution.py:596
  566.1 33.1 %collective-permute-done.42 = f32[512]{0:T(512)S(1)} collective-permute-done((f32[512]{0:T(512)S(1)}, f32[512]{0:T(512)S(1)}, u32[]{:S(2)}, u32[]{:S(2)}) %collective-permute-start.42) | collective-permute-done | bytes 2080 | tf_op jit(solution)/shard_map/ppermute | solution.py:27
  (308 shorter events, 254.7 us)
Async XLA Ops:
  7.2 118.3 %all-gather.5.cloned.1.call-start = ((), (), s32[]{:S(2)}) async-start(), calls=%async_computation.10 | async-start | bytes 9437184 | tf_op jit(solution)/shard_map/all_gather | solution.py:115
  30.8 37.7 %all-to-all-start.1 = ((bf16[4,64,4224]{2,1,0:T(8,128)(2,1)}), bf16[4,64,4224]{2,1,0:T(8,128)(2,1)S(1)}, u32[]{:S(2)}, u32[]{:S(2)}) async-start(bf16[4,64,4224]{2,1,0:T(8,128)(2,1)} %pad_maximum_fusion), calls=%async_computation.1 | async-start | bytes 4325376 | tf_op jit(solution)/shard_map/all_to_all | solution.py:111
  34.5 122.7 %all-gather.7.cloned.1.call-start = ((), (), s32[]{:S(2)}) async-start(), calls=%async_computation.11 | async-start | bytes 2359296 | tf_op jit(solution)/shard_map/all_gather | solution.py:115
  34.6 26.7 %collective-permute-start.6 = (bf16[64,3]{0,1:T(4,128)(2,1)S(1)}, bf16[64,3]{0,1:T(4,128)(2,1)S(1)}, u32[]{:S(2)}, u32[]{:S(2)}) collective-permute-start(bf16[64,3]{0,1:T(4,128)(2,1)S(1)} %pad_maximum_fusion.6), channel_id=1, source_target_pairs={{0,1},{1,0},{2,3},{3,2},{4,5},{5,4},{6,7},{7,6},{8,9},{9,8},{10,11... | collective-permute-start | bytes 1160 | tf_op jit(solution)/shard_map/ppermute | solution.py:27
  36.1 25.4 %collective-permute-start = (s32[256]{0:T(256)S(1)}, s32[256]{0:T(256)S(1)}, u32[]{:S(2)}, u32[]{:S(2)}) collective-permute-start(s32[256]{0:T(256)S(1)} %bitcast.70), channel_id=1, source_target_pairs={{0,1},{1,0},{2,3},{3,2},{4,5},{5,4},{6,7},{7,6},{8,9},{9,8},{10,11... | collective-permute-start | bytes 3080 | tf_op jit(solution)/shard_map/ppermute | solution.py:27
  36.2 79.9 %collective-permute-start.11 = (bf16[64,2048]{1,0:T(8,128)(2,1)}, bf16[64,2048]{1,0:T(8,128)(2,1)S(1)}, u32[]{:S(2)}, u32[]{:S(2)}) collective-permute-start(bf16[64,2048]{1,0:T(8,128)(2,1)} %param.25), channel_id=1, source_target_pairs={{0,0},{1,4},{2,8},{3,12},{4,16},{5,20},{6,24},{7,28},{8,1},{9,5},{... | collective-permute-start | bytes 786440 | tf_op jit(solution)/shard_map/ppermute | solution.py:875
  68.5 29.1 %collective-permute-start.2 = (bf16[256,2048]{1,0:T(8,128)(2,1)S(1)}, bf16[256,2048]{1,0:T(8,128)(2,1)S(1)}, u32[]{:S(2)}, u32[]{:S(2)}) collective-permute-start(bf16[256,2048]{1,0:T(8,128)(2,1)S(1)} %bitcast.36), channel_id=1, source_target_pairs={{0,1},{1,0},{2,3},{3,2},{4,5},{5,4},{6,7},{7,6},{8,9},{9,8},{10,11... | collective-permute-start | bytes 3145736 | tf_op jit(solution)/shard_map/ppermute | solution.py:27
  70.6 27.4 %collective-permute-start.3 = (bf16[256,2048]{1,0:T(8,128)(2,1)S(1)}, bf16[256,2048]{1,0:T(8,128)(2,1)S(1)}, u32[]{:S(2)}, u32[]{:S(2)}) collective-permute-start(bf16[256,2048]{1,0:T(8,128)(2,1)S(1)} %bitcast.37), channel_id=1, source_target_pairs={{0,2},{1,3},{2,0},{3,1},{4,6},{5,7},{6,4},{7,5},{8,10},{9,11},{10,... | collective-permute-start | bytes 3145736 | tf_op jit(solution)/shard_map/ppermute | solution.py:27
  70.6 24.6 %collective-permute-start.1 = (s32[512]{0:T(512)S(1)}, s32[512]{0:T(512)S(1)}, u32[]{:S(2)}, u32[]{:S(2)}) collective-permute-start(s32[512]{0:T(512)S(1)} %pad_add_fusion.1), channel_id=1, source_target_pairs={{0,2},{1,3},{2,0},{3,1},{4,6},{5,7},{6,4},{7,5},{8,10},{9,11},{10,... | collective-permute-start | bytes 6152 | tf_op jit(solution)/shard_map/ppermute | solution.py:27
  116.9 143.6 %all-gather.9.cloned.1.call-start = ((), (), s32[]{:S(2)}) async-start(), calls=%async_computation.12 | async-start | bytes 12976128 | tf_op jit(solution)/shard_map/all_gather | solution.py:115
  119.6 201.1 %all-gather.11.cloned.1.call-start = ((), (), s32[]{:S(2)}) async-start(), calls=%async_computation.13 | async-start | bytes 6488064 | tf_op jit(solution)/shard_map/all_gather | solution.py:115
  123.4 44.8 %collective-permute-start.16 = (bf16[256,2048]{1,0:T(8,128)(2,1)S(1)}, bf16[256,2048]{1,0:T(8,128)(2,1)S(1)}, u32[]{:S(2)}, u32[]{:S(2)}) collective-permute-start(bf16[256,2048]{1,0:T(8,128)(2,1)S(1)} %bitcast.41), channel_id=1, source_target_pairs={{0,1},{1,0},{2,3},{3,2},{4,5},{5,4},{6,7},{7,6},{8,9},{9,8},{10,11... | collective-permute-start | bytes 3145736 | tf_op jit(solution)/shard_map/ppermute | solution.py:27
  124.8 44.2 %collective-permute-start.17 = (bf16[256,2048]{1,0:T(8,128)(2,1)S(1)}, bf16[256,2048]{1,0:T(8,128)(2,1)}, u32[]{:S(2)}, u32[]{:S(2)}) collective-permute-start(bf16[256,2048]{1,0:T(8,128)(2,1)S(1)} %bitcast.42), channel_id=1, source_target_pairs={{0,2},{1,3},{2,0},{3,1},{4,6},{5,7},{6,4},{7,5},{8,10},{9,11},{10,... | collective-permute-start | bytes 3145736 | tf_op jit(solution)/shard_map/ppermute | solution.py:27
  140.2 237.0 %reduce-scatter.4.cloned.1.call-start = ((), (), s32[]{:S(2)}) async-start(), calls=%async_computation.14 | async-start | bytes 3604480 | tf_op jit(solution)/shard_map/reduce_scatter | solution.py:120
  168.2 31.6 %collective-permute-start.18 = (bf16[128,2048]{1,0:T(8,128)(2,1)S(1)}, bf16[128,2048]{1,0:T(8,128)(2,1)S(1)}, u32[]{:S(2)}, u32[]{:S(2)}) collective-permute-start(bf16[128,2048]{1,0:T(8,128)(2,1)S(1)} %slice.100), channel_id=1, source_target_pairs={{0,2},{1,3},{2,0},{3,1},{4,6},{5,7},{6,4},{7,5},{8,10},{9,11},{10,... | collective-permute-start | bytes 1572872 | tf_op jit(solution)/shard_map/ppermute | solution.py:27
  170.1 29.7 %collective-permute-start.19 = (bf16[128,2048]{1,0:T(8,128)(2,1)S(1)}, bf16[128,2048]{1,0:T(8,128)(2,1)S(1)}, u32[]{:S(2)}, u32[]{:S(2)}) collective-permute-start(bf16[128,2048]{1,0:T(8,128)(2,1)S(1)} %slice.101), channel_id=1, source_target_pairs={{0,1},{1,0},{2,3},{3,2},{4,5},{5,4},{6,7},{7,6},{8,9},{9,8},{10,11... | collective-permute-start | bytes 1572872 | tf_op jit(solution)/shard_map/ppermute | solution.py:27
  305.2 220.8 %reduce-scatter.6.cloned.1.call-start = ((), (), s32[]{:S(2)}) async-start(), calls=%async_computation.15 | async-start | bytes 12976128 | tf_op jit(solution)/shard_map/reduce_scatter | solution.py:902
  354.6 24.8 %collective-permute-start.25 = (bf16[256,2048]{1,0:T(8,128)(2,1)}, bf16[256,2048]{1,0:T(8,128)(2,1)S(1)}, u32[]{:S(2)}, u32[]{:S(2)}) collective-permute-start(bf16[256,2048]{1,0:T(8,128)(2,1)} %get-tuple-element.95), channel_id=1, source_target_pairs={{0,1},{1,0},{2,3},{3,2},{4,5},{5,4},{6,7},{7,6},{8,9},{9,8},{10,11... | collective-permute-start | bytes 3145736 | tf_op jit(solution)/shard_map/ppermute | solution.py:27
  355.8 24.5 %collective-permute-start.26 = (bf16[256,2048]{1,0:T(8,128)(2,1)}, bf16[256,2048]{1,0:T(8,128)(2,1)}, u32[]{:S(2)}, u32[]{:S(2)}) collective-permute-start(bf16[256,2048]{1,0:T(8,128)(2,1)} %get-tuple-element.98), channel_id=1, source_target_pairs={{0,2},{1,3},{2,0},{3,1},{4,6},{5,7},{6,4},{7,5},{8,10},{9,11},{10,... | collective-permute-start | bytes 3145736 | tf_op jit(solution)/shard_map/ppermute | solution.py:27
  442.4 51.9 %all-to-all-start.2 = ((bf16[4,256,2048]{2,1,0:T(8,128)(2,1)}), bf16[4,256,2048]{2,1,0:T(8,128)(2,1)}, u32[]{:S(2)}, u32[]{:S(2)}) async-start(bf16[4,256,2048]{2,1,0:T(8,128)(2,1)} %bitcast.54), calls=%async_computation.3 | async-start | bytes 8388608 | tf_op jit(solution)/shard_map/all_to_all | solution.py:111
  447.4 156.9 %reduce-scatter.8.cloned.1.call-start = ((), (), s32[]{:S(2)}) async-start(), calls=%async_computation.16 | async-start | bytes 6553600 | tf_op jit(solution)/shard_map/reduce_scatter | solution.py:120
  548.0 56.3 %all-to-all-start.5 = ((bf16[4,256,2048]{2,1,0:T(8,128)(2,1)}), bf16[4,256,2048]{2,1,0:T(8,128)(2,1)}, u32[]{:S(2)}, u32[]{:S(2)}) async-start(bf16[4,256,2048]{2,1,0:T(8,128)(2,1)} %bitcast.45), calls=%async_computation.7 | async-start | bytes 8388608 | tf_op jit(solution)/shard_map/all_to_all | solution.py:111
  564.4 34.8 %collective-permute-start.42 = (f32[512]{0:T(512)S(1)}, f32[512]{0:T(512)S(1)}, u32[]{:S(2)}, u32[]{:S(2)}) collective-permute-start(f32[512]{0:T(512)S(1)} %add_add_fusion), channel_id=1, source_target_pairs={{0,1},{1,0},{2,3},{3,2},{4,5},{5,4},{6,7},{7,6},{8,9},{9,8},{10,11... | collective-permute-start | bytes 6152 | tf_op jit(solution)/shard_map/ppermute | solution.py:27
  606.8 31.4 %all-to-all-start.6 = ((bf16[4,64,2048]{2,1,0:T(8,128)(2,1)}), bf16[4,64,2048]{2,1,0:T(8,128)(2,1)S(1)}, u32[]{:S(2)}, u32[]{:S(2)}) async-start(bf16[4,64,2048]{2,1,0:T(8,128)(2,1)} %bitcast.56), calls=%async_computation.9 | async-start | bytes 2097152 | tf_op jit(solution)/shard_map/all_to_all | solution.py:111
  (98 other events, 952.2 us)
Sparse Core Ops, SparseCore 0:
  28.7 90.5 all-gather.4
  121.4 29.0 all-gather.6
  152.7 107.6 all-gather.8
  262.0 58.7 all-gather.10
  322.8 54.2 reduce-scatter.3
  380.4 116.0 reduce-scatter.5
  511.8 91.0 reduce-scatter.7

commit v4 on v3

--- a/solution.py
+++ b/solution.py
@@ -12,7 +12,6 @@
 
 eps_model = 1e-06
 eps_group = 1e-05
-highest = lax.Precision.HIGHEST
 f32 = jnp.float32
 bf16 = jnp.bfloat16
 
@@ -224,14 +223,11 @@
     return grads, sums[:, 0]
 
 
-def exact_product(left, right, left_dim, right_dim):
-    return lax.dot_general(
-        left,
-        right,
-        (((left_dim,), (right_dim,)), ((), ())),
-        precision=highest,
-        preferred_element_type=f32,
-    )
+def sums(mask, terms):
+    high = terms.astype(bf16)
+    low = (terms - high.astype(f32)).astype(bf16)
+    ones = mask.astype(bf16)
+    return matmul(ones, low) + matmul(ones, high)
 
 
 def product(left, right, left_dim, right_dim):
@@ -265,7 +261,7 @@
     key = bound_ref[...] * forget_sig
     query_sig = jax.nn.sigmoid(query_pre)
     lower = (at >= of).astype(f32)
-    cumul = exact_product(lower, jnp.log1p(-key), 1, 0)
+    cumul = sums(lower, jnp.log1p(-key))
     grow = jnp.exp(cumul)
     shrink = jnp.exp(-cumul)
     end = grow[size - 1 :, :]
@@ -336,7 +332,7 @@
         key_t_grad = product(value, back, 1, 0)
         key_grad = key_d_grad * shrink + (p["tail"] * end * shrink) * key_t_grad
         change = query_d * query_d_grad - key_d * key_d_grad - key_t * key_t_grad
-        through = exact_product(upper, change, 1, 0) + through_ref[:, cols]
+        through = sums(upper, change) + through_ref[:, cols]
         key_total = key_grad - through / (1.0 - key)
         new_back = back * keep + product(mixed_grad, query_d * p["linked"], 0, 0)
         back_ref[h] = new_back
@@ -676,7 +672,7 @@
     return pl.pallas_call(
         functools.partial(gated_grad_kernel, places, half),
         grid=(1,),
-        in_specs=[block(*piece.shape) for piece in pieces] + [block(my_width, width)],
+        in_specs=[block(*piece.shape) for piece in pieces] + [block(*out_rows.shape)],
         out_specs=[block(tokens, width), block(tokens, my_width)],
         out_shape=[
             jax.ShapeDtypeStruct((tokens, width), bf16),
@@ -857,31 +853,28 @@
     mix_weights = [query_weight, forget_weight, input_weight, output_gate_weight]
     mix_pieces = swap_seq(column_pieces(mix_weights))
     mix_cols = gather_dp(mix_pieces.reshape(rank_rows, 4 * my_width))
-    ffn_width = 2 * ffn_gate_weight.shape[1] // ranks
-    ffn_pieces = column_pieces([after(ffn_gate_weight, mix_pieces), ffn_up_weight], True)
-    down_pieces = column_pieces([ffn_down_weight])
-    ffn_pieces = swap_seq(jnp.concatenate((ffn_pieces, down_pieces), axis=2))
-    x_pieces, places = gather_seq(after(x_low, ffn_pieces))
+    out_rows = gather_dp(lax.ppermute(output_weight, ("dp", "seq"), row_route()))
+    x_pieces, places = gather_seq(after(x_low, mix_pieces))
     vectors = jnp.stack((mix_gain, bound_logit, ffn_gain), axis=1)
-    vectors = gather_small(gather_small(vectors, "seq"), "dp").astype(f32)
+    vectors = gather_small(gather_small(vectors, "seq"), "dp")
+    segments = gather_small(segment_ids[0], "seq")
+    vectors = vectors.astype(f32)
     gain_in, logit, gain_mid = (vectors[:, 0], vectors[:, 1], vectors[:, 2])
     gain_in, gain_mid = (gain_in[None, :], gain_mid[None, :])
-    segments = gather_small(segment_ids[0], "seq")
     table = slot_table()
     bound = jax.nn.sigmoid(-lax.dynamic_slice_in_dim(logit, rank * my_width, my_width))[None, :]
     normed_in, in_mine, in_theirs = assemble(
         (x_pieces, places), core, rank_rows, after(gain_in, segments, bound)
     )
-    out_piece = lax.ppermute(output_weight, ("dp", "seq"), row_route())
-    out_rows = gather_dp(after(out_piece, normed_in))
-    ffn_cols = gather_dp(after(ffn_pieces[:, :, :ffn_width].reshape(rank_rows, ffn_width), out_piece))
-    down_pieces = ffn_pieces[:, :, ffn_width:].reshape(rank_rows, ffn_width // 2)
-
-    pre = dense(normed_in, mix_cols, f32, parts=4)
-    down_cols = gather_dp(after(down_pieces, pre))
+    ffn_pieces = swap_seq(column_pieces([after(ffn_gate_weight, normed_in, out_rows), ffn_up_weight], True))
+    ffn_cols = gather_dp(ffn_pieces.reshape(rank_rows, ffn_pieces.shape[2]))
+    down_pieces = swap_seq(column_pieces([after(ffn_down_weight, ffn_pieces)]))
+    down_cols = gather_dp(down_pieces.reshape(rank_rows, down_pieces.shape[2]))
+
+    pre = dense(after(normed_in, down_pieces), mix_cols, f32, parts=4)
     mixed, states = recurrence_forward(segments, table, pre, bound)
-    gated, partials = gate_out(mixed, pre, out_rows, half)
-    cotangent = gather_seq(after(cotangent_low, normed_in))
+    cotangent = gather_seq(after(cotangent_low, down_pieces))
+    gated, partials = gate_out(after(mixed, *cotangent[0][:3]), pre, out_rows, half)
     branch_parts = scatter_seq(partials, half)
     cotangent_all, cotangent_mine, cotangent_theirs = assemble(cotangent, core, rank_rows)
     resid, normed_low = combine(

time: 659 us -> 647 us (0.982)
  blocking collectives: 17 us -> 39.4 us
  waiting for transfers between devices: 229 us -> 209 us
  local copies, waits for them, and re-layouts: 51.8 us -> 44.5 us
    all_to_all x1 -> x2, blocking collectives: 17 us -> 39.4 us  [swap_seq(): lax.all_to_all(pieces, 'seq', split_axis=0, concat_axis=0, tiled=True)]
    all_gather x4, waiting for transfers between devices: 24.1 us -> 4.48 us  [gather_dp(): return lax.all_gather(block, 'dp', axis=0, tiled=True)]
    ppermute x43, waiting for transfers between devices: 189 us -> 179 us  [flip(): lax.ppermute(block, axis, [(i, i ^ bits) for i in range(lax.axis_size(axi...]
    all_to_all x6, waiting for transfers between devices: 13.5 us -> 21.4 us  [swap_seq(): lax.all_to_all(pieces, 'seq', split_axis=0, concat_axis=0, tiled=True)]
    unnamed x128 -> x126, local copies, waits for them, and re-layouts: 39.1 us -> 36.4 us
  transfers between devices with their start and end apart: 58 -> 58, of which waited for: 27 -> 28; matrix products, arithmetic and copies ran while one was open for 4% -> 3% of each run, Pallas kernels for 35% -> 36%
where the time goes in v4:
time: 647 us; the launch traced here: 637 us
  Pallas kernels  230 us (36%)
  waiting for transfers between devices  209 us (32%)
  starting transfers between devices  88.1 us (14%)
  local copies, waits for them, and re-layouts  44.5 us (7%)
  blocking collectives  39.4 us (6%)
  between operations  15.2 us (2%)
  other arithmetic  10.4 us (2%)
    ppermute x43, waiting for transfers between devices, flip(): lax.ppermute(block, axis, [(i, i ^ bits) for i in range(lax.axis_size(axi...  179 us
    pallas_call x6, Pallas kernels, dense(): pl.pallas_call(functools.partial(product_kernel, left_dim), grid=(width /...  54.9 us
    ppermute x43, starting transfers between devices, flip(): lax.ppermute(block, axis, [(i, i ^ bits) for i in range(lax.axis_size(axi...  51.9 us
    all_to_all x2, blocking collectives, swap_seq(): lax.all_to_all(pieces, 'seq', split_axis=0, concat_axis=0, tiled=True)  39.4 us
    unnamed x126, local copies, waits for them, and re-layouts  36.4 us
    pallas_call x1, Pallas kernels, recurrence_backward(): pl.pallas_call(backward_kernel, grid_spec=pltpu.PrefetchScalarGridSpec(nu...  27.3 us
    pallas_call x2, Pallas kernels, exchanged_product(): pl.pallas_call(functools.partial(ordered_kernel, half), grid_spec=pltpu.P...  25.9 us
    all_to_all x6, starting transfers between devices, swap_seq(): lax.all_to_all(pieces, 'seq', split_axis=0, concat_axis=0, tiled=True)  24.1 us
  transfers between devices with their start and end apart: 58, of which 28 were waited for; matrix products, arithmetic and copies ran while one was open for 3% of the time, Pallas kernels for 36%

profile of v4, /device:TPU:1, one launch (start us, length us, event | category | flops | bytes accessed | tf_op | source)
XLA Modules:
  0.0 637.0 jit_solution(17314303288374713617)
XLA Ops:
  21.5 20.4 %all_to_all.40 = bf16[4,64,2048]{2,1,0:T(8,128)(2,1)} all-to-all(bf16[4,64,2048]{2,1,0:T(8,128)(2,1)S(1)} %column_pieces.3), channel_id=1, replica_groups=mesh['dp'=8,'seq'=4] {'seq'}, dimensions={0} | all-to-all | bytes 2097152 | tf_op jit(solution)/shard_map/all_to_all | solution.py:110
  54.9 23.0 %collective-permute-done.1 = s32[512]{0:T(512)S(1)} collective-permute-done((s32[512]{0:T(512)S(1)}, s32[512]{0:T(512)S(1)}, u32[]{:S(2)}, u32[]{:S(2)}) %collective-permute-start.1) | collective-permute-done | bytes 2080 | tf_op jit(solution)/shard_map/ppermute | solution.py:26
  82.6 8.9 %collective-permute-done.4.refs_3_ = bf16[128,2048]{1,0:T(8,128)(2,1)S(1)} collective-permute-done((bf16[128,2048]{1,0:T(8,128)(2,1)S(1)}, bf16[128,2048]{1,0:T(8,128)(2,1)S(1)}, u32[]{:S(2)}, u32[]{:S(2)}) %collective-permute-start.4) | collective-permute-done | bytes 524320 | tf_op jit(solution)/shard_map/ppermute | solution.py:26
  98.5 19.0 %all_to_all.41 = bf16[4,64,2816]{2,1,0:T(8,128)(2,1)} all-to-all(bf16[4,64,2816]{2,1,0:T(8,128)(2,1)S(1)} %column_pieces.4), channel_id=1, replica_groups=mesh['dp'=8,'seq'=4] {'seq'}, dimensions={0} | all-to-all | bytes 2883584 | tf_op jit(solution)/shard_map/all_to_all | solution.py:110
  138.4 12.9 %dense.6.pre_ref.outgate_pre_ref = f32[1024,2048]{1,0:T(8,128)} custom-call(bf16[1024,2048]{1,0:T(8,128)(2,1)S(1)} %copy-done.34, bf16[2048,2048]{1,0:T(8,128)(2,1)} %all-gather.7.cloned.1.call-done.refs_1_.weight_ref), custom_call_target="tpu_custom_call" | custom-call | flops 12884901888 | tf_op jit(solution)/shard_map/dense/pallas_call | solution.py:452
  151.3 12.1 %recurrence_forward.1 = (f32[1024,512]{1,0:T(8,128)S(1)}, f32[8,4,128,128]{3,2,1,0:T(8,128)S(1)}) custom-call(s32[1024]{0:T(1024)S(1)} %pad_add_fusion.seg_ref, s32[8]{0:T(128)S(1)} %reshape.123.slot_ref, s32[1024,1]{1,0:T(8,128)S(1)} %copy-done.26, s32[1,1024]{1,0:T(1,128)S(1)} %bitcast.49, f32[1024,2048]{1,0:T(8,128)} %dense.6.pre_ref.outgate_pre_ref, ...), custom_call_target="tpu_custom_call" | custom-call | flops 21474836480 | tf_op jit(solution)/shard_map/recurrence_forward/pallas_call | solution.py:355
  164.8 8.0 %gate_out.1 = (bf16[1024,512]{1,0:T(8,128)(2,1)S(1)}, bf16[256,2048]{1,0:T(8,128)(2,1)S(1)}, bf16[256,2048]{1,0:T(8,128)(2,1)S(1)}, f32[512,2048]{1,0:T(8,128)}) custom-call(f32[1024,512]{1,0:T(8,128)S(1)} %get-tuple-element.81.mixed_ref, f32[1024,2048]{1,0:T(8,128)} %dense.6.pre_ref.outgate_pre_ref, ...), custom_call_target="tpu_custom_call" | custom-call | flops 3221225472 | bytes 33554432 | tf_op jit(solution)/shard_map/gate_out/pallas_call | solution.py:644
  178.0 20.1 %collective-permute-done.14.refs_1_ = bf16[256,2048]{1,0:T(8,128)(2,1)S(1)} collective-permute-done((bf16[256,2048]{1,0:T(8,128)(2,1)S(1)}, bf16[256,2048]{1,0:T(8,128)(2,1)S(1)}, u32[]{:S(2)}, u32[]{:S(2)}) %collective-permute-start.14) | collective-permute-done | bytes 1048608 | tf_op jit(solution)/shard_map/ppermute | solution.py:26
  202.6 7.0 %collective-permute-done.18.refs_3_ = bf16[128,2048]{1,0:T(8,128)(2,1)S(1)} collective-permute-done((bf16[128,2048]{1,0:T(8,128)(2,1)S(1)}, bf16[128,2048]{1,0:T(8,128)(2,1)S(1)}, u32[]{:S(2)}, u32[]{:S(2)}) %collective-permute-start.18) | collective-permute-done | bytes 524320 | tf_op jit(solution)/shard_map/ppermute | solution.py:26
  226.5 20.2 %collective-permute-done.20.refs_1_ = bf16[256,2048]{1,0:T(8,128)(2,1)S(1)} collective-permute-done((bf16[256,2048]{1,0:T(8,128)(2,1)S(1)}, bf16[256,2048]{1,0:T(8,128)(2,1)S(1)}, u32[]{:S(2)}, u32[]{:S(2)}) %collective-permute-start.20) | collective-permute-done | bytes 1048608 | tf_op jit(solution)/shard_map/ppermute | solution.py:26
  251.1 8.8 %collective-permute-done.22.refs_3_ = bf16[128,2048]{1,0:T(8,128)(2,1)S(1)} collective-permute-done((bf16[128,2048]{1,0:T(8,128)(2,1)S(1)}, bf16[128,2048]{1,0:T(8,128)(2,1)S(1)}, u32[]{:S(2)}, u32[]{:S(2)}) %collective-permute-start.22) | collective-permute-done | bytes 524320 | tf_op jit(solution)/shard_map/ppermute | solution.py:26
  267.2 19.9 %ffn_forward.1 = (f32[1024,2816]{1,0:T(8,128)}, bf16[1024,1408]{1,0:T(8,128)(2,1)}, bf16[1024,2048]{1,0:T(8,128)(2,1)}) custom-call(bf16[256,2048]{1,0:T(8,128)(2,1)S(1)} %copy-done.42, bf16[256,2048]{1,0:T(8,128)(2,1)S(1)} %collective-permute-done.20.refs_1_, bf16[256,2048]{1,0:T(8,128)(2,1)S(1)} %copy-done.29, bf16[128,2048]{1,0:T(8,128)(2,1)S(1)} %copy-done.44, ...), custom_call_target="tpu_custom_call" | custom-call | flops 17716740096 | tf_op jit(solution)/shard_map/ffn_forward/pallas_call | solution.py:711
  312.9 13.5 %ffn_backward.1.left_ref.refs_1_ = bf16[1024,2816]{1,0:T(8,128)(2,1)} custom-call(bf16[1024,2048]{1,0:T(8,128)(2,1)S(1)} %copy-done.33, bf16[2048,1408]{1,0:T(8,128)(2,1)} %all-gather.11.cloned.1.call-done.weight_ref, f32[1024,2816]{1,0:T(8,128)} %get-tuple-element.92.both_ref), custom_call_target="tpu_custom_call" | custom-call | flops 11811160064 | tf_op jit(solution)/shard_map/ffn_backward/pallas_call | solution.py:755
  326.4 17.8 %partial_product.1 = (bf16[256,2048]{1,0:T(8,128)(2,1)}, bf16[256,2048]{1,0:T(8,128)(2,1)}, f32[512,2048]{1,0:T(8,128)}) custom-call(bf16[1024,2816]{1,0:T(8,128)(2,1)} %ffn_backward.1.left_ref.refs_1_, bf16[2048,2816]{1,0:T(8,128)(2,1)} %all-gather.9.cloned.1.call-done.refs_5_.refs_0_), custom_call_target="tpu_custom_call" | custom-call | flops 17716740096 | tf_op jit(solution)/shard_map/partial_product/pallas_call | solution.py:614
  344.8 17.9 %dense.9 = bf16[2048,2816]{1,0:T(8,128)(2,1)} custom-call(bf16[1024,2048]{1,0:T(8,128)(2,1)S(1)} %copy-done.49, bf16[1024,2816]{1,0:T(8,128)(2,1)} %ffn_backward.1.left_ref.refs_1_), custom_call_target="tpu_custom_call" | custom-call | flops 17716740096 | tf_op jit(solution)/shard_map/dense/pallas_call | solution.py:452
  372.5 10.9 %collective-permute-done.27.refs_3_ = bf16[128,2048]{1,0:T(8,128)(2,1)S(1)} collective-permute-done((bf16[128,2048]{1,0:T(8,128)(2,1)S(1)}, bf16[128,2048]{1,0:T(8,128)(2,1)S(1)}, u32[]{:S(2)}, u32[]{:S(2)}) %collective-permute-start.27) | collective-permute-done | bytes 524320 | tf_op jit(solution)/shard_map/ppermute | solution.py:26
  390.3 20.5 %collective-permute-done.29.refs_1_ = bf16[256,2048]{1,0:T(8,128)(2,1)S(1)} collective-permute-done((bf16[256,2048]{1,0:T(8,128)(2,1)S(1)}, bf16[256,2048]{1,0:T(8,128)(2,1)S(1)}, u32[]{:S(2)}, u32[]{:S(2)}) %collective-permute-start.29) | collective-permute-done | bytes 1048608 | tf_op jit(solution)/shard_map/ppermute | solution.py:26
  412.8 11.9 %exchanged_product.2 = bf16[1024,2048]{1,0:T(8,128)(2,1)} custom-call(s32[8]{0:T(128)S(1)} %multiply_add_fusion.places_ref, bf16[1024,1408]{1,0:T(8,128)(2,1)S(1)} %copy-done.47, bf16[2048,1408]{1,0:T(8,128)(2,1)} %all-gather.11.cloned.1.call-done.weight_ref), custom_call_target="tpu_custom_call" | custom-call | flops 8858370048 | tf_op jit(solution)/shard_map/exchanged_product/pallas_call | solution.py:592
  438.8 27.3 %recurrence_backward.1 = (bf16[1024,2048]{1,0:T(8,128)(2,1)}, f32[1,512]{1,0:T(1,128)S(1)}) custom-call(s32[1024]{0:T(1024)S(1)} %pad_add_fusion.seg_ref, s32[8]{0:T(128)S(1)} %reshape.123.slot_ref, s32[1024,1]{1,0:T(8,128)S(1)} %copy-done.27, s32[1,1024]{1,0:T(1,128)S(1)} %bitcast.50, f32[1024,2048]{1,0:T(8,128)} %dense.6.pre_ref.outgate_pre_ref, ...), custom_call_target="tpu_custom_call" | custom-call | flops 41607495680 | tf_op jit(solution)/shard_map/recurrence_backward/pallas_call | solution.py:388
  466.1 7.9 %dense.10 = bf16[1024,2048]{1,0:T(8,128)(2,1)} custom-call(bf16[1024,1024]{1,0:T(8,128)(2,1)S(1)} %copy-done.36, bf16[1024,2048]{1,0:T(8,128)(2,1)} %get-tuple-element.112.refs_1_.right_ref.left_ref), custom_call_target="tpu_custom_call" | custom-call | flops 6442450944 | tf_op jit(solution)/shard_map/dense/pallas_call | solution.py:452
  491.4 9.0 %mixer_sums.1 = bf16[1024,2560]{1,0:T(8,128)(2,1)} custom-call(s32[1]{0:T(128)} %bitcast.4.core_ref, bf16[1024,1024]{1,0:T(8,128)(2,1)S(1)} %copy-done.35, bf16[1024,2048]{1,0:T(8,128)(2,1)} %get-tuple-element.112.refs_1_.right_ref.left_ref, bf16[1024,2048]{1,0:T(8,128)(2,1)} %collective-permute-done.33.theirs_ref, bf16[4,2,64,2048]{3,2,1,0:T(8,128)(2,1)S(1)} %bitcast.47, ...), custom_call_target="tpu_custom_call" | custom-call | flops 6442450944 | tf_op jit(solution)/shard_map/mixer_sums/pallas_call | solution.py:489
  504.0 9.9 %all-to-all-done.4.refs_0_ = bf16[4,64,1408]{2,1,0:T(8,128)(2,1)S(1)} async-done(((bf16[4,64,1408]{2,1,0:T(8,128)(2,1)}), bf16[4,64,1408]{2,1,0:T(8,128)(2,1)S(1)}, u32[]{:S(2)}, u32[]{:S(2)}) %all-to-all-start.4) | async-done | bytes 720928 | tf_op jit(solution)/shard_map/all_to_all | solution.py:110
  518.3 14.0 %exchanged_product.3 = bf16[1024,2048]{1,0:T(8,128)(2,1)S(1)} custom-call(s32[8]{0:T(128)S(1)} %multiply_add_fusion.places_ref, bf16[1024,2048]{1,0:T(8,128)(2,1)} %get-tuple-element.112.refs_1_.right_ref.left_ref, bf16[2048,2048]{1,0:T(8,128)(2,1)} %all-gather.7.cloned.1.call-done.refs_1_.weight_ref), custom_call_target="tpu_custom_call" | custom-call | flops 12884901888 | tf_op jit(solution)/shard_map/exchanged_product/pallas_call | solution.py:592
  554.9 33.1 %collective-permute-done.42 = f32[512]{0:T(512)S(1)} collective-permute-done((f32[512]{0:T(512)S(1)}, f32[512]{0:T(512)S(1)}, u32[]{:S(2)}, u32[]{:S(2)}) %collective-permute-start.42) | collective-permute-done | bytes 2080 | tf_op jit(solution)/shard_map/ppermute | solution.py:26
  (304 shorter events, 247.7 us)
Async XLA Ops:
  7.2 90.8 %all-gather.5.cloned.1.call-start = ((), (), s32[]{:S(2)}) async-start(), calls=%async_computation.11 | async-start | bytes 2359296 | tf_op jit(solution)/shard_map/all_gather | solution.py:114
  17.4 118.9 %all-gather.7.cloned.1.call-start = ((), (), s32[]{:S(2)}) async-start(), calls=%async_computation.12 | async-start | bytes 9437184 | tf_op jit(solution)/shard_map/all_gather | solution.py:114
  42.0 220.7 %all-gather.9.cloned.1.call-start = ((), (), s32[]{:S(2)}) async-start(), calls=%async_computation.13 | async-start | bytes 12976128 | tf_op jit(solution)/shard_map/all_gather | solution.py:114
  52.6 26.6 %collective-permute-start.2 = (bf16[256,2048]{1,0:T(8,128)(2,1)S(1)}, bf16[256,2048]{1,0:T(8,128)(2,1)S(1)}, u32[]{:S(2)}, u32[]{:S(2)}) collective-permute-start(bf16[256,2048]{1,0:T(8,128)(2,1)S(1)} %bitcast.36), channel_id=1, source_target_pairs={{0,1},{1,0},{2,3},{3,2},{4,5},{5,4},{6,7},{7,6},{8,9},{9,8},{10,11... | collective-permute-start | bytes 3145736 | tf_op jit(solution)/shard_map/ppermute | solution.py:26
  53.3 26.4 %collective-permute-start.3 = (bf16[256,2048]{1,0:T(8,128)(2,1)S(1)}, bf16[256,2048]{1,0:T(8,128)(2,1)S(1)}, u32[]{:S(2)}, u32[]{:S(2)}) collective-permute-start(bf16[256,2048]{1,0:T(8,128)(2,1)S(1)} %bitcast.37), channel_id=1, source_target_pairs={{0,2},{1,3},{2,0},{3,1},{4,6},{5,7},{6,4},{7,5},{8,10},{9,11},{10,... | collective-permute-start | bytes 3145736 | tf_op jit(solution)/shard_map/ppermute | solution.py:26
  53.6 24.3 %collective-permute-start.1 = (s32[512]{0:T(512)S(1)}, s32[512]{0:T(512)S(1)}, u32[]{:S(2)}, u32[]{:S(2)}) collective-permute-start(s32[512]{0:T(512)S(1)} %pad_add_fusion.1), channel_id=1, source_target_pairs={{0,2},{1,3},{2,0},{3,1},{4,6},{5,7},{6,4},{7,5},{8,10},{9,11},{10,... | collective-permute-start | bytes 6152 | tf_op jit(solution)/shard_map/ppermute | solution.py:26
  122.5 188.1 %all-gather.11.cloned.1.call-start = ((), (), s32[]{:S(2)}) async-start(), calls=%async_computation.14 | async-start | bytes 6488064 | tf_op jit(solution)/shard_map/all_gather | solution.py:114
  130.3 34.5 %collective-permute-start.12 = (bf16[256,2048]{1,0:T(8,128)(2,1)S(1)}, bf16[256,2048]{1,0:T(8,128)(2,1)S(1)}, u32[]{:S(2)}, u32[]{:S(2)}) collective-permute-start(bf16[256,2048]{1,0:T(8,128)(2,1)S(1)} %bitcast.41), channel_id=1, source_target_pairs={{0,1},{1,0},{2,3},{3,2},{4,5},{5,4},{6,7},{7,6},{8,9},{9,8},{10,11... | collective-permute-start | bytes 3145736 | tf_op jit(solution)/shard_map/ppermute | solution.py:26
  131.4 33.4 %collective-permute-start.13 = (bf16[256,2048]{1,0:T(8,128)(2,1)S(1)}, bf16[256,2048]{1,0:T(8,128)(2,1)}, u32[]{:S(2)}, u32[]{:S(2)}) collective-permute-start(bf16[256,2048]{1,0:T(8,128)(2,1)S(1)} %bitcast.42), channel_id=1, source_target_pairs={{0,2},{1,3},{2,0},{3,1},{4,6},{5,7},{6,4},{7,5},{8,10},{9,11},{10,... | collective-permute-start | bytes 3145736 | tf_op jit(solution)/shard_map/ppermute | solution.py:26
  131.7 231.2 %reduce-scatter.4.cloned.1.call-start = ((), (), s32[]{:S(2)}) async-start(), calls=%async_computation.15 | async-start | bytes 3604480 | tf_op jit(solution)/shard_map/reduce_scatter | solution.py:119
  173.8 24.3 %collective-permute-start.14 = (bf16[256,2048]{1,0:T(8,128)(2,1)S(1)}, bf16[256,2048]{1,0:T(8,128)(2,1)S(1)}, u32[]{:S(2)}, u32[]{:S(2)}) collective-permute-start(bf16[256,2048]{1,0:T(8,128)(2,1)S(1)} %get-tuple-element.83), channel_id=1, source_target_pairs={{0,1},{1,0},{2,3},{3,2},{4,5},{5,4},{6,7},{7,6},{8,9},{9,8},{10,11... | collective-permute-start | bytes 3145736 | tf_op jit(solution)/shard_map/ppermute | solution.py:26
  174.9 23.5 %collective-permute-start.15 = (bf16[256,2048]{1,0:T(8,128)(2,1)S(1)}, bf16[256,2048]{1,0:T(8,128)(2,1)S(1)}, u32[]{:S(2)}, u32[]{:S(2)}) collective-permute-start(bf16[256,2048]{1,0:T(8,128)(2,1)S(1)} %get-tuple-element.84), channel_id=1, source_target_pairs={{0,2},{1,3},{2,0},{3,1},{4,6},{5,7},{6,4},{7,5},{8,10},{9,11},{10,... | collective-permute-start | bytes 3145736 | tf_op jit(solution)/shard_map/ppermute | solution.py:26
  176.1 33.5 %collective-permute-start.18 = (bf16[128,2048]{1,0:T(8,128)(2,1)S(1)}, bf16[128,2048]{1,0:T(8,128)(2,1)S(1)}, u32[]{:S(2)}, u32[]{:S(2)}) collective-permute-start(bf16[128,2048]{1,0:T(8,128)(2,1)S(1)} %slice.92), channel_id=1, source_target_pairs={{0,2},{1,3},{2,0},{3,1},{4,6},{5,7},{6,4},{7,5},{8,10},{9,11},{10,... | collective-permute-start | bytes 1572872 | tf_op jit(solution)/shard_map/ppermute | solution.py:26
  177.6 32.0 %collective-permute-start.19 = (bf16[128,2048]{1,0:T(8,128)(2,1)S(1)}, bf16[128,2048]{1,0:T(8,128)(2,1)S(1)}, u32[]{:S(2)}, u32[]{:S(2)}) collective-permute-start(bf16[128,2048]{1,0:T(8,128)(2,1)S(1)} %slice.93), channel_id=1, source_target_pairs={{0,1},{1,0},{2,3},{3,2},{4,5},{5,4},{6,7},{7,6},{8,9},{9,8},{10,11... | collective-permute-start | bytes 1572872 | tf_op jit(solution)/shard_map/ppermute | solution.py:26
  225.1 24.7 %collective-permute-start.21 = (bf16[256,2048]{1,0:T(8,128)(2,1)S(1)}, bf16[256,2048]{1,0:T(8,128)(2,1)S(1)}, u32[]{:S(2)}, u32[]{:S(2)}) collective-permute-start(bf16[256,2048]{1,0:T(8,128)(2,1)S(1)} %get-tuple-element.87.refs_0_), channel_id=1, source_target_pairs={{0,2},{1,3},{2,0},{3,1},{4,6},{5,7},{6,4},{7,5},{8,10},{9,11},{10,... | collective-permute-start | bytes 3145736 | tf_op jit(solution)/shard_map/ppermute | solution.py:26
  310.4 204.4 %reduce-scatter.6.cloned.1.call-start = ((), (), s32[]{:S(2)}) async-start(), calls=%async_computation.16 | async-start | bytes 12976128 | tf_op jit(solution)/shard_map/reduce_scatter | solution.py:895
  344.2 24.8 %collective-permute-start.25 = (bf16[256,2048]{1,0:T(8,128)(2,1)}, bf16[256,2048]{1,0:T(8,128)(2,1)S(1)}, u32[]{:S(2)}, u32[]{:S(2)}) collective-permute-start(bf16[256,2048]{1,0:T(8,128)(2,1)} %get-tuple-element.95), channel_id=1, source_target_pairs={{0,1},{1,0},{2,3},{3,2},{4,5},{5,4},{6,7},{7,6},{8,9},{9,8},{10,11... | collective-permute-start | bytes 3145736 | tf_op jit(solution)/shard_map/ppermute | solution.py:26
  344.2 24.8 %collective-permute-start.26 = (bf16[256,2048]{1,0:T(8,128)(2,1)}, bf16[256,2048]{1,0:T(8,128)(2,1)}, u32[]{:S(2)}, u32[]{:S(2)}) collective-permute-start(bf16[256,2048]{1,0:T(8,128)(2,1)} %get-tuple-element.98), channel_id=1, source_target_pairs={{0,2},{1,3},{2,0},{3,1},{4,6},{5,7},{6,4},{7,5},{8,10},{9,11},{10,... | collective-permute-start | bytes 3145736 | tf_op jit(solution)/shard_map/ppermute | solution.py:26
  431.1 51.9 %all-to-all-start.3 = ((bf16[4,256,2048]{2,1,0:T(8,128)(2,1)}), bf16[4,256,2048]{2,1,0:T(8,128)(2,1)}, u32[]{:S(2)}, u32[]{:S(2)}) async-start(bf16[4,256,2048]{2,1,0:T(8,128)(2,1)} %bitcast.54), calls=%async_computation.4 | async-start | bytes 8388608 | tf_op jit(solution)/shard_map/all_to_all | solution.py:110
  436.1 157.0 %reduce-scatter.8.cloned.1.call-start = ((), (), s32[]{:S(2)}) async-start(), calls=%async_computation.17 | async-start | bytes 6553600 | tf_op jit(solution)/shard_map/reduce_scatter | solution.py:119
  536.8 56.3 %all-to-all-start.6 = ((bf16[4,256,2048]{2,1,0:T(8,128)(2,1)}), bf16[4,256,2048]{2,1,0:T(8,128)(2,1)}, u32[]{:S(2)}, u32[]{:S(2)}) async-start(bf16[4,256,2048]{2,1,0:T(8,128)(2,1)} %bitcast.45), calls=%async_computation.8 | async-start | bytes 8388608 | tf_op jit(solution)/shard_map/all_to_all | solution.py:110
  553.2 34.8 %collective-permute-start.42 = (f32[512]{0:T(512)S(1)}, f32[512]{0:T(512)S(1)}, u32[]{:S(2)}, u32[]{:S(2)}) collective-permute-start(f32[512]{0:T(512)S(1)} %add_add_fusion), channel_id=1, source_target_pairs={{0,1},{1,0},{2,3},{3,2},{4,5},{5,4},{6,7},{7,6},{8,9},{9,8},{10,11... | collective-permute-start | bytes 6152 | tf_op jit(solution)/shard_map/ppermute | solution.py:26
  595.6 31.4 %all-to-all-start.7 = ((bf16[4,64,2048]{2,1,0:T(8,128)(2,1)}), bf16[4,64,2048]{2,1,0:T(8,128)(2,1)S(1)}, u32[]{:S(2)}, u32[]{:S(2)}) async-start(bf16[4,64,2048]{2,1,0:T(8,128)(2,1)} %bitcast.56), calls=%async_computation.10 | async-start | bytes 2097152 | tf_op jit(solution)/shard_map/all_to_all | solution.py:110
  601.5 23.7 %collective-permute-start.44 = (bf16[4,64,512]{2,1,0:T(8,128)(2,1)}, bf16[4,64,512]{2,1,0:T(8,128)(2,1)}, u32[]{:S(2)}, u32[]{:S(2)}) collective-permute-start(bf16[4,64,512]{2,1,0:T(8,128)(2,1)} %bitcast.27), channel_id=1, source_target_pairs={{0,0},{4,1},{8,2},{12,3},{16,4},{20,5},{24,6},{28,7},{1,8},{5,9},{... | collective-permute-start | bytes 786440 | tf_op jit(solution)/shard_map/ppermute | solution.py:932
  (97 other events, 948.9 us)
Sparse Core Ops, SparseCore 0:
  17.5 35.1 all-gather.4
  54.3 81.9 all-gather.6
  137.9 106.4 all-gather.8
  246.5 58.6 all-gather.10
  310.5 52.3 reduce-scatter.3
  369.1 115.1 reduce-scatter.5
  500.6 90.9 reduce-scatter.7

commit v5 on v4

--- a/solution.py
+++ b/solution.py
@@ -585,7 +585,7 @@
         out_ref[pl.ds(to, half), :] = total[slot * half : (slot + 1) * half, :]
 
 
-def exchanged_product(left, weight, places, half, columns=256):
+def exchanged_product(left, weight, places, half, columns=512):
     tokens, depth = left.shape
     width = weight.shape[0]
     ranks = lax.axis_size("seq")
@@ -605,7 +605,7 @@
     return partial.reshape(ranks, 2 * half, width)
 
 
-def partial_product(left, weights, widths, half, columns=256):
+def partial_product(left, weights, widths, half, columns=512):
     tokens, depth = left.shape
     width = weights[0].shape[0]
     layout = partial_layout(tokens)
@@ -730,15 +730,18 @@
 
 
 def ffn_backward_kernel(cotangent_ref, weight_ref, both_ref, grads_ref):
-    hidden_grad = matmul(cotangent_ref[...], weight_ref[...])
-    for j in range(hidden_grad.shape[1] // LANES):
-        grad = hidden_grad[:, j * LANES : (j + 1) * LANES]
-        gate = both_ref[:, 2 * j * LANES : (2 * j + 1) * LANES]
-        up = both_ref[:, (2 * j + 1) * LANES : (2 * j + 2) * LANES]
-        sig = jax.nn.sigmoid(gate)
-        slope = sig * (1.0 + gate * (1.0 - sig))
-        grads_ref[:, 2 * j * LANES : (2 * j + 1) * LANES] = (grad * up * slope).astype(bf16)
-        grads_ref[:, (2 * j + 1) * LANES : (2 * j + 2) * LANES] = (grad * (gate * sig)).astype(bf16)
+    width = weight_ref.shape[1]
+    for first in range(0, width, 2 * LANES):
+        last = min(first + 2 * LANES, width)
+        hidden_grad = matmul(cotangent_ref[...], weight_ref[:, first:last])
+        for at in range(first, last, LANES):
+            grad = hidden_grad[:, at - first : at - first + LANES]
+            gate = both_ref[:, 2 * at : 2 * at + LANES]
+            up = both_ref[:, 2 * at + LANES : 2 * at + 2 * LANES]
+            sig = jax.nn.sigmoid(gate)
+            slope = sig * (1.0 + gate * (1.0 - sig))
+            grads_ref[:, 2 * at : 2 * at + LANES] = (grad * up * slope).astype(bf16)
+            grads_ref[:, 2 * at + LANES : 2 * at + 2 * LANES] = (grad * (gate * sig)).astype(bf16)
 
 
 def ffn_backward(cotangent_all, down_cols, both):
@@ -751,16 +754,16 @@
         gate_grad = hidden_grad * up * (sig * (1.0 + gate * (1.0 - sig)))
         up_grad = hidden_grad * (gate * sig)
         return jnp.concatenate((gate_grad, up_grad), axis=1).astype(bf16)
-    size = 2 * LANES
+    rows = tokens // 2
     return pl.pallas_call(
         ffn_backward_kernel,
-        grid=(pl.cdiv(mine, size),),
+        grid=(2,),
         in_specs=[
-            block(tokens, width),
-            block(width, size, at=lambda j: (0, j)),
-            block(tokens, 2 * size, at=lambda j: (0, j)),
+            block(rows, width, at=lambda i: (i, 0)),
+            block(width, mine),
+            block(rows, 2 * mine, at=lambda i: (i, 0)),
         ],
-        out_specs=block(tokens, 2 * size, at=lambda j: (0, j)),
+        out_specs=block(rows, 2 * mine, at=lambda i: (i, 0)),
         out_shape=jax.ShapeDtypeStruct((tokens, 2 * mine), bf16),
         compiler_params=vmem,
         cost_estimate=cost(4 * tokens * width * mine),
@@ -912,11 +915,11 @@
     mix_mine = scatter_dp(mix_sum)
     down_back = swap_columns(after(down_mine, mix_sum))
     ffn_back = swap_columns(after(ffn_mine, down_back))
-    in_partial = exchanged_product(after(mix_right, mix_sum), mix_cols, row_place, half)
+    (block_output,) = combine(
+        lambda total, resid: (resid + total,), (out_parts,), (after(resid, mix_sum),), (bf16,), half
+    )
+    in_partial = exchanged_product(after(mix_right, block_output), mix_cols, row_place, half)
     in_parts = swap_seq(after(in_partial, ffn_back))
-    (block_output,) = combine(
-        lambda total, resid: (resid + total,), (out_parts,), (after(resid, in_partial),), (bf16,), half
-    )
     (ffn_gate_weight_grad, ffn_up_weight_grad), ffn_sums = return_columns(
         after(ffn_back, in_partial), [ffn_gate_weight, ffn_up_weight], True
     )

time: 647 us -> 645 us (level)
    unnamed x126 -> x118, local copies, waits for them, and re-layouts: 36.4 us -> 33.3 us
  transfers between devices with their start and end apart: 58 -> 58, of which waited for: 28 -> 31; matrix products, arithmetic and copies ran while one was open for 3% -> 3% of each run, Pallas kernels for 36% -> 36%
where the time goes in v5:
time: 645 us; the launch traced here: 633 us
  Pallas kernels  230 us (36%)
  waiting for transfers between devices  209 us (32%)
  starting transfers between devices  87.8 us (14%)
  local copies, waits for them, and re-layouts  41.2 us (6%)
  blocking collectives  39.4 us (6%)
  between operations  15 us (2%)
  other arithmetic  10.4 us (2%)
    ppermute x43, waiting for transfers between devices, flip(): lax.ppermute(block, axis, [(i, i ^ bits) for i in range(lax.axis_size(axi...  179 us
    pallas_call x6, Pallas kernels, dense(): pl.pallas_call(functools.partial(product_kernel, left_dim), grid=(width /...  54.5 us
    ppermute x43, starting transfers between devices, flip(): lax.ppermute(block, axis, [(i, i ^ bits) for i in range(lax.axis_size(axi...  52 us
    all_to_all x2, blocking collectives, swap_seq(): lax.all_to_all(pieces, 'seq', split_axis=0, concat_axis=0, tiled=True)  39.4 us
    unnamed x118, local copies, waits for them, and re-layouts  33.3 us
    pallas_call x1, Pallas kernels, recurrence_backward(): pl.pallas_call(backward_kernel, grid_spec=pltpu.PrefetchScalarGridSpec(nu...  27.1 us
    all_to_all x6, starting transfers between devices, swap_seq(): lax.all_to_all(pieces, 'seq', split_axis=0, concat_axis=0, tiled=True)  25.1 us
    pallas_call x2, Pallas kernels, exchanged_product(): pl.pallas_call(functools.partial(ordered_kernel, half), grid_spec=pltpu.P...  23.6 us
  transfers between devices with their start and end apart: 58, of which 31 were waited for; matrix products, arithmetic and copies ran while one was open for 3% of the time, Pallas kernels for 36%

profile of v5, /device:TPU:1, one launch (start us, length us, event | category | flops | bytes accessed | tf_op | source)
XLA Modules:
  0.0 633.3 jit_solution(8779055151100999874)
XLA Ops:
  21.5 20.4 %all_to_all.40 = bf16[4,64,2048]{2,1,0:T(8,128)(2,1)} all-to-all(bf16[4,64,2048]{2,1,0:T(8,128)(2,1)S(1)} %column_pieces.3), channel_id=1, replica_groups=mesh['dp'=8,'seq'=4] {'seq'}, dimensions={0} | all-to-all | bytes 2097152 | tf_op jit(solution)/shard_map/all_to_all | solution.py:110
  54.9 23.0 %collective-permute-done.1 = s32[512]{0:T(512)S(1)} collective-permute-done((s32[512]{0:T(512)S(1)}, s32[512]{0:T(512)S(1)}, u32[]{:S(2)}, u32[]{:S(2)}) %collective-permute-start.1) | collective-permute-done | bytes 2080 | tf_op jit(solution)/shard_map/ppermute | solution.py:26
  82.6 8.9 %collective-permute-done.4.refs_3_ = bf16[128,2048]{1,0:T(8,128)(2,1)S(1)} collective-permute-done((bf16[128,2048]{1,0:T(8,128)(2,1)S(1)}, bf16[128,2048]{1,0:T(8,128)(2,1)S(1)}, u32[]{:S(2)}, u32[]{:S(2)}) %collective-permute-start.4) | collective-permute-done | bytes 524320 | tf_op jit(solution)/shard_map/ppermute | solution.py:26
  98.5 19.0 %all_to_all.41 = bf16[4,64,2816]{2,1,0:T(8,128)(2,1)} all-to-all(bf16[4,64,2816]{2,1,0:T(8,128)(2,1)S(1)} %column_pieces.4), channel_id=1, replica_groups=mesh['dp'=8,'seq'=4] {'seq'}, dimensions={0} | all-to-all | bytes 2883584 | tf_op jit(solution)/shard_map/all_to_all | solution.py:110
  138.4 12.9 %dense.6.pre_ref.outgate_pre_ref = f32[1024,2048]{1,0:T(8,128)} custom-call(bf16[1024,2048]{1,0:T(8,128)(2,1)S(1)} %copy-done.30, bf16[2048,2048]{1,0:T(8,128)(2,1)} %all-gather.7.cloned.1.call-done.refs_1_.weight_ref), custom_call_target="tpu_custom_call" | custom-call | flops 12884901888 | tf_op jit(solution)/shard_map/dense/pallas_call | solution.py:452
  151.3 12.1 %recurrence_forward.1 = (f32[1024,512]{1,0:T(8,128)S(1)}, f32[8,4,128,128]{3,2,1,0:T(8,128)S(1)}) custom-call(s32[1024]{0:T(1024)S(1)} %pad_add_fusion.seg_ref, s32[8]{0:T(128)S(1)} %reshape.123.slot_ref, s32[1024,1]{1,0:T(8,128)S(1)} %copy-done.22, s32[1,1024]{1,0:T(1,128)S(1)} %bitcast.49, f32[1024,2048]{1,0:T(8,128)} %dense.6.pre_ref.outgate_pre_ref, ...), custom_call_target="tpu_custom_call" | custom-call | flops 21474836480 | tf_op jit(solution)/shard_map/recurrence_forward/pallas_call | solution.py:355
  164.8 8.0 %gate_out.1 = (bf16[1024,512]{1,0:T(8,128)(2,1)S(1)}, bf16[256,2048]{1,0:T(8,128)(2,1)S(1)}, bf16[256,2048]{1,0:T(8,128)(2,1)S(1)}, f32[512,2048]{1,0:T(8,128)}) custom-call(f32[1024,512]{1,0:T(8,128)S(1)} %get-tuple-element.81.mixed_ref, f32[1024,2048]{1,0:T(8,128)} %dense.6.pre_ref.outgate_pre_ref, ...), custom_call_target="tpu_custom_call" | custom-call | flops 3221225472 | bytes 33554432 | tf_op jit(solution)/shard_map/gate_out/pallas_call | solution.py:644
  177.9 20.1 %collective-permute-done.14.refs_1_ = bf16[256,2048]{1,0:T(8,128)(2,1)S(1)} collective-permute-done((bf16[256,2048]{1,0:T(8,128)(2,1)S(1)}, bf16[256,2048]{1,0:T(8,128)(2,1)S(1)}, u32[]{:S(2)}, u32[]{:S(2)}) %collective-permute-start.14) | collective-permute-done | bytes 1048608 | tf_op jit(solution)/shard_map/ppermute | solution.py:26
  202.6 6.9 %collective-permute-done.18.refs_3_ = bf16[128,2048]{1,0:T(8,128)(2,1)S(1)} collective-permute-done((bf16[128,2048]{1,0:T(8,128)(2,1)S(1)}, bf16[128,2048]{1,0:T(8,128)(2,1)S(1)}, u32[]{:S(2)}, u32[]{:S(2)}) %collective-permute-start.18) | collective-permute-done | bytes 524320 | tf_op jit(solution)/shard_map/ppermute | solution.py:26
  226.5 20.2 %collective-permute-done.20.refs_1_ = bf16[256,2048]{1,0:T(8,128)(2,1)S(1)} collective-permute-done((bf16[256,2048]{1,0:T(8,128)(2,1)S(1)}, bf16[256,2048]{1,0:T(8,128)(2,1)S(1)}, u32[]{:S(2)}, u32[]{:S(2)}) %collective-permute-start.20) | collective-permute-done | bytes 1048608 | tf_op jit(solution)/shard_map/ppermute | solution.py:26
  251.1 8.8 %collective-permute-done.22.refs_3_ = bf16[128,2048]{1,0:T(8,128)(2,1)S(1)} collective-permute-done((bf16[128,2048]{1,0:T(8,128)(2,1)S(1)}, bf16[128,2048]{1,0:T(8,128)(2,1)S(1)}, u32[]{:S(2)}, u32[]{:S(2)}) %collective-permute-start.22) | collective-permute-done | bytes 524320 | tf_op jit(solution)/shard_map/ppermute | solution.py:26
  267.2 19.8 %ffn_forward.1 = (f32[1024,2816]{1,0:T(8,128)}, bf16[1024,1408]{1,0:T(8,128)(2,1)}, bf16[1024,2048]{1,0:T(8,128)(2,1)}) custom-call(bf16[256,2048]{1,0:T(8,128)(2,1)S(1)} %copy-done.38, bf16[256,2048]{1,0:T(8,128)(2,1)S(1)} %collective-permute-done.20.refs_1_, bf16[256,2048]{1,0:T(8,128)(2,1)S(1)} %copy-done.25, bf16[128,2048]{1,0:T(8,128)(2,1)S(1)} %copy-done.40, ...), custom_call_target="tpu_custom_call" | custom-call | flops 17716740096 | tf_op jit(solution)/shard_map/ffn_forward/pallas_call | solution.py:711
  313.0 14.5 %ffn_backward.1.left_ref.refs_1_ = bf16[1024,2816]{1,0:T(8,128)(2,1)} custom-call(bf16[1024,2048]{1,0:T(8,128)(2,1)S(1)} %copy-done.29, bf16[2048,1408]{1,0:T(8,128)(2,1)} %all-gather.11.cloned.1.call-done.weight_ref, f32[1024,2816]{1,0:T(8,128)} %get-tuple-element.92.both_ref), custom_call_target="tpu_custom_call" | custom-call | flops 11811160064 | tf_op jit(solution)/shard_map/ffn_backward/pallas_call | solution.py:758
  327.5 17.4 %partial_product.1 = (bf16[256,2048]{1,0:T(8,128)(2,1)}, bf16[256,2048]{1,0:T(8,128)(2,1)}, f32[512,2048]{1,0:T(8,128)}) custom-call(bf16[1024,2816]{1,0:T(8,128)(2,1)} %ffn_backward.1.left_ref.refs_1_, bf16[2048,2816]{1,0:T(8,128)(2,1)} %all-gather.9.cloned.1.call-done.refs_5_.refs_0_), custom_call_target="tpu_custom_call" | custom-call | flops 17716740096 | tf_op jit(solution)/shard_map/partial_product/pallas_call | solution.py:614
  346.2 17.8 %dense.9 = bf16[2048,2816]{1,0:T(8,128)(2,1)} custom-call(bf16[1024,2048]{1,0:T(8,128)(2,1)S(1)} %copy-done.45, bf16[1024,2816]{1,0:T(8,128)(2,1)} %ffn_backward.1.left_ref.refs_1_), custom_call_target="tpu_custom_call" | custom-call | flops 17716740096 | tf_op jit(solution)/shard_map/dense/pallas_call | solution.py:452
  373.1 10.8 %collective-permute-done.27.refs_3_ = bf16[128,2048]{1,0:T(8,128)(2,1)S(1)} collective-permute-done((bf16[128,2048]{1,0:T(8,128)(2,1)S(1)}, bf16[128,2048]{1,0:T(8,128)(2,1)S(1)}, u32[]{:S(2)}, u32[]{:S(2)}) %collective-permute-start.27) | collective-permute-done | bytes 524320 | tf_op jit(solution)/shard_map/ppermute | solution.py:26
  391.2 20.3 %collective-permute-done.29.refs_1_ = bf16[256,2048]{1,0:T(8,128)(2,1)S(1)} collective-permute-done((bf16[256,2048]{1,0:T(8,128)(2,1)S(1)}, bf16[256,2048]{1,0:T(8,128)(2,1)S(1)}, u32[]{:S(2)}, u32[]{:S(2)}) %collective-permute-start.29) | collective-permute-done | bytes 1048608 | tf_op jit(solution)/shard_map/ppermute | solution.py:26
  413.6 10.3 %exchanged_product.2 = bf16[1024,2048]{1,0:T(8,128)(2,1)} custom-call(s32[8]{0:T(128)S(1)} %multiply_add_fusion.places_ref, bf16[1024,1408]{1,0:T(8,128)(2,1)S(1)} %copy-done.43, bf16[2048,1408]{1,0:T(8,128)(2,1)} %all-gather.11.cloned.1.call-done.weight_ref), custom_call_target="tpu_custom_call" | custom-call | flops 8858370048 | tf_op jit(solution)/shard_map/exchanged_product/pallas_call | solution.py:592
  423.9 6.5 %gated_gradient.1 = (bf16[1024,2048]{1,0:T(8,128)(2,1)}, f32[1024,512]{1,0:T(8,128)}) custom-call(bf16[256,2048]{1,0:T(8,128)(2,1)S(1)} %get-tuple-element.102.refs_0_, bf16[256,2048]{1,0:T(8,128)(2,1)S(1)} %collective-permute-done.29.refs_1_, bf16[256,2048]{1,0:T(8,128)(2,1)S(1)} %collective-permute-done.30.refs_2_, ...), custom_call_target="tpu_custom_call" | custom-call | flops 3221225472 | tf_op jit(solution)/shard_map/gated_gradient/pallas_call | solution.py:672
  438.1 27.1 %recurrence_backward.1 = (bf16[1024,2048]{1,0:T(8,128)(2,1)}, f32[1,512]{1,0:T(1,128)S(1)}) custom-call(s32[1024]{0:T(1024)S(1)} %pad_add_fusion.seg_ref, s32[8]{0:T(128)S(1)} %reshape.123.slot_ref, s32[1024,1]{1,0:T(8,128)S(1)} %copy-done.23, s32[1,1024]{1,0:T(1,128)S(1)} %bitcast.50, f32[1024,2048]{1,0:T(8,128)} %dense.6.pre_ref.outgate_pre_ref, ...), custom_call_target="tpu_custom_call" | custom-call | flops 41607495680 | tf_op jit(solution)/shard_map/recurrence_backward/pallas_call | solution.py:388
  465.3 7.8 %dense.10 = bf16[1024,2048]{1,0:T(8,128)(2,1)} custom-call(bf16[1024,1024]{1,0:T(8,128)(2,1)S(1)} %copy-done.32, bf16[1024,2048]{1,0:T(8,128)(2,1)} %get-tuple-element.113.refs_1_.right_ref.left_ref), custom_call_target="tpu_custom_call" | custom-call | flops 6442450944 | tf_op jit(solution)/shard_map/dense/pallas_call | solution.py:452
  490.7 9.0 %mixer_sums.1 = bf16[1024,2560]{1,0:T(8,128)(2,1)} custom-call(s32[1]{0:T(128)} %bitcast.4.core_ref, bf16[1024,1024]{1,0:T(8,128)(2,1)S(1)} %copy-done.31, bf16[1024,2048]{1,0:T(8,128)(2,1)} %get-tuple-element.113.refs_1_.right_ref.left_ref, bf16[1024,2048]{1,0:T(8,128)(2,1)} %collective-permute-done.33.theirs_ref, bf16[4,2,64,2048]{3,2,1,0:T(8,128)(2,1)S(1)} %bitcast.47, ...), custom_call_target="tpu_custom_call" | custom-call | flops 6442450944 | tf_op jit(solution)/shard_map/mixer_sums/pallas_call | solution.py:489
  517.7 13.3 %exchanged_product.3 = bf16[1024,2048]{1,0:T(8,128)(2,1)S(1)} custom-call(s32[8]{0:T(128)S(1)} %multiply_add_fusion.places_ref, bf16[1024,2048]{1,0:T(8,128)(2,1)} %get-tuple-element.113.refs_1_.right_ref.left_ref, bf16[2048,2048]{1,0:T(8,128)(2,1)} %all-gather.7.cloned.1.call-done.refs_1_.weight_ref), custom_call_target="tpu_custom_call" | custom-call | flops 12884901888 | tf_op jit(solution)/shard_map/exchanged_product/pallas_call | solution.py:592
  553.2 33.0 %collective-permute-done.42 = f32[512]{0:T(512)S(1)} collective-permute-done((f32[512]{0:T(512)S(1)}, f32[512]{0:T(512)S(1)}, u32[]{:S(2)}, u32[]{:S(2)}) %collective-permute-start.42) | collective-permute-done | bytes 2080 | tf_op jit(solution)/shard_map/ppermute | solution.py:26
  (296 shorter events, 250.3 us)
Async XLA Ops:
  7.2 90.9 %all-gather.5.cloned.1.call-start = ((), (), s32[]{:S(2)}) async-start(), calls=%async_computation.11 | async-start | bytes 2359296 | tf_op jit(solution)/shard_map/all_gather | solution.py:114
  17.4 118.9 %all-gather.7.cloned.1.call-start = ((), (), s32[]{:S(2)}) async-start(), calls=%async_computation.12 | async-start | bytes 9437184 | tf_op jit(solution)/shard_map/all_gather | solution.py:114
  42.0 220.6 %all-gather.9.cloned.1.call-start = ((), (), s32[]{:S(2)}) async-start(), calls=%async_computation.13 | async-start | bytes 12976128 | tf_op jit(solution)/shard_map/all_gather | solution.py:114
  52.6 26.6 %collective-permute-start.2 = (bf16[256,2048]{1,0:T(8,128)(2,1)S(1)}, bf16[256,2048]{1,0:T(8,128)(2,1)S(1)}, u32[]{:S(2)}, u32[]{:S(2)}) collective-permute-start(bf16[256,2048]{1,0:T(8,128)(2,1)S(1)} %bitcast.36), channel_id=1, source_target_pairs={{0,1},{1,0},{2,3},{3,2},{4,5},{5,4},{6,7},{7,6},{8,9},{9,8},{10,11... | collective-permute-start | bytes 3145736 | tf_op jit(solution)/shard_map/ppermute | solution.py:26
  53.3 26.4 %collective-permute-start.3 = (bf16[256,2048]{1,0:T(8,128)(2,1)S(1)}, bf16[256,2048]{1,0:T(8,128)(2,1)S(1)}, u32[]{:S(2)}, u32[]{:S(2)}) collective-permute-start(bf16[256,2048]{1,0:T(8,128)(2,1)S(1)} %bitcast.37), channel_id=1, source_target_pairs={{0,2},{1,3},{2,0},{3,1},{4,6},{5,7},{6,4},{7,5},{8,10},{9,11},{10,... | collective-permute-start | bytes 3145736 | tf_op jit(solution)/shard_map/ppermute | solution.py:26
  53.6 24.3 %collective-permute-start.1 = (s32[512]{0:T(512)S(1)}, s32[512]{0:T(512)S(1)}, u32[]{:S(2)}, u32[]{:S(2)}) collective-permute-start(s32[512]{0:T(512)S(1)} %pad_add_fusion.1), channel_id=1, source_target_pairs={{0,2},{1,3},{2,0},{3,1},{4,6},{5,7},{6,4},{7,5},{8,10},{9,11},{10,... | collective-permute-start | bytes 6152 | tf_op jit(solution)/shard_map/ppermute | solution.py:26
  54.8 23.1 %collective-permute-start.9 = (bf16[512,3]{0,1:T(4,128)(2,1)S(1)}, bf16[512,3]{0,1:T(4,128)(2,1)S(1)}, u32[]{:S(2)}, u32[]{:S(2)}) collective-permute-start(bf16[512,3]{0,1:T(4,128)(2,1)S(1)} %pad_maximum_fusion.2), channel_id=1, source_target_pairs={{0,8},{4,12},{8,0},{12,4},{16,24},{20,28},{24,16},{28,20},{1,9},{5... | collective-permute-start | bytes 9224 | tf_op jit(solution)/shard_map/ppermute | solution.py:26
  122.5 188.3 %all-gather.11.cloned.1.call-start = ((), (), s32[]{:S(2)}) async-start(), calls=%async_computation.14 | async-start | bytes 6488064 | tf_op jit(solution)/shard_map/all_gather | solution.py:114
  130.3 34.5 %collective-permute-start.12 = (bf16[256,2048]{1,0:T(8,128)(2,1)S(1)}, bf16[256,2048]{1,0:T(8,128)(2,1)S(1)}, u32[]{:S(2)}, u32[]{:S(2)}) collective-permute-start(bf16[256,2048]{1,0:T(8,128)(2,1)S(1)} %bitcast.41), channel_id=1, source_target_pairs={{0,1},{1,0},{2,3},{3,2},{4,5},{5,4},{6,7},{7,6},{8,9},{9,8},{10,11... | collective-permute-start | bytes 3145736 | tf_op jit(solution)/shard_map/ppermute | solution.py:26
  131.4 33.4 %collective-permute-start.13 = (bf16[256,2048]{1,0:T(8,128)(2,1)S(1)}, bf16[256,2048]{1,0:T(8,128)(2,1)}, u32[]{:S(2)}, u32[]{:S(2)}) collective-permute-start(bf16[256,2048]{1,0:T(8,128)(2,1)S(1)} %bitcast.42), channel_id=1, source_target_pairs={{0,2},{1,3},{2,0},{3,1},{4,6},{5,7},{6,4},{7,5},{8,10},{9,11},{10,... | collective-permute-start | bytes 3145736 | tf_op jit(solution)/shard_map/ppermute | solution.py:26
  131.7 232.3 %reduce-scatter.4.cloned.1.call-start = ((), (), s32[]{:S(2)}) async-start(), calls=%async_computation.15 | async-start | bytes 3604480 | tf_op jit(solution)/shard_map/reduce_scatter | solution.py:119
  173.7 24.3 %collective-permute-start.14 = (bf16[256,2048]{1,0:T(8,128)(2,1)S(1)}, bf16[256,2048]{1,0:T(8,128)(2,1)S(1)}, u32[]{:S(2)}, u32[]{:S(2)}) collective-permute-start(bf16[256,2048]{1,0:T(8,128)(2,1)S(1)} %get-tuple-element.83), channel_id=1, source_target_pairs={{0,1},{1,0},{2,3},{3,2},{4,5},{5,4},{6,7},{7,6},{8,9},{9,8},{10,11... | collective-permute-start | bytes 3145736 | tf_op jit(solution)/shard_map/ppermute | solution.py:26
  174.9 23.4 %collective-permute-start.15 = (bf16[256,2048]{1,0:T(8,128)(2,1)S(1)}, bf16[256,2048]{1,0:T(8,128)(2,1)S(1)}, u32[]{:S(2)}, u32[]{:S(2)}) collective-permute-start(bf16[256,2048]{1,0:T(8,128)(2,1)S(1)} %get-tuple-element.84), channel_id=1, source_target_pairs={{0,2},{1,3},{2,0},{3,1},{4,6},{5,7},{6,4},{7,5},{8,10},{9,11},{10,... | collective-permute-start | bytes 3145736 | tf_op jit(solution)/shard_map/ppermute | solution.py:26
  176.0 33.5 %collective-permute-start.18 = (bf16[128,2048]{1,0:T(8,128)(2,1)S(1)}, bf16[128,2048]{1,0:T(8,128)(2,1)S(1)}, u32[]{:S(2)}, u32[]{:S(2)}) collective-permute-start(bf16[128,2048]{1,0:T(8,128)(2,1)S(1)} %slice.92), channel_id=1, source_target_pairs={{0,2},{1,3},{2,0},{3,1},{4,6},{5,7},{6,4},{7,5},{8,10},{9,11},{10,... | collective-permute-start | bytes 1572872 | tf_op jit(solution)/shard_map/ppermute | solution.py:26
  177.5 32.0 %collective-permute-start.19 = (bf16[128,2048]{1,0:T(8,128)(2,1)S(1)}, bf16[128,2048]{1,0:T(8,128)(2,1)S(1)}, u32[]{:S(2)}, u32[]{:S(2)}) collective-permute-start(bf16[128,2048]{1,0:T(8,128)(2,1)S(1)} %slice.93), channel_id=1, source_target_pairs={{0,1},{1,0},{2,3},{3,2},{4,5},{5,4},{6,7},{7,6},{8,9},{9,8},{10,11... | collective-permute-start | bytes 1572872 | tf_op jit(solution)/shard_map/ppermute | solution.py:26
  225.0 24.7 %collective-permute-start.21 = (bf16[256,2048]{1,0:T(8,128)(2,1)S(1)}, bf16[256,2048]{1,0:T(8,128)(2,1)S(1)}, u32[]{:S(2)}, u32[]{:S(2)}) collective-permute-start(bf16[256,2048]{1,0:T(8,128)(2,1)S(1)} %get-tuple-element.87.refs_0_), channel_id=1, source_target_pairs={{0,2},{1,3},{2,0},{3,1},{4,6},{5,7},{6,4},{7,5},{8,10},{9,11},{10,... | collective-permute-start | bytes 3145736 | tf_op jit(solution)/shard_map/ppermute | solution.py:26
  310.3 203.6 %reduce-scatter.6.cloned.1.call-start = ((), (), s32[]{:S(2)}) async-start(), calls=%async_computation.16 | async-start | bytes 12976128 | tf_op jit(solution)/shard_map/reduce_scatter | solution.py:898
  345.0 24.7 %collective-permute-start.25 = (bf16[256,2048]{1,0:T(8,128)(2,1)}, bf16[256,2048]{1,0:T(8,128)(2,1)S(1)}, u32[]{:S(2)}, u32[]{:S(2)}) collective-permute-start(bf16[256,2048]{1,0:T(8,128)(2,1)} %get-tuple-element.95), channel_id=1, source_target_pairs={{0,1},{1,0},{2,3},{3,2},{4,5},{5,4},{6,7},{7,6},{8,9},{9,8},{10,11... | collective-permute-start | bytes 3145736 | tf_op jit(solution)/shard_map/ppermute | solution.py:26
  345.5 24.3 %collective-permute-start.26 = (bf16[256,2048]{1,0:T(8,128)(2,1)}, bf16[256,2048]{1,0:T(8,128)(2,1)}, u32[]{:S(2)}, u32[]{:S(2)}) collective-permute-start(bf16[256,2048]{1,0:T(8,128)(2,1)} %get-tuple-element.98), channel_id=1, source_target_pairs={{0,2},{1,3},{2,0},{3,1},{4,6},{5,7},{6,4},{7,5},{8,10},{9,11},{10,... | collective-permute-start | bytes 3145736 | tf_op jit(solution)/shard_map/ppermute | solution.py:26
  430.4 51.9 %all-to-all-start.3 = ((bf16[4,256,2048]{2,1,0:T(8,128)(2,1)}), bf16[4,256,2048]{2,1,0:T(8,128)(2,1)}, u32[]{:S(2)}, u32[]{:S(2)}) async-start(bf16[4,256,2048]{2,1,0:T(8,128)(2,1)} %bitcast.54), calls=%async_computation.4 | async-start | bytes 8388608 | tf_op jit(solution)/shard_map/all_to_all | solution.py:110
  435.4 155.5 %reduce-scatter.8.cloned.1.call-start = ((), (), s32[]{:S(2)}) async-start(), calls=%async_computation.17 | async-start | bytes 6553600 | tf_op jit(solution)/shard_map/reduce_scatter | solution.py:119
  535.1 55.8 %all-to-all-start.6 = ((bf16[4,256,2048]{2,1,0:T(8,128)(2,1)}), bf16[4,256,2048]{2,1,0:T(8,128)(2,1)}, u32[]{:S(2)}, u32[]{:S(2)}) async-start(bf16[4,256,2048]{2,1,0:T(8,128)(2,1)} %bitcast.45), calls=%async_computation.8 | async-start | bytes 8388608 | tf_op jit(solution)/shard_map/all_to_all | solution.py:110
  551.7 34.5 %collective-permute-start.42 = (f32[512]{0:T(512)S(1)}, f32[512]{0:T(512)S(1)}, u32[]{:S(2)}, u32[]{:S(2)}) collective-permute-start(f32[512]{0:T(512)S(1)} %add_add_fusion), channel_id=1, source_target_pairs={{0,1},{1,0},{2,3},{3,2},{4,5},{5,4},{6,7},{7,6},{8,9},{9,8},{10,11... | collective-permute-start | bytes 6152 | tf_op jit(solution)/shard_map/ppermute | solution.py:26
  593.2 30.3 %all-to-all-start.7 = ((bf16[4,64,2048]{2,1,0:T(8,128)(2,1)}), bf16[4,64,2048]{2,1,0:T(8,128)(2,1)S(1)}, u32[]{:S(2)}, u32[]{:S(2)}) async-start(bf16[4,64,2048]{2,1,0:T(8,128)(2,1)} %bitcast.56), calls=%async_computation.10 | async-start | bytes 2097152 | tf_op jit(solution)/shard_map/all_to_all | solution.py:110
  (93 other events, 873.9 us)
Sparse Core Ops, SparseCore 0:
  17.5 35.1 all-gather.4
  54.3 81.9 all-gather.6
  137.9 106.4 all-gather.8
  246.5 58.6 all-gather.10
  310.5 52.3 reduce-scatter.3
  370.0 115.0 reduce-scatter.5
  499.8 91.0 reduce-scatter.7

commit v6 on v5

--- a/solution.py
+++ b/solution.py
@@ -874,7 +874,7 @@
     down_pieces = swap_seq(column_pieces([after(ffn_down_weight, ffn_pieces)]))
     down_cols = gather_dp(down_pieces.reshape(rank_rows, down_pieces.shape[2]))
 
-    pre = dense(after(normed_in, down_pieces), mix_cols, f32, parts=4)
+    pre = dense(after(normed_in, down_pieces), mix_cols, f32, parts=2)
     mixed, states = recurrence_forward(segments, table, pre, bound)
     cotangent = gather_seq(after(cotangent_low, down_pieces))
     gated, partials = gate_out(after(mixed, *cotangent[0][:3]), pre, out_rows, half)

time: 645 us -> 646 us (level)
  no operation moved by 1% of the time
where the time goes in v6:
time: 646 us; the launch traced here: 634 us
  Pallas kernels  231 us (36%)
  waiting for transfers between devices  210 us (33%)
  starting transfers between devices  87 us (13%)
  local copies, waits for them, and re-layouts  41.2 us (6%)
  blocking collectives  39.4 us (6%)
  between operations  15 us (2%)
  other arithmetic  10.4 us (2%)
    ppermute x43, waiting for transfers between devices, flip(): lax.ppermute(block, axis, [(i, i ^ bits) for i in range(lax.axis_size(axi...  180 us
    pallas_call x6, Pallas kernels, dense(): pl.pallas_call(functools.partial(product_kernel, left_dim), grid=(width /...  55 us
    ppermute x43, starting transfers between devices, flip(): lax.ppermute(block, axis, [(i, i ^ bits) for i in range(lax.axis_size(axi...  51.2 us
    all_to_all x2, blocking collectives, swap_seq(): lax.all_to_all(pieces, 'seq', split_axis=0, concat_axis=0, tiled=True)  39.4 us
    unnamed x118, local copies, waits for them, and re-layouts  33.3 us
    pallas_call x1, Pallas kernels, recurrence_backward(): pl.pallas_call(backward_kernel, grid_spec=pltpu.PrefetchScalarGridSpec(nu...  27.1 us
    all_to_all x6, starting transfers between devices, swap_seq(): lax.all_to_all(pieces, 'seq', split_axis=0, concat_axis=0, tiled=True)  25.1 us
    pallas_call x2, Pallas kernels, exchanged_product(): pl.pallas_call(functools.partial(ordered_kernel, half), grid_spec=pltpu.P...  23.6 us
  transfers between devices with their start and end apart: 58, of which 31 were waited for; matrix products, arithmetic and copies ran while one was open for 3% of the time, Pallas kernels for 36%

profile of v6, /device:TPU:1, one launch (start us, length us, event | category | flops | bytes accessed | tf_op | source)
XLA Modules:
  0.0 633.5 jit_solution(6878240634782547949)
XLA Ops:
  21.5 20.4 %all_to_all.40 = bf16[4,64,2048]{2,1,0:T(8,128)(2,1)} all-to-all(bf16[4,64,2048]{2,1,0:T(8,128)(2,1)S(1)} %column_pieces.3), channel_id=1, replica_groups=mesh['dp'=8,'seq'=4] {'seq'}, dimensions={0} | all-to-all | bytes 2097152 | tf_op jit(solution)/shard_map/all_to_all | solution.py:110
  54.9 23.0 %collective-permute-done.1 = s32[512]{0:T(512)S(1)} collective-permute-done((s32[512]{0:T(512)S(1)}, s32[512]{0:T(512)S(1)}, u32[]{:S(2)}, u32[]{:S(2)}) %collective-permute-start.1) | collective-permute-done | bytes 2080 | tf_op jit(solution)/shard_map/ppermute | solution.py:26
  82.6 8.9 %collective-permute-done.4.refs_3_ = bf16[128,2048]{1,0:T(8,128)(2,1)S(1)} collective-permute-done((bf16[128,2048]{1,0:T(8,128)(2,1)S(1)}, bf16[128,2048]{1,0:T(8,128)(2,1)S(1)}, u32[]{:S(2)}, u32[]{:S(2)}) %collective-permute-start.4) | collective-permute-done | bytes 524320 | tf_op jit(solution)/shard_map/ppermute | solution.py:26
  98.5 19.0 %all_to_all.41 = bf16[4,64,2816]{2,1,0:T(8,128)(2,1)} all-to-all(bf16[4,64,2816]{2,1,0:T(8,128)(2,1)S(1)} %column_pieces.4), channel_id=1, replica_groups=mesh['dp'=8,'seq'=4] {'seq'}, dimensions={0} | all-to-all | bytes 2883584 | tf_op jit(solution)/shard_map/all_to_all | solution.py:110
  138.4 13.3 %dense.6.pre_ref.outgate_pre_ref = f32[1024,2048]{1,0:T(8,128)} custom-call(bf16[1024,2048]{1,0:T(8,128)(2,1)S(1)} %copy-done.30, bf16[2048,2048]{1,0:T(8,128)(2,1)} %all-gather.7.cloned.1.call-done.refs_1_.weight_ref), custom_call_target="tpu_custom_call" | custom-call | flops 12884901888 | tf_op jit(solution)/shard_map/dense/pallas_call | solution.py:452
  151.7 12.1 %recurrence_forward.1 = (f32[1024,512]{1,0:T(8,128)S(1)}, f32[8,4,128,128]{3,2,1,0:T(8,128)S(1)}) custom-call(s32[1024]{0:T(1024)S(1)} %pad_add_fusion.seg_ref, s32[8]{0:T(128)S(1)} %reshape.123.slot_ref, s32[1024,1]{1,0:T(8,128)S(1)} %copy-done.22, s32[1,1024]{1,0:T(1,128)S(1)} %bitcast.49, f32[1024,2048]{1,0:T(8,128)} %dense.6.pre_ref.outgate_pre_ref, ...), custom_call_target="tpu_custom_call" | custom-call | flops 21474836480 | tf_op jit(solution)/shard_map/recurrence_forward/pallas_call | solution.py:355
  165.2 8.0 %gate_out.1 = (bf16[1024,512]{1,0:T(8,128)(2,1)S(1)}, bf16[256,2048]{1,0:T(8,128)(2,1)S(1)}, bf16[256,2048]{1,0:T(8,128)(2,1)S(1)}, f32[512,2048]{1,0:T(8,128)}) custom-call(f32[1024,512]{1,0:T(8,128)S(1)} %get-tuple-element.81.mixed_ref, f32[1024,2048]{1,0:T(8,128)} %dense.6.pre_ref.outgate_pre_ref, ...), custom_call_target="tpu_custom_call" | custom-call | flops 3221225472 | bytes 33554432 | tf_op jit(solution)/shard_map/gate_out/pallas_call | solution.py:644
  178.4 20.1 %collective-permute-done.14.refs_1_ = bf16[256,2048]{1,0:T(8,128)(2,1)S(1)} collective-permute-done((bf16[256,2048]{1,0:T(8,128)(2,1)S(1)}, bf16[256,2048]{1,0:T(8,128)(2,1)S(1)}, u32[]{:S(2)}, u32[]{:S(2)}) %collective-permute-start.14) | collective-permute-done | bytes 1048608 | tf_op jit(solution)/shard_map/ppermute | solution.py:26
  203.0 7.2 %collective-permute-done.18.refs_3_ = bf16[128,2048]{1,0:T(8,128)(2,1)S(1)} collective-permute-done((bf16[128,2048]{1,0:T(8,128)(2,1)S(1)}, bf16[128,2048]{1,0:T(8,128)(2,1)S(1)}, u32[]{:S(2)}, u32[]{:S(2)}) %collective-permute-start.18) | collective-permute-done | bytes 524320 | tf_op jit(solution)/shard_map/ppermute | solution.py:26
  227.0 20.5 %collective-permute-done.20.refs_1_ = bf16[256,2048]{1,0:T(8,128)(2,1)S(1)} collective-permute-done((bf16[256,2048]{1,0:T(8,128)(2,1)S(1)}, bf16[256,2048]{1,0:T(8,128)(2,1)S(1)}, u32[]{:S(2)}, u32[]{:S(2)}) %collective-permute-start.20) | collective-permute-done | bytes 1048608 | tf_op jit(solution)/shard_map/ppermute | solution.py:26
  251.5 8.6 %collective-permute-done.22.refs_3_ = bf16[128,2048]{1,0:T(8,128)(2,1)S(1)} collective-permute-done((bf16[128,2048]{1,0:T(8,128)(2,1)S(1)}, bf16[128,2048]{1,0:T(8,128)(2,1)S(1)}, u32[]{:S(2)}, u32[]{:S(2)}) %collective-permute-start.22) | collective-permute-done | bytes 524320 | tf_op jit(solution)/shard_map/ppermute | solution.py:26
  267.3 19.8 %ffn_forward.1 = (f32[1024,2816]{1,0:T(8,128)}, bf16[1024,1408]{1,0:T(8,128)(2,1)}, bf16[1024,2048]{1,0:T(8,128)(2,1)}) custom-call(bf16[256,2048]{1,0:T(8,128)(2,1)S(1)} %copy-done.38, bf16[256,2048]{1,0:T(8,128)(2,1)S(1)} %collective-permute-done.20.refs_1_, bf16[256,2048]{1,0:T(8,128)(2,1)S(1)} %copy-done.25, bf16[128,2048]{1,0:T(8,128)(2,1)S(1)} %copy-done.40, ...), custom_call_target="tpu_custom_call" | custom-call | flops 17716740096 | tf_op jit(solution)/shard_map/ffn_forward/pallas_call | solution.py:711
  313.1 14.7 %ffn_backward.1.left_ref.refs_1_ = bf16[1024,2816]{1,0:T(8,128)(2,1)} custom-call(bf16[1024,2048]{1,0:T(8,128)(2,1)S(1)} %copy-done.29, bf16[2048,1408]{1,0:T(8,128)(2,1)} %all-gather.11.cloned.1.call-done.weight_ref, f32[1024,2816]{1,0:T(8,128)} %get-tuple-element.92.both_ref), custom_call_target="tpu_custom_call" | custom-call | flops 11811160064 | tf_op jit(solution)/shard_map/ffn_backward/pallas_call | solution.py:758
  327.7 17.4 %partial_product.1 = (bf16[256,2048]{1,0:T(8,128)(2,1)}, bf16[256,2048]{1,0:T(8,128)(2,1)}, f32[512,2048]{1,0:T(8,128)}) custom-call(bf16[1024,2816]{1,0:T(8,128)(2,1)} %ffn_backward.1.left_ref.refs_1_, bf16[2048,2816]{1,0:T(8,128)(2,1)} %all-gather.9.cloned.1.call-done.refs_5_.refs_0_), custom_call_target="tpu_custom_call" | custom-call | flops 17716740096 | tf_op jit(solution)/shard_map/partial_product/pallas_call | solution.py:614
  346.6 17.8 %dense.9 = bf16[2048,2816]{1,0:T(8,128)(2,1)} custom-call(bf16[1024,2048]{1,0:T(8,128)(2,1)S(1)} %copy-done.45, bf16[1024,2816]{1,0:T(8,128)(2,1)} %ffn_backward.1.left_ref.refs_1_), custom_call_target="tpu_custom_call" | custom-call | flops 17716740096 | tf_op jit(solution)/shard_map/dense/pallas_call | solution.py:452
  373.4 11.2 %collective-permute-done.27.refs_3_ = bf16[128,2048]{1,0:T(8,128)(2,1)S(1)} collective-permute-done((bf16[128,2048]{1,0:T(8,128)(2,1)S(1)}, bf16[128,2048]{1,0:T(8,128)(2,1)S(1)}, u32[]{:S(2)}, u32[]{:S(2)}) %collective-permute-start.27) | collective-permute-done | bytes 524320 | tf_op jit(solution)/shard_map/ppermute | solution.py:26
  391.5 20.4 %collective-permute-done.29.refs_1_ = bf16[256,2048]{1,0:T(8,128)(2,1)S(1)} collective-permute-done((bf16[256,2048]{1,0:T(8,128)(2,1)S(1)}, bf16[256,2048]{1,0:T(8,128)(2,1)S(1)}, u32[]{:S(2)}, u32[]{:S(2)}) %collective-permute-start.29) | collective-permute-done | bytes 1048608 | tf_op jit(solution)/shard_map/ppermute | solution.py:26
  413.9 10.3 %exchanged_product.2 = bf16[1024,2048]{1,0:T(8,128)(2,1)} custom-call(s32[8]{0:T(128)S(1)} %multiply_add_fusion.places_ref, bf16[1024,1408]{1,0:T(8,128)(2,1)S(1)} %copy-done.43, bf16[2048,1408]{1,0:T(8,128)(2,1)} %all-gather.11.cloned.1.call-done.weight_ref), custom_call_target="tpu_custom_call" | custom-call | flops 8858370048 | tf_op jit(solution)/shard_map/exchanged_product/pallas_call | solution.py:592
  424.1 6.5 %gated_gradient.1 = (bf16[1024,2048]{1,0:T(8,128)(2,1)}, f32[1024,512]{1,0:T(8,128)}) custom-call(bf16[256,2048]{1,0:T(8,128)(2,1)S(1)} %get-tuple-element.102.refs_0_, bf16[256,2048]{1,0:T(8,128)(2,1)S(1)} %collective-permute-done.29.refs_1_, bf16[256,2048]{1,0:T(8,128)(2,1)S(1)} %collective-permute-done.30.refs_2_, ...), custom_call_target="tpu_custom_call" | custom-call | flops 3221225472 | tf_op jit(solution)/shard_map/gated_gradient/pallas_call | solution.py:672
  438.4 27.1 %recurrence_backward.1 = (bf16[1024,2048]{1,0:T(8,128)(2,1)}, f32[1,512]{1,0:T(1,128)S(1)}) custom-call(s32[1024]{0:T(1024)S(1)} %pad_add_fusion.seg_ref, s32[8]{0:T(128)S(1)} %reshape.123.slot_ref, s32[1024,1]{1,0:T(8,128)S(1)} %copy-done.23, s32[1,1024]{1,0:T(1,128)S(1)} %bitcast.50, f32[1024,2048]{1,0:T(8,128)} %dense.6.pre_ref.outgate_pre_ref, ...), custom_call_target="tpu_custom_call" | custom-call | flops 41607495680 | tf_op jit(solution)/shard_map/recurrence_backward/pallas_call | solution.py:388
  465.6 7.8 %dense.10 = bf16[1024,2048]{1,0:T(8,128)(2,1)} custom-call(bf16[1024,1024]{1,0:T(8,128)(2,1)S(1)} %copy-done.32, bf16[1024,2048]{1,0:T(8,128)(2,1)} %get-tuple-element.113.refs_1_.right_ref.left_ref), custom_call_target="tpu_custom_call" | custom-call | flops 6442450944 | tf_op jit(solution)/shard_map/dense/pallas_call | solution.py:452
  491.0 9.0 %mixer_sums.1 = bf16[1024,2560]{1,0:T(8,128)(2,1)} custom-call(s32[1]{0:T(128)} %bitcast.4.core_ref, bf16[1024,1024]{1,0:T(8,128)(2,1)S(1)} %copy-done.31, bf16[1024,2048]{1,0:T(8,128)(2,1)} %get-tuple-element.113.refs_1_.right_ref.left_ref, bf16[1024,2048]{1,0:T(8,128)(2,1)} %collective-permute-done.33.theirs_ref, bf16[4,2,64,2048]{3,2,1,0:T(8,128)(2,1)S(1)} %bitcast.47, ...), custom_call_target="tpu_custom_call" | custom-call | flops 6442450944 | tf_op jit(solution)/shard_map/mixer_sums/pallas_call | solution.py:489
  518.0 13.3 %exchanged_product.3 = bf16[1024,2048]{1,0:T(8,128)(2,1)S(1)} custom-call(s32[8]{0:T(128)S(1)} %multiply_add_fusion.places_ref, bf16[1024,2048]{1,0:T(8,128)(2,1)} %get-tuple-element.113.refs_1_.right_ref.left_ref, bf16[2048,2048]{1,0:T(8,128)(2,1)} %all-gather.7.cloned.1.call-done.refs_1_.weight_ref), custom_call_target="tpu_custom_call" | custom-call | flops 12884901888 | tf_op jit(solution)/shard_map/exchanged_product/pallas_call | solution.py:592
  553.5 33.0 %collective-permute-done.42 = f32[512]{0:T(512)S(1)} collective-permute-done((f32[512]{0:T(512)S(1)}, f32[512]{0:T(512)S(1)}, u32[]{:S(2)}, u32[]{:S(2)}) %collective-permute-start.42) | collective-permute-done | bytes 2080 | tf_op jit(solution)/shard_map/ppermute | solution.py:26
  (296 shorter events, 249.2 us)
Async XLA Ops:
  7.2 90.9 %all-gather.5.cloned.1.call-start = ((), (), s32[]{:S(2)}) async-start(), calls=%async_computation.11 | async-start | bytes 2359296 | tf_op jit(solution)/shard_map/all_gather | solution.py:114
  17.4 118.9 %all-gather.7.cloned.1.call-start = ((), (), s32[]{:S(2)}) async-start(), calls=%async_computation.12 | async-start | bytes 9437184 | tf_op jit(solution)/shard_map/all_gather | solution.py:114
  42.0 220.8 %all-gather.9.cloned.1.call-start = ((), (), s32[]{:S(2)}) async-start(), calls=%async_computation.13 | async-start | bytes 12976128 | tf_op jit(solution)/shard_map/all_gather | solution.py:114
  52.6 26.6 %collective-permute-start.2 = (bf16[256,2048]{1,0:T(8,128)(2,1)S(1)}, bf16[256,2048]{1,0:T(8,128)(2,1)S(1)}, u32[]{:S(2)}, u32[]{:S(2)}) collective-permute-start(bf16[256,2048]{1,0:T(8,128)(2,1)S(1)} %bitcast.36), channel_id=1, source_target_pairs={{0,1},{1,0},{2,3},{3,2},{4,5},{5,4},{6,7},{7,6},{8,9},{9,8},{10,11... | collective-permute-start | bytes 3145736 | tf_op jit(solution)/shard_map/ppermute | solution.py:26
  53.3 26.4 %collective-permute-start.3 = (bf16[256,2048]{1,0:T(8,128)(2,1)S(1)}, bf16[256,2048]{1,0:T(8,128)(2,1)S(1)}, u32[]{:S(2)}, u32[]{:S(2)}) collective-permute-start(bf16[256,2048]{1,0:T(8,128)(2,1)S(1)} %bitcast.37), channel_id=1, source_target_pairs={{0,2},{1,3},{2,0},{3,1},{4,6},{5,7},{6,4},{7,5},{8,10},{9,11},{10,... | collective-permute-start | bytes 3145736 | tf_op jit(solution)/shard_map/ppermute | solution.py:26
  53.6 24.3 %collective-permute-start.1 = (s32[512]{0:T(512)S(1)}, s32[512]{0:T(512)S(1)}, u32[]{:S(2)}, u32[]{:S(2)}) collective-permute-start(s32[512]{0:T(512)S(1)} %pad_add_fusion.1), channel_id=1, source_target_pairs={{0,2},{1,3},{2,0},{3,1},{4,6},{5,7},{6,4},{7,5},{8,10},{9,11},{10,... | collective-permute-start | bytes 6152 | tf_op jit(solution)/shard_map/ppermute | solution.py:26
  54.8 23.1 %collective-permute-start.9 = (bf16[512,3]{0,1:T(4,128)(2,1)S(1)}, bf16[512,3]{0,1:T(4,128)(2,1)S(1)}, u32[]{:S(2)}, u32[]{:S(2)}) collective-permute-start(bf16[512,3]{0,1:T(4,128)(2,1)S(1)} %pad_maximum_fusion.2), channel_id=1, source_target_pairs={{0,8},{4,12},{8,0},{12,4},{16,24},{20,28},{24,16},{28,20},{1,9},{5... | collective-permute-start | bytes 9224 | tf_op jit(solution)/shard_map/ppermute | solution.py:26
  122.5 188.3 %all-gather.11.cloned.1.call-start = ((), (), s32[]{:S(2)}) async-start(), calls=%async_computation.14 | async-start | bytes 6488064 | tf_op jit(solution)/shard_map/all_gather | solution.py:114
  130.3 34.9 %collective-permute-start.12 = (bf16[256,2048]{1,0:T(8,128)(2,1)S(1)}, bf16[256,2048]{1,0:T(8,128)(2,1)S(1)}, u32[]{:S(2)}, u32[]{:S(2)}) collective-permute-start(bf16[256,2048]{1,0:T(8,128)(2,1)S(1)} %bitcast.41), channel_id=1, source_target_pairs={{0,1},{1,0},{2,3},{3,2},{4,5},{5,4},{6,7},{7,6},{8,9},{9,8},{10,11... | collective-permute-start | bytes 3145736 | tf_op jit(solution)/shard_map/ppermute | solution.py:26
  131.4 33.8 %collective-permute-start.13 = (bf16[256,2048]{1,0:T(8,128)(2,1)S(1)}, bf16[256,2048]{1,0:T(8,128)(2,1)}, u32[]{:S(2)}, u32[]{:S(2)}) collective-permute-start(bf16[256,2048]{1,0:T(8,128)(2,1)S(1)} %bitcast.42), channel_id=1, source_target_pairs={{0,2},{1,3},{2,0},{3,1},{4,6},{5,7},{6,4},{7,5},{8,10},{9,11},{10,... | collective-permute-start | bytes 3145736 | tf_op jit(solution)/shard_map/ppermute | solution.py:26
  131.7 232.7 %reduce-scatter.4.cloned.1.call-start = ((), (), s32[]{:S(2)}) async-start(), calls=%async_computation.15 | async-start | bytes 3604480 | tf_op jit(solution)/shard_map/reduce_scatter | solution.py:119
  174.2 24.3 %collective-permute-start.14 = (bf16[256,2048]{1,0:T(8,128)(2,1)S(1)}, bf16[256,2048]{1,0:T(8,128)(2,1)S(1)}, u32[]{:S(2)}, u32[]{:S(2)}) collective-permute-start(bf16[256,2048]{1,0:T(8,128)(2,1)S(1)} %get-tuple-element.83), channel_id=1, source_target_pairs={{0,1},{1,0},{2,3},{3,2},{4,5},{5,4},{6,7},{7,6},{8,9},{9,8},{10,11... | collective-permute-start | bytes 3145736 | tf_op jit(solution)/shard_map/ppermute | solution.py:26
  175.4 23.6 %collective-permute-start.15 = (bf16[256,2048]{1,0:T(8,128)(2,1)S(1)}, bf16[256,2048]{1,0:T(8,128)(2,1)S(1)}, u32[]{:S(2)}, u32[]{:S(2)}) collective-permute-start(bf16[256,2048]{1,0:T(8,128)(2,1)S(1)} %get-tuple-element.84), channel_id=1, source_target_pairs={{0,2},{1,3},{2,0},{3,1},{4,6},{5,7},{6,4},{7,5},{8,10},{9,11},{10,... | collective-permute-start | bytes 3145736 | tf_op jit(solution)/shard_map/ppermute | solution.py:26
  176.6 33.6 %collective-permute-start.18 = (bf16[128,2048]{1,0:T(8,128)(2,1)S(1)}, bf16[128,2048]{1,0:T(8,128)(2,1)S(1)}, u32[]{:S(2)}, u32[]{:S(2)}) collective-permute-start(bf16[128,2048]{1,0:T(8,128)(2,1)S(1)} %slice.92), channel_id=1, source_target_pairs={{0,2},{1,3},{2,0},{3,1},{4,6},{5,7},{6,4},{7,5},{8,10},{9,11},{10,... | collective-permute-start | bytes 1572872 | tf_op jit(solution)/shard_map/ppermute | solution.py:26
  178.0 32.1 %collective-permute-start.19 = (bf16[128,2048]{1,0:T(8,128)(2,1)S(1)}, bf16[128,2048]{1,0:T(8,128)(2,1)S(1)}, u32[]{:S(2)}, u32[]{:S(2)}) collective-permute-start(bf16[128,2048]{1,0:T(8,128)(2,1)S(1)} %slice.93), channel_id=1, source_target_pairs={{0,1},{1,0},{2,3},{3,2},{4,5},{5,4},{6,7},{7,6},{8,9},{9,8},{10,11... | collective-permute-start | bytes 1572872 | tf_op jit(solution)/shard_map/ppermute | solution.py:26
  225.4 24.6 %collective-permute-start.21 = (bf16[256,2048]{1,0:T(8,128)(2,1)S(1)}, bf16[256,2048]{1,0:T(8,128)(2,1)S(1)}, u32[]{:S(2)}, u32[]{:S(2)}) collective-permute-start(bf16[256,2048]{1,0:T(8,128)(2,1)S(1)} %get-tuple-element.87.refs_0_), channel_id=1, source_target_pairs={{0,2},{1,3},{2,0},{3,1},{4,6},{5,7},{6,4},{7,5},{8,10},{9,11},{10,... | collective-permute-start | bytes 3145736 | tf_op jit(solution)/shard_map/ppermute | solution.py:26
  310.4 203.8 %reduce-scatter.6.cloned.1.call-start = ((), (), s32[]{:S(2)}) async-start(), calls=%async_computation.16 | async-start | bytes 12976128 | tf_op jit(solution)/shard_map/reduce_scatter | solution.py:898
  345.2 24.7 %collective-permute-start.25 = (bf16[256,2048]{1,0:T(8,128)(2,1)}, bf16[256,2048]{1,0:T(8,128)(2,1)S(1)}, u32[]{:S(2)}, u32[]{:S(2)}) collective-permute-start(bf16[256,2048]{1,0:T(8,128)(2,1)} %get-tuple-element.95), channel_id=1, source_target_pairs={{0,1},{1,0},{2,3},{3,2},{4,5},{5,4},{6,7},{7,6},{8,9},{9,8},{10,11... | collective-permute-start | bytes 3145736 | tf_op jit(solution)/shard_map/ppermute | solution.py:26
  346.2 24.4 %collective-permute-start.26 = (bf16[256,2048]{1,0:T(8,128)(2,1)}, bf16[256,2048]{1,0:T(8,128)(2,1)}, u32[]{:S(2)}, u32[]{:S(2)}) collective-permute-start(bf16[256,2048]{1,0:T(8,128)(2,1)} %get-tuple-element.98), channel_id=1, source_target_pairs={{0,2},{1,3},{2,0},{3,1},{4,6},{5,7},{6,4},{7,5},{8,10},{9,11},{10,... | collective-permute-start | bytes 3145736 | tf_op jit(solution)/shard_map/ppermute | solution.py:26
  430.6 51.9 %all-to-all-start.3 = ((bf16[4,256,2048]{2,1,0:T(8,128)(2,1)}), bf16[4,256,2048]{2,1,0:T(8,128)(2,1)}, u32[]{:S(2)}, u32[]{:S(2)}) async-start(bf16[4,256,2048]{2,1,0:T(8,128)(2,1)} %bitcast.54), calls=%async_computation.4 | async-start | bytes 8388608 | tf_op jit(solution)/shard_map/all_to_all | solution.py:110
  435.7 155.5 %reduce-scatter.8.cloned.1.call-start = ((), (), s32[]{:S(2)}) async-start(), calls=%async_computation.17 | async-start | bytes 6553600 | tf_op jit(solution)/shard_map/reduce_scatter | solution.py:119
  535.4 55.8 %all-to-all-start.6 = ((bf16[4,256,2048]{2,1,0:T(8,128)(2,1)}), bf16[4,256,2048]{2,1,0:T(8,128)(2,1)}, u32[]{:S(2)}, u32[]{:S(2)}) async-start(bf16[4,256,2048]{2,1,0:T(8,128)(2,1)} %bitcast.45), calls=%async_computation.8 | async-start | bytes 8388608 | tf_op jit(solution)/shard_map/all_to_all | solution.py:110
  552.0 34.5 %collective-permute-start.42 = (f32[512]{0:T(512)S(1)}, f32[512]{0:T(512)S(1)}, u32[]{:S(2)}, u32[]{:S(2)}) collective-permute-start(f32[512]{0:T(512)S(1)} %add_add_fusion), channel_id=1, source_target_pairs={{0,1},{1,0},{2,3},{3,2},{4,5},{5,4},{6,7},{7,6},{8,9},{9,8},{10,11... | collective-permute-start | bytes 6152 | tf_op jit(solution)/shard_map/ppermute | solution.py:26
  593.5 30.3 %all-to-all-start.7 = ((bf16[4,64,2048]{2,1,0:T(8,128)(2,1)}), bf16[4,64,2048]{2,1,0:T(8,128)(2,1)S(1)}, u32[]{:S(2)}, u32[]{:S(2)}) async-start(bf16[4,64,2048]{2,1,0:T(8,128)(2,1)} %bitcast.56), calls=%async_computation.10 | async-start | bytes 2097152 | tf_op jit(solution)/shard_map/all_to_all | solution.py:110
  (93 other events, 872.9 us)
Sparse Core Ops, SparseCore 0:
  17.5 35.1 all-gather.4
  54.3 81.9 all-gather.6
  137.9 106.4 all-gather.8
  246.5 58.6 all-gather.10
  310.5 52.5 reduce-scatter.3
  370.7 114.5 reduce-scatter.5
  500.1 91.0 reduce-scatter.7
